TPU v7x, 512 devices: a whole 4x8x8 slice. The times are simulated.
512 devices in a mesh: tm: 32 (over x, y_lo, core), seq: 16 (over z, y_hi).
Axes of the slice: x: 4, y: 8 (y_hi: 2, y_lo: 4; y = y_hi * 4 + y_lo), z: 8, core: 2. Of those that a mesh axis runs over, the one named last changes fastest.
Arguments:
- query_in: bfloat16 [65536, 1024], P(('tm', 'seq')), may hold values from -6 to 6
- key_in: bfloat16 [65536, 1024], P(('tm', 'seq')), may hold values from -6 to 6
- value_in: bfloat16 [65536, 1024], P(('tm', 'seq')), may hold values from -6 to 6
- residual: bfloat16 [65536, 1024], P(('tm', 'seq')), may hold values from -6 to 6
- layer_gain: float32 [1024], replicated, may hold values from 0.5 to 1.5
- proj_weight: bfloat16 [1024, 2048], P(None, 'seq'), may hold values from -0.1875 to 0.1875
- conv_kernel: float32 [31, 1024], replicated, may hold values from -1 to 1
- batch_gamma: float32 [1024], replicated, may hold values from 0.25 to 1.75
- batch_beta: float32 [1024], replicated, may hold values from -3 to 3
- stale_mean: float32 [1024], replicated, may hold values from -1 to 1
- stale_variance: float32 [1024], replicated, may hold values from 0.05 to 0.5
- grad_conv: bfloat16 [65536, 1024], P(('tm', 'seq')), may hold values from -6 to 6
- grad_stream_in: bfloat16 [65536, 1024], P(('tm', 'seq')), may hold values from -6 to 6
Outputs:
- grad_query: bfloat16 [65536, 1024], P(('tm', 'seq'))
- grad_key: bfloat16 [65536, 1024], P(('tm', 'seq'))
- grad_value: bfloat16 [65536, 1024], P(('tm', 'seq'))
- grad_stream: bfloat16 [65536, 1024], P(('tm', 'seq'))
- grad_kernel: float32 [31, 1024], replicated
- grad_affine: float32 [2, 1024], replicated
- moments: float32 [2, 1024], replicated
All inputs are finite; a program needn't handle non-finite values.
Results may differ from a plain program's by a relative error of at most 0.019.
Values may be sent and summed in bfloat16 or wider, within the bound.
No kernel may reach another device: no remote copies, remote signals or barrier semaphores. Data moves between devices by JAX's collectives and lax.ppermute only.
A program may use at most 64 MiB of HBM per device.

v0:
```python
import jax
import jax.numpy as jnp
from jax import lax
from jax.sharding import PartitionSpec as P

HEADS = 16


epsilon = 1e-05


def with_halo(array, sides, width):
    for axis, dim in sides:
        size, length = (lax.axis_size(axis), array.shape[dim])
        up = [(i, (i + 1) % size) for i in range(size - 1)]
        down = [(j, i) for i, j in up]
        last = lax.slice_in_dim(array, length - width, length, axis=dim)
        initial = lax.slice_in_dim(array, 0, width, axis=dim)
        before = lax.ppermute(last, axis, up)
        after = lax.ppermute(initial, axis, down)
        array = jnp.concatenate([before, array, after], axis=dim)
    return array


def attend_forward(items):
    grouped_query, grouped_key, grouped_value = items
    queries = grouped_query[:, 0]
    key_rows = grouped_key[:, 0]
    value_rows = grouped_value[:, 0]
    frames, item_count, head_width = queries.shape
    score_scale = head_width ** (-0.5)
    row_block = min(512, frames)
    query_blocks = queries.reshape(frames // row_block, row_block, item_count, head_width)

    def one_block(query_block):
        scores = (
            jnp.einsum("qhd,khd->hqk", query_block, key_rows, preferred_element_type=jnp.float32)
            * score_scale
        )
        row_peak = jnp.max(scores, axis=-1)
        logsum = row_peak + jnp.log(jnp.sum(jnp.exp(scores - row_peak[..., None]), axis=-1))
        weights = jnp.exp(scores - logsum[..., None]).astype(jnp.bfloat16)
        attended = jnp.einsum(
            "hqk,khd->qhd", weights, value_rows, preferred_element_type=jnp.float32
        )
        return (attended.astype(jnp.bfloat16), logsum.T)

    attended, logsums = lax.map(one_block, query_blocks)
    attended = attended.reshape(frames, item_count, head_width)
    logsums = logsums.reshape(frames, item_count)
    return (attended[:, None], logsums[:, None], grouped_query, grouped_key, grouped_value)


def attend_backward(queries, key_rows, value_rows, attended, logsums, grad_heads):
    frames, item_count, head_width = queries.shape
    score_scale = head_width ** (-0.5)
    row_block = min(512, frames)
    block_count = frames // row_block

    def blocked(matrix):
        return matrix.reshape((block_count, row_block) + matrix.shape[1:])

    def one_block(running, inputs):
        key_total, value_total = running
        query_block, attended_block, grad_block, logsum_block = inputs
        scores = (
            jnp.einsum("qhd,khd->hqk", query_block, key_rows, preferred_element_type=jnp.float32)
            * score_scale
        )
        probs = jnp.exp(scores - logsum_block.T[..., None])
        weights = probs.astype(jnp.bfloat16)
        value_total = value_total + jnp.einsum(
            "hqk,qhd->khd", weights, grad_block, preferred_element_type=jnp.float32
        )
        grad_probs = jnp.einsum(
            "qhd,khd->hqk", grad_block, value_rows, preferred_element_type=jnp.float32
        )
        row_delta = jnp.sum(
            grad_block.astype(jnp.float32) * attended_block.astype(jnp.float32), axis=-1
        ).T
        grad_scores = (probs * (grad_probs - row_delta[..., None])).astype(jnp.bfloat16)
        query_grad = (
            jnp.einsum("hqk,khd->qhd", grad_scores, key_rows, preferred_element_type=jnp.float32)
            * score_scale
        )
        key_total = key_total + jnp.einsum(
            "hqk,qhd->khd", grad_scores, query_block, preferred_element_type=jnp.float32
        )
        return ((key_total, value_total), query_grad.astype(jnp.bfloat16))

    zeros_init = jnp.zeros((frames, item_count, head_width), jnp.float32)
    totals, query_grads = lax.scan(
        one_block,
        (zeros_init, zeros_init),
        (blocked(queries), blocked(attended), blocked(grad_heads), blocked(logsums)),
    )
    key_grad = (totals[0] * score_scale).astype(jnp.bfloat16)
    value_grad = totals[1].astype(jnp.bfloat16)
    return (query_grads.reshape(frames, item_count, head_width), key_grad, value_grad)


def to_heads(matrix, head_total):
    return matrix.reshape(matrix.shape[0], head_total, matrix.shape[1] // head_total)


def to_groups(matrix, head_total, group_count):
    return matrix.reshape(
        matrix.shape[0], group_count, head_total // group_count, matrix.shape[1] // head_total
    )


def local(
    query_in,
    key_in,
    value_in,
    residual,
    layer_gain,
    proj_weight,
    conv_kernel,
    batch_gamma,
    batch_beta,
    stale_mean,
    stale_variance,
    grad_conv,
    grad_stream_in,
):
    frames, model_width = residual.shape
    tap_count = conv_kernel.shape[0]
    half_span = tap_count // 2
    head_total = HEADS
    group_count = lax.axis_size("seq")
    grouped_att, grouped_logs, grouped_query, grouped_key, grouped_value = attend_forward(
        (
            lax.all_to_all(
                to_groups(query_in, head_total, group_count),
                "seq",
                split_axis=1,
                concat_axis=0,
                tiled=True,
            ),
            lax.all_to_all(
                to_groups(key_in, head_total, group_count),
                "seq",
                split_axis=1,
                concat_axis=0,
                tiled=True,
            ),
            lax.all_to_all(
                to_groups(value_in, head_total, group_count),
                "seq",
                split_axis=1,
                concat_axis=0,
                tiled=True,
            ),
        )
    )
    attended = grouped_att[:, 0]
    logsums = grouped_logs[:, 0]
    head_query = grouped_query[:, 0]
    head_key = grouped_key[:, 0]
    head_value = grouped_value[:, 0]
    attn_out = lax.all_to_all(attended, "seq", split_axis=0, concat_axis=1, tiled=True).reshape(
        frames, model_width
    )
    stream = residual.astype(jnp.float32) + attn_out.astype(jnp.float32)
    row_mean = jnp.mean(stream, axis=1, keepdims=True)
    centred = stream - row_mean
    inv_std = lax.rsqrt(jnp.mean(centred * centred, axis=1, keepdims=True) + epsilon)
    normed = centred * inv_std
    normed_low = (normed * layer_gain).astype(jnp.bfloat16)
    projected = jnp.dot(
        normed_low,
        lax.all_gather(proj_weight, "seq", axis=1, tiled=True),
        preferred_element_type=jnp.float32,
    )
    linear_half = projected[:, :model_width]
    gate_sig = jax.nn.sigmoid(projected[:, model_width:])
    glu_out = (linear_half * gate_sig).astype(jnp.bfloat16)
    glu_ext = with_halo(glu_out, ((("tm", "seq"), 0),), half_span)
    conv_sum = jnp.zeros((frames, model_width), jnp.float32)
    for offset in range(tap_count):
        conv_sum = conv_sum + conv_kernel[offset] * glu_ext[offset : offset + frames].astype(
            jnp.float32
        )
    inv_scale = lax.rsqrt(stale_variance + epsilon)
    zhat = (conv_sum - stale_mean) * inv_scale
    shifted = batch_gamma * zhat + batch_beta
    local_moments = jnp.stack([jnp.sum(conv_sum, axis=0), jnp.sum(conv_sum * conv_sum, axis=0)])
    frame_total = frames * lax.axis_size("tm") * lax.axis_size("seq")
    moments = lax.psum(local_moments, ("tm", "seq")) / frame_total
    sig_shift = jax.nn.sigmoid(shifted)
    grad_shift = grad_conv.astype(jnp.float32) * sig_shift * (1.0 + shifted * (1.0 - sig_shift))
    local_affine = jnp.stack([jnp.sum(grad_shift * zhat, axis=0), jnp.sum(grad_shift, axis=0)])
    grad_conv_out = (grad_shift * batch_gamma * inv_scale).astype(jnp.bfloat16)
    grad_wide = grad_conv_out.astype(jnp.float32)
    kernel_rows = []
    for offset in range(tap_count):
        kernel_rows.append(
            jnp.sum(grad_wide * glu_ext[offset : offset + frames].astype(jnp.float32), axis=0)
        )
    local_kernel = jnp.stack(kernel_rows)
    grad_ext = with_halo(grad_conv_out, ((("tm", "seq"), 0),), half_span)
    grad_glu = jnp.zeros((frames, model_width), jnp.float32)
    for offset in range(tap_count):
        begin = 2 * half_span - offset
        grad_glu = grad_glu + conv_kernel[offset] * grad_ext[begin : begin + frames].astype(
            jnp.float32
        )
    grad_proj = jnp.concatenate(
        [grad_glu * gate_sig, grad_glu * linear_half * gate_sig * (1.0 - gate_sig)], axis=1
    ).astype(jnp.bfloat16)
    grad_normed = lax.dot_general(
        grad_proj,
        lax.all_gather(proj_weight, "seq", axis=1, tiled=True),
        (((1,), (1,)), ((), ())),
        preferred_element_type=jnp.float32,
    )
    grad_hat = grad_normed * layer_gain
    grad_centre = inv_std * (
        grad_hat
        - jnp.mean(grad_hat, axis=1, keepdims=True)
        - normed * jnp.mean(grad_hat * normed, axis=1, keepdims=True)
    )
    grad_stream = (grad_centre + grad_stream_in.astype(jnp.float32)).astype(jnp.bfloat16)
    grad_heads = lax.all_to_all(
        to_heads(grad_stream, head_total), "seq", split_axis=1, concat_axis=0, tiled=True
    )
    query_grad, key_grad, value_grad = attend_backward(
        head_query, head_key, head_value, attended, logsums, grad_heads
    )
    query_back, key_back, value_back = (
        lax.all_to_all(query_grad, "seq", split_axis=0, concat_axis=1, tiled=True),
        lax.all_to_all(key_grad, "seq", split_axis=0, concat_axis=1, tiled=True),
        lax.all_to_all(value_grad, "seq", split_axis=0, concat_axis=1, tiled=True),
    )
    kernel_sum, affine_sum = lax.psum((local_kernel, local_affine), ("tm", "seq"))
    return (
        query_back.reshape(frames, model_width),
        key_back.reshape(frames, model_width),
        value_back.reshape(frames, model_width),
        grad_stream,
        kernel_sum,
        affine_sum,
        moments,
    )


def solution(mesh):
    in_specs = (
        P(("tm", "seq"), None),
        P(("tm", "seq"), None),
        P(("tm", "seq"), None),
        P(("tm", "seq"), None),
        P(),
        P(None, "seq"),
        P(),
        P(),
        P(),
        P(),
        P(),
        P(("tm", "seq"), None),
        P(("tm", "seq"), None),
    )
    out_specs = (
        P(("tm", "seq"), None),
        P(("tm", "seq"), None),
        P(("tm", "seq"), None),
        P(("tm", "seq"), None),
        P(),
        P(),
        P(),
    )
    return jax.shard_map(local, mesh=mesh, in_specs=in_specs, out_specs=out_specs, check_vma=False)
```

profile of v0, /device:TPU:1, one launch (start us, length us, event | category | flops | bytes accessed | tf_op | source)
XLA Modules:
  0.0 593.9 jit_solution(3130278587500688176)
XLA Ops:
  9.0 16.2 %all-to-all-start = ((bf16[128,16,1,64]{0,3,2,1:T(8,128)(2,1)}), bf16[128,16,1,64]{0,3,2,1:T(8,128)(2,1)S(1)}, u32[]{:S(2)}, u32[]{:S(2)}) async-start(bf16[128,16,1,64]{0,3,2,1:T(8,128)(2,1)} %bitcast.9), calls=%async_computation | async-start | bytes 524288 | tf_op jit(solution)/shard_map/all_to_all | solution.py:134
  27.7 10.3 %all-to-all-done = bf16[128,16,1,64]{0,3,2,1:T(8,128)(2,1)S(1)} async-done(((bf16[128,16,1,64]{0,3,2,1:T(8,128)(2,1)}), bf16[128,16,1,64]{0,3,2,1:T(8,128)(2,1)S(1)}, u32[]{:S(2)}, u32[]{:S(2)}) %all-to-all-start) | async-done | bytes 262176 | tf_op jit(solution)/shard_map/all_to_all | solution.py:134
  38.1 5.8 all-to-all-start.1
  45.7 10.9 %all-to-all-done.1 = bf16[128,16,1,64]{0,3,2,1:T(8,128)(2,1)S(1)} async-done(((bf16[128,16,1,64]{0,3,2,1:T(8,128)(2,1)}), bf16[128,16,1,64]{0,3,2,1:T(8,128)(2,1)S(1)}, u32[]{:S(2)}, u32[]{:S(2)}) %all-to-all-start.1) | async-done | bytes 262176 | tf_op jit(solution)/shard_map/all_to_all | solution.py:141
  56.5 7.2 %all-to-all-start.2 = ((bf16[128,16,1,64]{0,3,2,1:T(8,128)(2,1)}), bf16[128,16,1,64]{0,3,2,1:T(8,128)(2,1)S(1)}, u32[]{:S(2)}, u32[]{:S(2)}) async-start(bf16[128,16,1,64]{0,3,2,1:T(8,128)(2,1)} %bitcast.17), calls=%async_computation.2 | async-start | bytes 524288 | tf_op jit(solution)/shard_map/all_to_all | solution.py:148
  64.4 12.2 %all-to-all-done.2 = bf16[128,16,1,64]{0,3,2,1:T(8,128)(2,1)S(1)} async-done(((bf16[128,16,1,64]{0,3,2,1:T(8,128)(2,1)}), bf16[128,16,1,64]{0,3,2,1:T(8,128)(2,1)S(1)}, u32[]{:S(2)}, u32[]{:S(2)}) %all-to-all-start.2) | async-done | bytes 262176 | tf_op jit(solution)/shard_map/all_to_all | solution.py:148
  76.9 10.5 %while.27 = (s32[]{:T(128)}, bf16[4,512,1,64]{1,3,2,0:T(8,128)(2,1)S(1)}, f32[4,512,1]{1,2,0:T(1,128)S(1)}, bf16[4,512,1,64]{1,3,2,0:T(8,128)(2,1)S(1)}, bf16[20...) while((s32[]{:T(128)}, bf16[4,512,1,64]{1,3,2,0:T(8,128)(2,1)S(1)}, ...), condition=%wide.region_3.4_spmd, body=%wide.region_0.3_spmd.sunk | while | flops 276856320 | bytes 13256801 | solution.py:48
  89.1 11.5 %reduce.6 = bf16[2048,64]{1,0:T(8,128)(2,1)S(1)} reduce(bf16[2048,1,64]{2,1,0:T(2,128)(2,1)S(1)} %reshape.228, bf16[]{:T(256)} %broadcast.118), dimensions={1}, to_apply=%reshape.228.reduce_sub_computation | reduce | bytes 524290 | tf_op jit(solution)/shard_map/squeeze;broadcast_in_dim;reshape | solution.py:157
  101.8 7.2 %all-to-all-start.3 = ((bf16[16,2,4096]{2,1,0:T(2,128)(2,1)}), bf16[16,2,4096]{2,1,0:T(2,128)(2,1)S(1)}, u32[]{:S(2)}, u32[]{:S(2)}) async-start(bf16[16,2,4096]{2,1,0:T(2,128)(2,1)} %reshape.230), calls=%async_computation.3 | async-start | bytes 524288 | tf_op jit(solution)/shard_map/all_to_all | solution.py:162
  109.1 16.2 %all-to-all-done.3 = bf16[16,2,4096]{2,1,0:T(2,128)(2,1)S(1)} async-done(((bf16[16,2,4096]{2,1,0:T(2,128)(2,1)}), bf16[16,2,4096]{2,1,0:T(2,128)(2,1)S(1)}, u32[]{:S(2)}, u32[]{:S(2)}) %all-to-all-start.3) | async-done | bytes 262176 | tf_op jit(solution)/shard_map/all_to_all | solution.py:162
  127.5 46.6 %all-gather.2.cloned.1.call-done = bf16[1024,2048]{1,0:T(8,128)(2,1)} async-done(((bf16[1024,128]{1,0:T(8,128)(2,1)}), bf16[1024,2048]{1,0:T(8,128)(2,1)}) %all-gather.2.cloned.1.call-update) | async-done | bytes 4194320 | tf_op jit(solution)/shard_map/all_gather | solution.py:173
  179.5 9.7 %collective-permute-start.1 = (bf16[15,1024]{1,0:T(8,128)(2,1)S(1)}, bf16[15,1024]{1,0:T(8,128)(2,1)S(1)}, u32[]{:S(2)}, u32[]{:S(2)}) collective-permute-start(bf16[15,1024]{1,0:T(8,128)(2,1)S(1)} %get-tuple-element.314), channel_id=1, source_target_pairs={{1,0},{2,1},{3,2},{4,3},{5,4},{6,5},{7,6},{8,7},{9,8},{10,9},{11,1... | collective-permute-start | bytes 92168 | tf_op jit(solution)/shard_map/ppermute | solution.py:20
  193.9 10.2 %collective-permute-start.2 = (bf16[15,1024]{1,0:T(8,128)(2,1)S(1)}, bf16[15,1024]{1,0:T(8,128)(2,1)S(1)}, u32[]{:S(2)}, u32[]{:S(2)}) collective-permute-start(bf16[15,1024]{1,0:T(8,128)(2,1)S(1)} %get-tuple-element.311), channel_id=1, source_target_pairs={{1,0},{2,1},{3,2},{4,3},{5,4},{6,5},{7,6},{8,7},{9,8},{10,9},{11,1... | collective-permute-start | bytes 92168 | tf_op jit(solution)/shard_map/ppermute | solution.py:20
  206.1 9.3 %collective-permute-done.3 = bf16[15,1024]{1,0:T(8,128)(2,1)S(1)} collective-permute-done((bf16[15,1024]{1,0:T(8,128)(2,1)S(1)}, bf16[15,1024]{1,0:T(8,128)(2,1)S(1)}, u32[]{:S(2)}, u32[]{:S(2)}) %collective-permute-start.3) | collective-permute-done | bytes 30752 | tf_op jit(solution)/shard_map/ppermute | solution.py:19
  221.0 4.8 all-to-all-start.4
  225.8 12.4 %all-to-all-done.4 = bf16[128,16,64]{0,2,1:T(8,128)(2,1)S(1)} async-done(((bf16[128,16,64]{0,2,1:T(8,128)(2,1)}), bf16[128,16,64]{0,2,1:T(8,128)(2,1)S(1)}, u32[]{:S(2)}, u32[]{:S(2)}) %all-to-all-start.4) | async-done | bytes 262176 | tf_op jit(solution)/shard_map/all_to_all | solution.py:225
  238.6 20.4 %while.28 = (s32[]{:T(128)}, f32[2048,1,64]{0,2,1:T(8,128)S(1)}, f32[2048,1,64]{0,2,1:T(8,128)S(1)}, bf16[4,512,1,64]{1,3,2,0:T(8,128)(2,1)S(1)}, bf16[4,512,1,6...) while((s32[]{:T(128)}, f32[2048,1,64]{0,2,1:T(8,128)S(1)}, ...), condition=%wide.region_10.11_spmd.clone, body=%wide.region_8.10_spmd.clone.sunk | while | flops 680197632 | bytes 22229156 | solution.py:92
  261.2 3.8 all-to-all-start.7
  266.2 11.5 %reduce.7 = bf16[2048,64]{1,0:T(8,128)(2,1)S(1)} reduce(bf16[2048,1,64]{2,1,0:T(2,128)(2,1)S(1)} %reshape.229, bf16[]{:T(256)} %broadcast.118), dimensions={1}, to_apply=%reshape.229.reduce_sub_computation | reduce | bytes 524290 | tf_op jit(solution)/shard_map/reshape | solution.py:99
  278.8 11.2 %all-to-all-start.5 = ((bf16[16,2,4096]{2,1,0:T(2,128)(2,1)}), bf16[16,2,4096]{2,1,0:T(2,128)(2,1)S(1)}, u32[]{:S(2)}, u32[]{:S(2)}) async-start(bf16[16,2,4096]{2,1,0:T(2,128)(2,1)} %reshape.232), calls=%async_computation.5 | async-start | bytes 524288 | tf_op jit(solution)/shard_map/all_to_all | solution.py:232
  292.8 9.7 %all-to-all-done.5 = bf16[16,2,4096]{2,1,0:T(2,128)(2,1)S(1)} async-done(((bf16[16,2,4096]{2,1,0:T(2,128)(2,1)}), bf16[16,2,4096]{2,1,0:T(2,128)(2,1)S(1)}, u32[]{:S(2)}, u32[]{:S(2)}) %all-to-all-start.5) | async-done | bytes 262176 | tf_op jit(solution)/shard_map/all_to_all | solution.py:232
  302.5 3.5 all-to-all-start.6
  309.3 108.6 %all-reduce = (f32[2,1024]{1,0:T(2,128)}, f32[2,1024]{1,0:T(2,128)S(1)}) all-reduce(f32[2,1024]{1,0:T(2,128)S(1)} %get-tuple-element.349, f32[2,1024]{1,0:T(2,128)S(1)} %get-tuple-element.350), channel_id=1, replica_groups=mesh['tm'=32,'seq'=16] {'tm','seq'}, use_global_device_ids=true, to_apply=%region_45.46 | all-reduce | flops 4096 | bytes 32768 | tf_op jit(solution)/shard_map/psum | solution.py:236
  425.1 160.4 %all-reduce.3.cloned.1.call-done = f32[31,1024]{1,0:T(8,128)} async-done(((f32[31,1024]{1,0:T(8,128)}), f32[31,1024]{1,0:T(8,128)}) %all-reduce.3.cloned.1.call-update) | async-done | bytes 126992 | tf_op jit(solution)/shard_map/psum | solution.py:236
  (163 shorter events, 79.7 us)
Async XLA Ops:
  9.0 29.1 %all-to-all-start = ((bf16[128,16,1,64]{0,3,2,1:T(8,128)(2,1)}), bf16[128,16,1,64]{0,3,2,1:T(8,128)(2,1)S(1)}, u32[]{:S(2)}, u32[]{:S(2)}) async-start(bf16[128,16,1,64]{0,3,2,1:T(8,128)(2,1)} %bitcast.9), calls=%async_computation | async-start | bytes 524288 | tf_op jit(solution)/shard_map/all_to_all | solution.py:134
  25.2 148.9 %all-gather.2.cloned.1.call-start = ((), (), s32[]{:S(2)}) async-start(), calls=%async_computation.8 | async-start | bytes 4456448 | tf_op jit(solution)/shard_map/all_gather | solution.py:173
  38.1 18.5 %all-to-all-start.1 = ((bf16[128,16,1,64]{0,3,2,1:T(8,128)(2,1)}), bf16[128,16,1,64]{0,3,2,1:T(8,128)(2,1)S(1)}, u32[]{:S(2)}, u32[]{:S(2)}) async-start(bf16[128,16,1,64]{0,3,2,1:T(8,128)(2,1)} %bitcast.13), calls=%async_computation.1 | async-start | bytes 524288 | tf_op jit(solution)/shard_map/all_to_all | solution.py:141
  56.5 20.0 %all-to-all-start.2 = ((bf16[128,16,1,64]{0,3,2,1:T(8,128)(2,1)}), bf16[128,16,1,64]{0,3,2,1:T(8,128)(2,1)S(1)}, u32[]{:S(2)}, u32[]{:S(2)}) async-start(bf16[128,16,1,64]{0,3,2,1:T(8,128)(2,1)} %bitcast.17), calls=%async_computation.2 | async-start | bytes 524288 | tf_op jit(solution)/shard_map/all_to_all | solution.py:148
  87.4 21.6 %copy-start.6 = (f32[31,1024]{1,0:T(8,128)S(1)}, f32[31,1024]{1,0:T(8,128)}, u32[]{:S(2)}) copy-start(f32[31,1024]{1,0:T(8,128)} %param.23) | copy-start | bytes 380932
  100.7 26.4 %copy-start.1 = (bf16[128,1024]{1,0:T(8,128)(2,1)S(1)}, bf16[128,1024]{1,0:T(8,128)(2,1)}, u32[]{:S(2)}) copy-start(bf16[128,1024]{1,0:T(8,128)(2,1)} %param.20) | copy-start | bytes 786436
  101.8 23.5 %all-to-all-start.3 = ((bf16[16,2,4096]{2,1,0:T(2,128)(2,1)}), bf16[16,2,4096]{2,1,0:T(2,128)(2,1)S(1)}, u32[]{:S(2)}, u32[]{:S(2)}) async-start(bf16[16,2,4096]{2,1,0:T(2,128)(2,1)} %reshape.230), calls=%async_computation.3 | async-start | bytes 524288 | tf_op jit(solution)/shard_map/all_to_all | solution.py:162
  109.0 65.1 %copy-start.8 = (f32[1024]{0:T(1024)S(1)}, f32[1024]{0:T(1024)}, u32[]{:S(2)}) copy-start(f32[1024]{0:T(1024)} %param.21) | copy-start | bytes 12292
  127.2 61.9 %copy-start.11 = (f32[1024]{0:T(1024)S(1)}, f32[1024]{0:T(1024)}, u32[]{:S(2)}) copy-start(f32[1024]{0:T(1024)} %param.27) | copy-start | bytes 12292
  127.2 62.9 %copy-start.4 = (bf16[128,1024]{1,0:T(8,128)(2,1)S(1)}, bf16[128,1024]{1,0:T(8,128)(2,1)}, u32[]{:S(2)}) copy-start(bf16[128,1024]{1,0:T(8,128)(2,1)} %param.28) | copy-start | bytes 786436
  127.2 62.9 %copy-start.7 = (f32[1024]{0:T(1024)S(1)}, f32[1024]{0:T(1024)}, u32[]{:S(2)}) copy-start(f32[1024]{0:T(1024)} %param.24) | copy-start | bytes 12292
  127.2 62.9 %copy-start.9 = (f32[1024]{0:T(1024)S(1)}, f32[1024]{0:T(1024)}, u32[]{:S(2)}) copy-start(f32[1024]{0:T(1024)} %param.26) | copy-start | bytes 12292
  127.2 62.9 %copy-start.10 = (f32[1024]{0:T(1024)S(1)}, f32[1024]{0:T(1024)}, u32[]{:S(2)}) copy-start(f32[1024]{0:T(1024)} %param.25) | copy-start | bytes 12292
  177.1 41.1 %copy-start = (bf16[1024,2048]{1,0:T(8,128)(2,1)S(1)}, bf16[1024,2048]{1,0:T(8,128)(2,1)}, u32[]{:S(2)}) copy-start(bf16[1024,2048]{1,0:T(8,128)(2,1)} %all-gather.2.cloned.1.call-done) | copy-start | bytes 12582916
  177.3 11.9 %collective-permute-start = (bf16[15,1024]{1,0:T(8,128)(2,1)S(1)}, bf16[15,1024]{1,0:T(8,128)(2,1)S(1)}, u32[]{:S(2)}, u32[]{:S(2)}) collective-permute-start(bf16[15,1024]{1,0:T(8,128)(2,1)S(1)} %get-tuple-element.313), channel_id=1, source_target_pairs={{0,1},{1,2},{2,3},{3,4},{4,5},{5,6},{6,7},{7,8},{8,9},{9,10},{10,1... | collective-permute-start | bytes 92168 | tf_op jit(solution)/shard_map/ppermute | solution.py:19
  179.5 10.7 %collective-permute-start.1 = (bf16[15,1024]{1,0:T(8,128)(2,1)S(1)}, bf16[15,1024]{1,0:T(8,128)(2,1)S(1)}, u32[]{:S(2)}, u32[]{:S(2)}) collective-permute-start(bf16[15,1024]{1,0:T(8,128)(2,1)S(1)} %get-tuple-element.314), channel_id=1, source_target_pairs={{1,0},{2,1},{3,2},{4,3},{5,4},{6,5},{7,6},{8,7},{9,8},{10,9},{11,1... | collective-permute-start | bytes 92168 | tf_op jit(solution)/shard_map/ppermute | solution.py:20
  193.9 12.2 %collective-permute-start.2 = (bf16[15,1024]{1,0:T(8,128)(2,1)S(1)}, bf16[15,1024]{1,0:T(8,128)(2,1)S(1)}, u32[]{:S(2)}, u32[]{:S(2)}) collective-permute-start(bf16[15,1024]{1,0:T(8,128)(2,1)S(1)} %get-tuple-element.311), channel_id=1, source_target_pairs={{1,0},{2,1},{3,2},{4,3},{5,4},{6,5},{7,6},{8,7},{9,8},{10,9},{11,1... | collective-permute-start | bytes 92168 | tf_op jit(solution)/shard_map/ppermute | solution.py:20
  204.2 11.3 %collective-permute-start.3 = (bf16[15,1024]{1,0:T(8,128)(2,1)S(1)}, bf16[15,1024]{1,0:T(8,128)(2,1)S(1)}, u32[]{:S(2)}, u32[]{:S(2)}) collective-permute-start(bf16[15,1024]{1,0:T(8,128)(2,1)S(1)} %get-tuple-element.312), channel_id=1, source_target_pairs={{0,1},{1,2},{2,3},{3,4},{4,5},{5,6},{6,7},{7,8},{8,9},{9,10},{10,1... | collective-permute-start | bytes 92168 | tf_op jit(solution)/shard_map/ppermute | solution.py:19
  220.1 18.5 %copy-start.3 = (bf16[128,1024]{1,0:T(8,128)(2,1)}, bf16[128,1024]{1,0:T(8,128)(2,1)S(1)}, u32[]{:S(2)}) copy-start(bf16[128,1024]{1,0:T(8,128)(2,1)S(1)} %add_convert_fusion) | copy-start | bytes 786436
  221.0 17.2 %all-to-all-start.4 = ((bf16[128,16,64]{0,2,1:T(8,128)(2,1)}), bf16[128,16,64]{0,2,1:T(8,128)(2,1)S(1)}, u32[]{:S(2)}, u32[]{:S(2)}) async-start(bf16[128,16,64]{0,2,1:T(8,128)(2,1)} %bitcast.53), calls=%async_computation.4 | async-start | bytes 524288 | tf_op jit(solution)/shard_map/all_to_all | solution.py:225
  261.2 17.6 %all-to-all-start.7 = ((bf16[16,2,4096]{2,1,0:T(2,128)(2,1)}), bf16[16,2,4096]{2,1,0:T(2,128)(2,1)S(1)}, u32[]{:S(2)}, u32[]{:S(2)}) async-start(bf16[16,2,4096]{2,1,0:T(2,128)(2,1)} %reshape.236), calls=%async_computation.7 | async-start | bytes 524288 | tf_op jit(solution)/shard_map/all_to_all | solution.py:234
  278.8 23.6 %all-to-all-start.5 = ((bf16[16,2,4096]{2,1,0:T(2,128)(2,1)}), bf16[16,2,4096]{2,1,0:T(2,128)(2,1)S(1)}, u32[]{:S(2)}, u32[]{:S(2)}) async-start(bf16[16,2,4096]{2,1,0:T(2,128)(2,1)} %reshape.232), calls=%async_computation.5 | async-start | bytes 524288 | tf_op jit(solution)/shard_map/all_to_all | solution.py:232
  302.5 120.5 %all-to-all-start.6 = ((bf16[16,2,4096]{2,1,0:T(2,128)(2,1)}), bf16[16,2,4096]{2,1,0:T(2,128)(2,1)S(1)}, u32[]{:S(2)}, u32[]{:S(2)}) async-start(bf16[16,2,4096]{2,1,0:T(2,128)(2,1)} %reshape.234), calls=%async_computation.6 | async-start | bytes 524288 | tf_op jit(solution)/shard_map/all_to_all | solution.py:233
  306.0 279.5 %all-reduce.3.cloned.1.call-start = ((), (), s32[]{:S(2)}) async-start(), calls=%async_computation.9 | async-start | bytes 262144 | tf_op jit(solution)/shard_map/psum | solution.py:236
  (2 other events, 2.6 us)
Sparse Core Ops, SparseCore 0:
  29.1 144.9 all-gather.1
  312.4 273.0 all-reduce.2
where the time goes:
time: 595 us; the launch traced here: 594 us
  waiting for transfers between devices  290 us (49%)
  blocking collectives  109 us (18%)
  starting transfers between devices  83.7 us (14%)
  other arithmetic  41.2 us (7%)
  matrix products  28.3 us (5%)
  local copies, waits for them, and re-layouts  27.4 us (5%)
  between operations  14.8 us (2%)
    psum x1, waiting for transfers between devices, local(): lax.psum((local_kernel, local_affine), ('tm', 'seq'))  160 us
    psum x1, blocking collectives, local(): lax.psum((local_kernel, local_affine), ('tm', 'seq'))  109 us
    all_gather x1, waiting for transfers between devices, local(): lax.all_gather(proj_weight, 'seq', axis=1, tiled=True)  46.6 us
    ppermute x2, starting transfers between devices, with_halo(): after = lax.ppermute(initial, axis, down)  19.9 us
    unnamed x47, local copies, waits for them, and re-layouts  18 us
    all_to_all x1, starting transfers between devices, local(): lax.all_to_all(to_groups(query_in, head_total, group_count), 'seq', split...  16.2 us
    all_to_all x1, waiting for transfers between devices, local(): lax.all_to_all(attended, 'seq', split_axis=0, concat_axis=1, tiled=True)  16.2 us
    all_to_all x1, waiting for transfers between devices, local(): lax.all_to_all(to_heads(grad_stream, head_total), 'seq', split_axis=1, co...  12.4 us
  transfers between devices with their start and end apart: 14, of which 10 were waited for; matrix products, arithmetic and copies ran while one was open for 10% of the time, Pallas kernels for 0%

commit v1 on v0

v1 whole, which is shorter than its diff:
```python
import math

import jax
import jax.numpy as jnp
from jax import lax
from jax.experimental import pallas as pl
from jax.experimental.pallas import tpu as pltpu
from jax.sharding import PartitionSpec as P

HEADS = 16
HD = 64
D = 1024
FR = 128
KW = 31
HALF = KW // 2
STRETCH = FR * HEADS
epsilon = 1e-05
LOG2E = math.log2(math.e)
SCALE = HD ** (-0.5)
BLOCK = 256
PART_ROWS = 24

f32 = jnp.float32
bf16 = jnp.bfloat16
NT = (((1,), (1,)), ((), ()))


def params(megabytes=48):
    return pltpu.CompilerParams(vmem_limit_bytes=megabytes * 1024 * 1024)


def dot(left, right):
    return jnp.dot(left, right, preferred_element_type=f32)


def dot_nt(left, right):
    return lax.dot_general(left, right, NT, preferred_element_type=f32)


def two_parts(value):
    high = value.astype(bf16)
    low = (value - high.astype(f32)).astype(bf16)
    return high, low


def three_parts(value):
    high = value.astype(bf16)
    rest = value - high.astype(f32)
    mid = rest.astype(bf16)
    low = (rest - mid.astype(f32)).astype(bf16)
    return high, mid, low


def pack_kernel(query_ref, key_ref, value_ref, out_ref):
    for item, ref in enumerate((query_ref, key_ref, value_ref)):
        for pair in range(HEADS // 2):
            turned = ref[:, 128 * pair : 128 * (pair + 1)].T
            out_ref[2 * pair, HD * item : HD * (item + 1), :] = turned[:HD]
            out_ref[2 * pair + 1, HD * item : HD * (item + 1), :] = turned[HD:]


def forward_kernel(qkv_ref, out_ref, log_ref, keys_ref, query_ref, value_ref, score_ref):
    for source in range(HEADS):
        span = slice(FR * source, FR * (source + 1))
        key_block = qkv_ref[source, HD : 2 * HD, :]
        keys_ref[span, :] = jnp.concatenate([key_block, key_block], axis=0).T
        high, low = two_parts(qkv_ref[source, 0:HD, :].astype(f32) * (SCALE * LOG2E))
        query_ref[0:HD, span] = high
        query_ref[HD : 2 * HD, span] = low
        value_ref[0:HD, span] = qkv_ref[source, 2 * HD : 3 * HD, :]
    extra = lax.broadcasted_iota(jnp.int32, (16, STRETCH), 0)
    value_ref[HD : HD + 16, :] = jnp.where(extra == 0, 1.0, 0.0).astype(bf16)
    chunks = STRETCH // BLOCK

    def scores(block, slot):
        queries = query_ref[:, pl.ds(pl.multiple_of(block * BLOCK, BLOCK), BLOCK)]
        peak = None
        for chunk in range(chunks):
            rows = slice(BLOCK * chunk, BLOCK * (chunk + 1))
            part = dot(keys_ref[rows, :], queries)
            score_ref[slot, rows, :] = part
            part = jnp.max(part.reshape(BLOCK // 8, 8, BLOCK), axis=0)
            peak = part if peak is None else jnp.maximum(peak, part)
        return jnp.max(peak, axis=0, keepdims=True)

    def step(block, peak):
        slot = lax.rem(block, 2)
        following = scores(jnp.minimum(block + 1, chunks - 1), 1 - slot)
        total = jnp.zeros((HD + 16, BLOCK), f32)
        for chunk in range(chunks):
            rows = slice(BLOCK * chunk, BLOCK * (chunk + 1))
            weights = jnp.exp2(score_ref[slot, rows, :] - peak).astype(bf16)
            total = total + dot(value_ref[:, rows], weights)
        norm = total[HD : HD + 1]
        attended = (total[:HD] / norm).astype(bf16)
        out_ref[2 * block] = attended[:, :FR]
        out_ref[2 * block + 1] = attended[:, FR:]
        log_ref[:, pl.ds(pl.multiple_of(block * BLOCK, BLOCK), BLOCK)] = peak + jnp.log2(norm)
        return following

    lax.fori_loop(0, chunks, step, scores(0, 0))


def project_kernel(
    att_ref, residual_ref, gain_ref, weight_ref, normed_ref, inv_ref, linear_ref, gate_ref, glu_ref, first_ref, last_ref
):
    for pair in range(HEADS // 2):
        cols = slice(128 * pair, 128 * (pair + 1))
        turned = att_ref[2 * pair : 2 * pair + 2].reshape(128, FR).T
        normed_ref[:, cols] = residual_ref[:, cols].astype(f32) + turned.astype(f32)
    stream = normed_ref[...]
    centred = stream - jnp.mean(stream, axis=1, keepdims=True)
    inv_std = lax.rsqrt(jnp.mean(centred * centred, axis=1, keepdims=True) + epsilon)
    normed = centred * inv_std
    normed_ref[...] = normed
    inv_ref[...] = jnp.broadcast_to(inv_std, (FR, 128))
    low = (normed * gain_ref[...]).astype(bf16)
    for part in range(8):
        cols = slice(128 * part, 128 * (part + 1))
        weights = jnp.concatenate(
            [weight_ref[:, part].reshape(D, 128), weight_ref[:, part + 8].reshape(D, 128)], axis=1
        )
        projected = dot(low, weights)
        linear = projected[:, :128]
        gate = jax.nn.sigmoid(projected[:, 128:])
        linear_ref[:, cols] = linear
        gate_ref[:, cols] = gate
        glu = (linear * gate).astype(bf16)
        glu_ref[:, cols] = glu
        first_ref[:, cols] = glu[:16]
        last_ref[:, cols] = glu[FR - 16 :]


def fill_extended(ext_ref, before_ref, own_ref, after_ref):
    for part in range(8):
        cols = slice(128 * part, 128 * (part + 1))
        ext_ref[part, 0:16, :] = before_ref[:, cols].astype(f32)
        ext_ref[part, 16 : 16 + FR, :] = own_ref[:, cols].astype(f32)
        ext_ref[part, 16 + FR : 32 + FR, :] = after_ref[:, cols].astype(f32)


def conv_kernel_body(
    glu_ref, before_ref, after_ref, taps_ref, vec_ref, grad_ref, out_ref, first_ref, last_ref, sums_ref, ext_ref
):
    fill_extended(ext_ref, before_ref, glu_ref, after_ref)
    for part in range(8):
        cols = slice(128 * part, 128 * (part + 1))
        conv = jnp.zeros((FR, 128), f32)
        for tap in range(KW):
            conv = conv + taps_ref[tap : tap + 1, cols] * ext_ref[part, tap + 1 : tap + 1 + FR, :]
        gamma = vec_ref[0:1, cols]
        inv_scale = lax.rsqrt(vec_ref[3:4, cols] + epsilon)
        zhat = (conv - vec_ref[2:3, cols]) * inv_scale
        shifted = gamma * zhat + vec_ref[1:2, cols]
        sig = jax.nn.sigmoid(shifted)
        grad_shift = grad_ref[:, cols].astype(f32) * sig * (1.0 + shifted * (1.0 - sig))
        grad_out = (grad_shift * (gamma * inv_scale)).astype(bf16)
        out_ref[:, cols] = grad_out
        first_ref[:, cols] = grad_out[:16]
        last_ref[:, cols] = grad_out[FR - 16 :]
        sums_ref[0:1, cols] = jnp.sum(grad_shift * zhat, axis=0, keepdims=True)
        sums_ref[1:2, cols] = jnp.sum(grad_shift, axis=0, keepdims=True)
        sums_ref[2:3, cols] = jnp.sum(conv, axis=0, keepdims=True)
        sums_ref[3:4, cols] = jnp.sum(conv * conv, axis=0, keepdims=True)


def taps_kernel(glu_ref, before_ref, after_ref, grad_ref, sums_ref, part_ref, ext_ref):
    fill_extended(ext_ref, before_ref, glu_ref, after_ref)
    part_ref[...] = jnp.zeros_like(part_ref)
    for part in range(8):
        cols = slice(128 * part, 128 * (part + 1))
        grad = grad_ref[:, cols].astype(f32)
        for tap in range(KW):
            total = jnp.sum(grad * ext_ref[part, tap + 1 : tap + 1 + FR, :], axis=0, keepdims=True)
            place = (tap % 3) * 8 + part
            part_ref[tap // 3, place : place + 1, :] = total
        for row in range(4):
            tap = KW + row
            place = (tap % 3) * 8 + part
            part_ref[tap // 3, place : place + 1, :] = sums_ref[row : row + 1, cols]


def back_kernel(
    grad_ref,
    before_ref,
    after_ref,
    taps_ref,
    linear_ref,
    gate_ref,
    normed_ref,
    inv_ref,
    gain_ref,
    weight_ref,
    skip_ref,
    part_ref,
    stream_ref,
    payload_ref,
    ext_ref,
    proj_ref,
    hat_ref,
):
    fill_extended(ext_ref, before_ref, grad_ref, after_ref)
    high, low = two_parts(part_ref[...])
    payload_ref[:, 0:PART_ROWS, :] = high
    payload_ref[:, PART_ROWS : 2 * PART_ROWS, :] = low
    for part in range(8):
        cols = slice(128 * part, 128 * (part + 1))
        grad_glu = jnp.zeros((FR, 128), f32)
        for tap in range(KW):
            begin = 2 * HALF - tap + 1
            grad_glu = grad_glu + taps_ref[tap : tap + 1, cols] * ext_ref[part, begin : begin + FR, :]
        gate = gate_ref[:, cols]
        half = grad_glu * gate
        proj_ref[:, cols] = half.astype(bf16)
        proj_ref[:, 1024 + 128 * part : 1024 + 128 * (part + 1)] = (
            half * linear_ref[:, cols] * (1.0 - gate)
        ).astype(bf16)
    proj = proj_ref[...]
    for part in range(4):
        cols = slice(256 * part, 256 * (part + 1))
        rows = [
            jnp.concatenate([weight_ref[2 * part + half, s] for s in range(16)], axis=1) for half in range(2)
        ]
        hat_ref[:, cols] = dot_nt(proj, jnp.concatenate(rows, axis=0)) * gain_ref[:, cols]
    hat = hat_ref[...]
    normed = normed_ref[...]
    mean = jnp.mean(hat, axis=1, keepdims=True)
    mean_normed = jnp.mean(hat * normed, axis=1, keepdims=True)
    centre = inv_ref[:, 0:1] * (hat - mean - normed * mean_normed)
    stream = (centre + skip_ref[...].astype(f32)).astype(bf16)
    stream_ref[...] = stream
    for pair in range(HEADS // 2):
        turned = stream[:, 128 * pair : 128 * (pair + 1)].T
        payload_ref[2 * pair, 2 * PART_ROWS :, :] = turned[:HD]
        payload_ref[2 * pair + 1, 2 * PART_ROWS :, :] = turned[HD:]


def spread_kernel(payload_ref, out_ref):
    both = payload_ref[...].astype(f32)
    total = jnp.sum(both[:, :PART_ROWS] + both[:, PART_ROWS:], axis=0)
    out_ref[...] = jnp.broadcast_to(total[None], out_ref.shape)


def backward_kernel(
    qkv_ref,
    att_ref,
    log_ref,
    payload_ref,
    out_ref,
    keys_ref,
    values_ref,
    query_ref,
    grad_ref,
    turned_ref,
    key_total_ref,
    value_total_ref,
):
    pad_rows = lax.broadcasted_iota(jnp.int32, (HD, FR), 0)
    ones = jnp.where(pad_rows < 3, 1.0, 0.0).astype(bf16)
    for source in range(HEADS):
        span = slice(FR * source, FR * (source + 1))
        key_block = qkv_ref[source, HD : 2 * HD, :]
        turned_ref[:, span] = key_block
        keys_ref[span, :] = jnp.concatenate([key_block, ones], axis=0).T
        values_ref[span, :] = jnp.concatenate([qkv_ref[source, 2 * HD :, :], ones], axis=0).T
        query_ref[0:HD, span] = qkv_ref[source, 0:HD, :]
        grads = payload_ref[source, 2 * PART_ROWS :, :]
        grad_ref[0:HD, span] = grads
        delta = jnp.sum(grads.astype(f32) * att_ref[source].astype(f32), axis=0, keepdims=True)
        logs = log_ref[:, span] * (1.0 / (SCALE * LOG2E))
        for ref, row in ((query_ref, logs), (grad_ref, delta)):
            parts = three_parts(jnp.broadcast_to(-row, (HD, FR)))
            tail = jnp.where(
                pad_rows == 0,
                parts[0].astype(f32),
                jnp.where(
                    pad_rows == 1, parts[1].astype(f32), jnp.where(pad_rows == 2, parts[2].astype(f32), 0.0)
                ),
            )
            ref[HD : 2 * HD, span] = tail.astype(bf16)
    key_total_ref[...] = jnp.zeros_like(key_total_ref)
    value_total_ref[...] = jnp.zeros_like(value_total_ref)
    chunks = STRETCH // BLOCK

    def step(block, carry):
        cols = pl.ds(pl.multiple_of(block * BLOCK, BLOCK), BLOCK)
        queries = query_ref[:, cols]
        grads = grad_ref[:, cols]
        query_total = jnp.zeros((HD, BLOCK), f32)
        for chunk in range(chunks):
            rows = slice(BLOCK * chunk, BLOCK * (chunk + 1))
            probs = jnp.exp2(dot(keys_ref[rows, :], queries) * (SCALE * LOG2E))
            grad_scores = (probs * dot(values_ref[rows, :], grads)).astype(bf16)
            query_total = query_total + dot(turned_ref[:, rows], grad_scores)
            value_total_ref[:, rows] += dot_nt(grads[:HD], probs.astype(bf16))
            key_total_ref[:, rows] += dot_nt(queries[:HD], grad_scores)
        query_grad = (query_total * SCALE).astype(bf16)
        out_ref[2 * block, 0:HD, :] = query_grad[:, :FR]
        out_ref[2 * block + 1, 0:HD, :] = query_grad[:, FR:]
        return carry

    lax.fori_loop(0, chunks, step, 0)
    for source in range(HEADS):
        span = slice(FR * source, FR * (source + 1))
        out_ref[source, HD : 2 * HD, :] = (key_total_ref[:, span] * SCALE).astype(bf16)
        out_ref[source, 2 * HD : 3 * HD, :] = value_total_ref[:, span].astype(bf16)


def finish_kernel(parts_ref, payload_ref, out_ref):
    total = jnp.sum(parts_ref[...], axis=0)
    high, low = two_parts(total)
    both = jnp.concatenate([high.astype(f32), low.astype(f32)], axis=0).astype(bf16)
    out_ref[...] = jnp.broadcast_to(both[None], out_ref.shape)


def unpack_kernel(frame_total, back_ref, query_ref, key_ref, value_ref, taps_ref, affine_ref, moments_ref):
    for item, ref in enumerate((query_ref, key_ref, value_ref)):
        for pair in range(HEADS // 2):
            turned = back_ref[2 * pair : 2 * pair + 2, HD * item : HD * (item + 1), :].reshape(128, FR)
            ref[:, 128 * pair : 128 * (pair + 1)] = turned.T
    for source in range(12):
        both = back_ref[source, 3 * HD :, :].astype(f32)
        total = both[:PART_ROWS] + both[PART_ROWS:]
        for local_row in range(3):
            row = 3 * source + local_row
            if row >= KW + 4:
                continue
            if row < KW:
                ref, place, factor = taps_ref, row, 1.0
            elif row < KW + 2:
                ref, place, factor = affine_ref, row - KW, 1.0
            else:
                ref, place, factor = moments_ref, row - KW - 2, 1.0 / frame_total
            for part in range(8):
                position = 8 * local_row + part
                ref[place : place + 1, 128 * part : 128 * (part + 1)] = total[position : position + 1] * factor


def call(kernel, out_shape, *args, scratch=(), **extra):
    return pl.pallas_call(
        kernel, out_shape=out_shape, scratch_shapes=list(scratch), compiler_params=params(), **extra
    )(*args)


def shape(dims, dtype):
    return jax.ShapeDtypeStruct(dims, dtype)


def gather_weights(proj_weight):
    place = lax.axis_index("tm")
    chunk = lax.rem(place, 2) * 4 + place // 8
    own = lax.dynamic_slice_in_dim(proj_weight, chunk * 128, 128, axis=0)
    rows = lax.all_gather(own, "seq", axis=0)
    along_x = [[x * 8 + low for x in range(4)] for low in range(8)]
    rows = lax.all_gather(rows, "tm", axis=0, axis_index_groups=along_x)
    cores = [[2 * chip, 2 * chip + 1] for chip in range(16)]
    rows = lax.all_gather(rows, "tm", axis=0, axis_index_groups=cores)
    return rows.reshape(8, 16, 128, 128)


def halo(first, last):
    size = lax.axis_size("tm") * lax.axis_size("seq")
    up = [(i, i + 1) for i in range(size - 1)]
    down = [(i + 1, i) for i in range(size - 1)]
    axes = ("tm", "seq")
    return lax.ppermute(last, axes, up), lax.ppermute(first, axes, down)


def local(
    query_in,
    key_in,
    value_in,
    residual,
    layer_gain,
    proj_weight,
    conv_kernel,
    batch_gamma,
    batch_beta,
    stale_mean,
    stale_variance,
    grad_conv,
    grad_stream_in,
):
    frame_total = FR * lax.axis_size("tm") * lax.axis_size("seq")
    weights = gather_weights(proj_weight)
    gain = layer_gain.reshape(1, D)
    vectors = jnp.stack([batch_gamma, batch_beta, stale_mean, stale_variance])

    packed = call(pack_kernel, shape((HEADS, 3 * HD, FR), bf16), query_in, key_in, value_in)
    qkv = lax.all_to_all(packed, "seq", 0, 0, tiled=True)
    attended, logs = call(
        forward_kernel,
        (shape((HEADS, HD, FR), bf16), shape((1, STRETCH), f32)),
        qkv,
        scratch=(
            pltpu.VMEM((STRETCH, 2 * HD), bf16),
            pltpu.VMEM((2 * HD, STRETCH), bf16),
            pltpu.VMEM((HD + 16, STRETCH), bf16),
            pltpu.VMEM((2, STRETCH, BLOCK), f32),
        ),
    )
    att_rows = lax.all_to_all(attended, "seq", 0, 0, tiled=True)
    wide = shape((FR, D), f32)
    narrow = shape((FR, D), bf16)
    edge = shape((16, D), bf16)
    ext = pltpu.VMEM((8, 32 + FR, 128), f32)
    normed, inv_std, linear, gate, glu, first, last = call(
        project_kernel,
        (wide, shape((FR, 128), f32), wide, wide, narrow, edge, edge),
        att_rows,
        residual,
        gain,
        weights,
    )
    before, after = halo(first, last)
    grad_out, first, last, sums = call(
        conv_kernel_body,
        (narrow, edge, edge, shape((4, D), f32)),
        glu,
        before,
        after,
        conv_kernel,
        vectors,
        grad_conv,
        scratch=(ext,),
    )
    grad_before, grad_after = halo(first, last)
    parts = call(
        taps_kernel,
        shape((HEADS, PART_ROWS, 128), f32),
        glu,
        before,
        after,
        grad_out,
        sums,
        scratch=(ext,),
    )
    grad_stream, payload = call(
        back_kernel,
        (narrow, shape((HEADS, 2 * PART_ROWS + HD, FR), bf16)),
        grad_out,
        grad_before,
        grad_after,
        conv_kernel,
        linear,
        gate,
        normed,
        inv_std,
        gain,
        weights,
        grad_stream_in,
        parts,
        scratch=(ext, pltpu.VMEM((FR, 2 * D), bf16), pltpu.VMEM((FR, D), f32)),
    )
    payload = lax.all_to_all(payload, "seq", 0, 0, tiled=True)
    groups = lax.axis_size("tm")
    spread = call(
        spread_kernel,
        shape((groups, PART_ROWS, 128), f32),
        payload,
        grid=(1,),
        in_specs=[pl.BlockSpec((HEADS, 2 * PART_ROWS, 128), lambda i: (0, 0, 0))],
        out_specs=pl.BlockSpec((groups, PART_ROWS, 128), lambda i: (0, 0, 0)),
    )
    totals = lax.all_to_all(spread, "tm", 0, 0, tiled=True)
    back = call(
        backward_kernel,
        shape((HEADS, 3 * HD + 2 * PART_ROWS, FR), bf16),
        qkv,
        attended,
        logs,
        payload,
        scratch=(
            pltpu.VMEM((STRETCH, 2 * HD), bf16),
            pltpu.VMEM((STRETCH, 2 * HD), bf16),
            pltpu.VMEM((2 * HD, STRETCH), bf16),
            pltpu.VMEM((2 * HD, STRETCH), bf16),
            pltpu.VMEM((HD, STRETCH), bf16),
            pltpu.VMEM((HD, STRETCH), f32),
            pltpu.VMEM((HD, STRETCH), f32),
        ),
    )
    back = call(
        finish_kernel,
        shape(back.shape, bf16),
        totals,
        back,
        grid=(1,),
        in_specs=[
            pl.BlockSpec((groups, PART_ROWS, 128), lambda i: (0, 0, 0)),
            pl.BlockSpec(memory_space=pl.ANY),
        ],
        out_specs=pl.BlockSpec((HEADS, 2 * PART_ROWS, 128), lambda i: (0, 4, 0)),
        input_output_aliases={1: 0},
    )
    back = lax.all_to_all(back, "seq", 0, 0, tiled=True)
    query_grad, key_grad, value_grad, kernel_sum, affine_sum, moments = call(
        lambda *refs: unpack_kernel(frame_total, *refs),
        (narrow, narrow, narrow, shape((KW, D), f32), shape((2, D), f32), shape((2, D), f32)),
        back,
    )
    return (query_grad, key_grad, value_grad, grad_stream, kernel_sum, affine_sum, moments)


def solution(mesh):
    rows = P(("tm", "seq"), None)
    in_specs = (rows, rows, rows, rows, P(), P(None, "seq"), P(), P(), P(), P(), P(), rows, rows)
    out_specs = (rows, rows, rows, rows, P(), P(), P())
    return jax.shard_map(local, mesh=mesh, in_specs=in_specs, out_specs=out_specs, check_vma=False)
```

time: 595 us -> 318 us (0.53)
  the two profiles are of different devices: /device:TPU:1 before, /device:TPU:18 now
where the time goes in v1:
time: 318 us
  blocking collectives  186 us (58%)
  Pallas kernels  46.2 us (15%)
  waiting for transfers between devices  35.3 us (11%)
  starting transfers between devices  30.5 us (10%)
  between operations  14.3 us (4%)
  local copies, waits for them, and re-layouts  5.66 us (2%)
    all_gather x1, blocking collectives, gather_weights(): rows = lax.all_gather(own, 'seq', axis=0)  68.8 us
    pallas_call x10, Pallas kernels, call(): pl.pallas_call(kernel, out_shape=out_shape, scratch_shapes=list(scratch),...  46.2 us
    all_to_all x1, blocking collectives, local(): back = lax.all_to_all(back, 'seq', 0, 0, tiled=True)  39.7 us
    all_to_all x1, blocking collectives, local(): qkv = lax.all_to_all(packed, 'seq', 0, 0, tiled=True)  38.1 us
    all_gather x1, waiting for transfers between devices, gather_weights(): rows = lax.all_gather(rows, 'tm', axis=0, axis_index_groups=along_x)  28.1 us
    ppermute x4, starting transfers between devices, halo(): return (lax.ppermute(last, axes, up), lax.ppermute(first, axes, down))  21.4 us
    all_to_all x1, blocking collectives, local(): payload = lax.all_to_all(payload, 'seq', 0, 0, tiled=True)  20.5 us
    all_to_all x1, blocking collectives, local(): att_rows = lax.all_to_all(attended, 'seq', 0, 0, tiled=True)  18.4 us
  transfers between devices with their start and end apart: 7, of which 3 were waited for; matrix products, arithmetic and copies ran while one was open for 0% of the time, Pallas kernels for 11%

profile of v1, /device:TPU:18, one launch (start us, length us, event | category | flops | bytes accessed | tf_op | source)
XLA Modules:
  0.0 317.6 jit_solution(371810853881823953)
XLA Ops:
  8.1 68.8 %all-gather = bf16[2048,128]{1,0:T(8,128)(2,1)} all-gather(bf16[128,128]{1,0:T(8,128)(2,1)S(1)} %constant_dynamic-slice_fusion), channel_id=2, replica_groups=mesh['tm'=32,'seq'=16] {'seq'}, dimensions={0}, use_global_device_ids=true | all-gather | bytes 557056 | tf_op jit(solution)/shard_map/all_gather | solution.py:353
  77.0 28.1 %all-gather.6.cloned.1.call-done = bf16[64,128,128]{2,1,0:T(8,128)(2,1)} async-done(((bf16[16,128,128]{2,1,0:T(8,128)(2,1)}), bf16[64,128,128]{2,1,0:T(8,128)(2,1)}) %all-gather.6.cloned.1.call-update) | async-done | bytes 2097168 | tf_op jit(solution)/shard_map/all_gather | solution.py:355
  106.1 0.9 copy-done.5
  107.0 0.9 copy-done.6
  108.3 38.1 %all_to_all.25.qkv_ref = bf16[16,192,128]{2,1,0:T(8,128)(2,1)S(1)} all-to-all(bf16[16,192,128]{2,1,0:T(8,128)(2,1)S(1)} %shard_map.180), channel_id=1, replica_groups=mesh['tm'=32,'seq'=16] {'seq'}, dimensions={0} | all-to-all | bytes 1572864 | tf_op jit(solution)/shard_map/all_to_all | solution.py:390
  146.4 14.1 %shard_map.181 = (bf16[16,64,128]{2,1,0:T(8,128)(2,1)S(1)}, f32[1,2048]{1,0:T(1,128)S(1)}) custom-call(bf16[16,192,128]{2,1,0:T(8,128)(2,1)S(1)} %all_to_all.25.qkv_ref), custom_call_target="tpu_custom_call" | custom-call | tf_op jit(solution)/shard_map/pallas_call | solution.py:340
  160.6 18.4 %all_to_all.26.att_ref = bf16[16,64,128]{2,1,0:T(8,128)(2,1)S(1)} all-to-all(bf16[16,64,128]{2,1,0:T(8,128)(2,1)S(1)} %get-tuple-element.28.att_ref), channel_id=1, replica_groups=mesh['tm'=32,'seq'=16] {'seq'}, dimensions={0} | all-to-all | bytes 524288 | tf_op jit(solution)/shard_map/all_to_all | solution.py:402
  179.0 0.9 copy-done.7
  179.9 3.2 %shard_map.182 = (f32[128,1024]{1,0:T(8,128)S(1)}, f32[128,128]{1,0:T(8,128)S(1)}, f32[128,1024]{1,0:T(8,128)S(1)}, f32[128,1024]{1,0:T(8,128)S(1)}, bf16[128,10...) custom-call(bf16[16,64,128]{2,1,0:T(8,128)(2,1)S(1)} %all_to_all.26.att_ref, ...), custom_call_target="tpu_custom_call" | custom-call | tf_op jit(solution)/shard_map/pallas_call | solution.py:340
  183.2 2.7 collective-permute-start
  185.8 8.0 %collective-permute-start.1 = (bf16[16,1024]{1,0:T(8,128)(2,1)S(1)}, bf16[16,1024]{1,0:T(8,128)(2,1)S(1)}, u32[]{:S(2)}, u32[]{:S(2)}) collective-permute-start(bf16[16,1024]{1,0:T(8,128)(2,1)S(1)} %get-tuple-element.31), channel_id=1, source_target_pairs={{1,0},{2,1},{3,2},{4,3},{5,4},{6,5},{7,6},{8,7},{9,8},{10,9},{11,1... | collective-permute-start | bytes 98312 | tf_op jit(solution)/shard_map/ppermute | solution.py:366
  193.9 1.6 collective-permute-done.1.after_ref
  195.5 1.5 shard_map.183
  197.0 7.9 %collective-permute-start.2 = (bf16[16,1024]{1,0:T(8,128)(2,1)S(1)}, bf16[16,1024]{1,0:T(8,128)(2,1)S(1)}, u32[]{:S(2)}, u32[]{:S(2)}) collective-permute-start(bf16[16,1024]{1,0:T(8,128)(2,1)S(1)} %get-tuple-element.33), channel_id=1, source_target_pairs={{0,1},{1,2},{2,3},{3,4},{4,5},{5,6},{6,7},{7,8},{8,9},{9,10},{10,1... | collective-permute-start | bytes 98312 | tf_op jit(solution)/shard_map/ppermute | solution.py:366
  205.0 2.8 collective-permute-start.3
  207.8 1.3 shard_map.184.part_ref
  209.1 5.5 %collective-permute-done.3.after_ref = bf16[16,1024]{1,0:T(8,128)(2,1)S(1)} collective-permute-done((bf16[16,1024]{1,0:T(8,128)(2,1)S(1)}, bf16[16,1024]{1,0:T(8,128)(2,1)S(1)}, u32[]{:S(2)}, u32[]{:S(2)}) %collective-permute-start.3) | collective-permute-done | bytes 32800 | tf_op jit(solution)/shard_map/ppermute | solution.py:366
  214.7 0.9 copy-done.3
  215.6 5.7 %shard_map.185 = (bf16[128,1024]{1,0:T(8,128)(2,1)}, bf16[16,112,128]{2,1,0:T(8,128)(2,1)S(1)}) custom-call(bf16[128,1024]{1,0:T(8,128)(2,1)S(1)} %get-tuple-element.32.grad_ref, bf16[16,1024]{1,0:T(8,128)(2,1)S(1)} %collective-permute-done.2.before_ref, bf16[16,1024]{1,0:T(8,128)(2,1)S(1)} %collective-permute-done.3.after_ref, f32[31,1024]{1,0:T(8,128)S(1)} %copy-done.1, ...), custom_call_target="tpu_custom_call" | custom-call | tf_op jit(solution)/shard_map/pallas_call | solution.py:340
  221.3 20.5 %all_to_all.27.payload_ref = bf16[16,112,128]{2,1,0:T(8,128)(2,1)S(1)} all-to-all(bf16[16,112,128]{2,1,0:T(8,128)(2,1)S(1)} %get-tuple-element.40), channel_id=1, replica_groups=mesh['tm'=32,'seq'=16] {'seq'}, dimensions={0} | all-to-all | bytes 917504 | tf_op jit(solution)/shard_map/all_to_all | solution.py:455
  242.7 8.9 %all-to-all-start.3 = ((f32[32,24,128]{2,1,0:T(8,128)}), f32[32,24,128]{2,1,0:T(8,128)S(1)}, u32[]{:S(2)}, u32[]{:S(2)}) async-start(f32[32,24,128]{2,1,0:T(8,128)} %shard_map.186), calls=%async_computation.3 | async-start | bytes 786432 | tf_op jit(solution)/shard_map/all_to_all | solution.py:465
  251.6 18.2 %shard_map.187.payload_ref = bf16[16,240,128]{2,1,0:T(8,128)(2,1)S(1)} custom-call(bf16[16,192,128]{2,1,0:T(8,128)(2,1)S(1)} %all_to_all.25.qkv_ref, bf16[16,64,128]{2,1,0:T(8,128)(2,1)S(1)} %get-tuple-element.28.att_ref, f32[1,2048]{1,0:T(1,128)S(1)} %get-tuple-element.41.log_ref, bf16[16,112,128]{2,1,0:T(8,128)(2,1)S(1)} %all_to_all.27.payload_ref), custom_call_target="tpu_custom_call" | custom-call | tf_op jit(solution)/shard_map/pallas_call | solution.py:340
  269.9 39.7 %all_to_all.28.refs_0_ = bf16[16,240,128]{2,1,0:T(8,128)(2,1)S(1)} all-to-all(bf16[16,240,128]{2,1,0:T(8,128)(2,1)S(1)} %shard_map.188), channel_id=1, replica_groups=mesh['tm'=32,'seq'=16] {'seq'}, dimensions={0} | all-to-all | bytes 1966080 | tf_op jit(solution)/shard_map/all_to_all | solution.py:496
  309.7 1.1 shard_map.189
  (35 shorter events, 3.2 us)
Async XLA Ops:
  7.2 1.0 copy-start
  7.2 171.8 %copy-start.8 = (f32[1024]{0:T(1024)S(1)}, f32[1024]{0:T(1024)}, u32[]{:S(2)}) copy-start(f32[1024]{0:T(1024)} %param.17) | copy-start | bytes 12292
  7.2 97.9 %all-gather.6.cloned.1.call-start = ((), (), s32[]{:S(2)}) async-start(), calls=%async_computation.5 | async-start | bytes 2621440 | tf_op jit(solution)/shard_map/all_gather | solution.py:355
  76.9 102.1 %all-gather.8.cloned.1.call-start = ((), (), s32[]{:S(2)}) async-start(), calls=%async_computation.6 | async-start | bytes 6291456 | tf_op jit(solution)/shard_map/all_gather | solution.py:357
  105.1 1.0 copy-start.4
  106.1 0.9 copy-start.5
  107.0 0.9 copy-start.6
  108.2 85.6 %copy-start.9 = (f32[1024]{0:T(1024)S(1)}, f32[1024]{0:T(1024)}, u32[]{:S(2)}) copy-start(f32[1024]{0:T(1024)} %param.23) | copy-start | bytes 12292
  108.2 85.6 %copy-start.10 = (f32[1024]{0:T(1024)S(1)}, f32[1024]{0:T(1024)}, u32[]{:S(2)}) copy-start(f32[1024]{0:T(1024)} %param.22) | copy-start | bytes 12292
  108.2 85.6 %copy-start.11 = (f32[1024]{0:T(1024)S(1)}, f32[1024]{0:T(1024)}, u32[]{:S(2)}) copy-start(f32[1024]{0:T(1024)} %param.21) | copy-start | bytes 12292
  108.3 85.6 %copy-start.12 = (f32[1024]{0:T(1024)S(1)}, f32[1024]{0:T(1024)}, u32[]{:S(2)}) copy-start(f32[1024]{0:T(1024)} %param.20) | copy-start | bytes 12292
  108.3 87.3 %copy-start.1 = (f32[31,1024]{1,0:T(8,128)S(1)}, f32[31,1024]{1,0:T(8,128)}, u32[]{:S(2)}) copy-start(f32[31,1024]{1,0:T(8,128)} %taps_ref.3) | copy-start | bytes 380932
  108.3 87.3 %copy-start.2 = (bf16[128,1024]{1,0:T(8,128)(2,1)S(1)}, bf16[128,1024]{1,0:T(8,128)(2,1)}, u32[]{:S(2)}) copy-start(bf16[128,1024]{1,0:T(8,128)(2,1)} %grad_ref.1) | copy-start | bytes 786436
  179.0 1.0 copy-start.7
  183.2 10.8 %collective-permute-start = (bf16[16,1024]{1,0:T(8,128)(2,1)S(1)}, bf16[16,1024]{1,0:T(8,128)(2,1)S(1)}, u32[]{:S(2)}, u32[]{:S(2)}) collective-permute-start(bf16[16,1024]{1,0:T(8,128)(2,1)S(1)} %get-tuple-element.30), channel_id=1, source_target_pairs={{0,1},{1,2},{2,3},{3,4},{4,5},{5,6},{6,7},{7,8},{8,9},{9,10},{10,1... | collective-permute-start | bytes 98312 | tf_op jit(solution)/shard_map/ppermute | solution.py:366
  185.8 9.7 %collective-permute-start.1 = (bf16[16,1024]{1,0:T(8,128)(2,1)S(1)}, bf16[16,1024]{1,0:T(8,128)(2,1)S(1)}, u32[]{:S(2)}, u32[]{:S(2)}) collective-permute-start(bf16[16,1024]{1,0:T(8,128)(2,1)S(1)} %get-tuple-element.31), channel_id=1, source_target_pairs={{1,0},{2,1},{3,2},{4,3},{5,4},{6,5},{7,6},{8,7},{9,8},{10,9},{11,1... | collective-permute-start | bytes 98312 | tf_op jit(solution)/shard_map/ppermute | solution.py:366
  197.0 12.1 %collective-permute-start.2 = (bf16[16,1024]{1,0:T(8,128)(2,1)S(1)}, bf16[16,1024]{1,0:T(8,128)(2,1)S(1)}, u32[]{:S(2)}, u32[]{:S(2)}) collective-permute-start(bf16[16,1024]{1,0:T(8,128)(2,1)S(1)} %get-tuple-element.33), channel_id=1, source_target_pairs={{0,1},{1,2},{2,3},{3,4},{4,5},{5,6},{6,7},{7,8},{8,9},{9,10},{10,1... | collective-permute-start | bytes 98312 | tf_op jit(solution)/shard_map/ppermute | solution.py:366
  205.0 9.7 %collective-permute-start.3 = (bf16[16,1024]{1,0:T(8,128)(2,1)S(1)}, bf16[16,1024]{1,0:T(8,128)(2,1)S(1)}, u32[]{:S(2)}, u32[]{:S(2)}) collective-permute-start(bf16[16,1024]{1,0:T(8,128)(2,1)S(1)} %get-tuple-element.34), channel_id=1, source_target_pairs={{1,0},{2,1},{3,2},{4,3},{5,4},{6,5},{7,6},{8,7},{9,8},{10,9},{11,1... | collective-permute-start | bytes 98312 | tf_op jit(solution)/shard_map/ppermute | solution.py:366
  214.7 1.0 copy-start.3
  242.7 27.2 %all-to-all-start.3 = ((f32[32,24,128]{2,1,0:T(8,128)}), f32[32,24,128]{2,1,0:T(8,128)S(1)}, u32[]{:S(2)}, u32[]{:S(2)}) async-start(f32[32,24,128]{2,1,0:T(8,128)} %shard_map.186), calls=%async_computation.3 | async-start | bytes 786432 | tf_op jit(solution)/shard_map/all_to_all | solution.py:465
Sparse Core Ops, SparseCore 0:
  77.1 27.9 all-gather.5
  107.2 22.8 all-gather.7

commit v2 on v1

v2 whole, which is shorter than its diff:
```python
import math

import jax
import jax.numpy as jnp
from jax import lax
from jax.experimental import pallas as pl
from jax.experimental.pallas import tpu as pltpu
from jax.sharding import PartitionSpec as P

HEADS = 16
HD = 64
D = 1024
FR = 128
KW = 31
HALF = KW // 2
STRETCH = FR * HEADS
epsilon = 1e-05
LOG2E = math.log2(math.e)
SCALE = HD ** (-0.5)
BLOCK = 256
PART_ROWS = 32
EDGE = 32
ROWS = FR + 2 * EDGE
WIDE = FR + EDGE

f32 = jnp.float32
bf16 = jnp.bfloat16
NT = (((1,), (1,)), ((), ()))


def params(megabytes=48):
    return pltpu.CompilerParams(vmem_limit_bytes=megabytes * 1024 * 1024)


def dot(left, right):
    return jnp.dot(left, right, preferred_element_type=f32)


def dot_nt(left, right):
    return lax.dot_general(left, right, NT, preferred_element_type=f32)


def two_parts(value):
    high = value.astype(bf16)
    low = (value - high.astype(f32)).astype(bf16)
    return high, low


def three_parts(value):
    high = value.astype(bf16)
    rest = value - high.astype(f32)
    mid = rest.astype(bf16)
    low = (rest - mid.astype(f32)).astype(bf16)
    return high, mid, low


def pack_kernel(
    query_ref,
    key_ref,
    value_ref,
    res_first_ref,
    res_last_ref,
    grad_first_ref,
    grad_last_ref,
    out_ref,
    first_ref,
    last_ref,
):
    for item, ref in enumerate((query_ref, key_ref, value_ref)):
        for pair in range(HEADS // 2):
            turned = ref[:, 128 * pair : 128 * (pair + 1)].T
            out_ref[2 * pair, HD * item : HD * (item + 1), :] = turned[:HD]
            out_ref[2 * pair + 1, HD * item : HD * (item + 1), :] = turned[HD:]
    first_ref[:EDGE] = res_first_ref[...]
    first_ref[EDGE:] = grad_first_ref[...]
    last_ref[:EDGE] = res_last_ref[...]
    last_ref[EDGE:] = grad_last_ref[...]


CHUNKS = STRETCH // BLOCK


def block_rows(block):
    if isinstance(block, int):
        return slice(block * BLOCK, (block + 1) * BLOCK)
    return pl.ds(pl.multiple_of(block * BLOCK, BLOCK), BLOCK)


def low_lanes(rows):
    return lax.broadcasted_iota(jnp.int32, (rows, 128), 1) < HD


def soft_stage(keys_ref, query_ref, value_ref, following, current):
    queries = peak = total = None
    if following is not None:
        block, next_ref = following
        queries = query_ref[block_rows(block), :]
    for chunk in range(CHUNKS):
        rows = slice(BLOCK * chunk, BLOCK * (chunk + 1))
        if following is not None:
            part = dot(queries, keys_ref[:, rows])
            next_ref[:, rows] = part
            part = jnp.maximum(part[:, :128], part[:, 128:])
            peak = part if peak is None else jnp.maximum(peak, part)
        if current is not None:
            score_ref, top = current
            weights = jnp.exp2(score_ref[:, rows] - jnp.concatenate([top, top], axis=1)).astype(bf16)
            part = dot(weights, value_ref[rows, :])
            total = part if total is None else total + part
    if peak is not None:
        peak = jnp.broadcast_to(jnp.max(peak, axis=1, keepdims=True), (BLOCK, 128))
    return peak, total


def store_attended(total, peak, nat_ref, rows, turned_ref, log_ref, place):
    norm = jnp.broadcast_to(total[:, HD : HD + 1], (BLOCK, 128))
    attended = (total / norm).astype(bf16).astype(f32)
    low = low_lanes(BLOCK)
    nat_ref[rows, :] = jnp.where(low, attended, pltpu.roll(attended, HD, 1)).astype(bf16)
    turned = jnp.where(low, attended, peak + jnp.log2(norm)).T
    turned_ref[place] = turned[:HD].astype(bf16)
    log_ref[place] = turned[HD : HD + 8]


def edge_forward_kernel(
    qkv_ref,
    keys_ref,
    query_ref,
    value_ref,
    nat_ref,
    turned_ref,
    log_ref,
    first_ref,
    last_ref,
    score_ref,
    other_ref,
):
    pad_rows = lax.broadcasted_iota(jnp.int32, (HD, FR), 0)
    ones = jnp.where(pad_rows == 0, 1.0, 0.0).astype(bf16)
    for source in range(HEADS):
        span = slice(FR * source, FR * (source + 1))
        key_block = qkv_ref[source, HD : 2 * HD, :]
        keys_ref[0:HD, span] = key_block
        keys_ref[HD : 2 * HD, span] = key_block
        high, low = two_parts(qkv_ref[source, 0:HD, :].astype(f32) * (SCALE * LOG2E))
        query_ref[span, :] = jnp.concatenate([high, low], axis=0).T
        value_ref[span, :] = jnp.concatenate([qkv_ref[source, 2 * HD : 3 * HD, :], ones], axis=0).T
    stage = lambda *pair: soft_stage(keys_ref, query_ref, value_ref, *pair)
    top, _ = stage((0, score_ref), None)
    final_top, total = stage((CHUNKS - 1, other_ref), (score_ref, top))
    store_attended(total, top, nat_ref, slice(0, BLOCK), turned_ref, log_ref, 0)
    _, total = stage(None, (other_ref, final_top))
    store_attended(total, final_top, nat_ref, slice(BLOCK, 2 * BLOCK), turned_ref, log_ref, 1)
    first_ref[...] = nat_ref[0:EDGE, :]
    last_ref[...] = nat_ref[2 * BLOCK - EDGE : 2 * BLOCK, :]


def middle_forward_kernel(
    keys_ref, query_ref, value_ref, nat_ref, turned_ref, log_ref, score_ref, other_ref
):
    stage = lambda *pair: soft_stage(keys_ref, query_ref, value_ref, *pair)

    def store(total, top, place):
        store_attended(total, top, nat_ref, block_rows(place), turned_ref, log_ref, place)

    def two(index, top):
        place = 2 * index
        next_top, total = stage((place + 2, other_ref), (score_ref, top))
        store(total, top, place)
        last_top, total = stage((place + 3, score_ref), (other_ref, next_top))
        store(total, next_top, place + 1)
        return last_top

    top, _ = stage((1, score_ref), None)
    top = lax.fori_loop(0, 2, two, top)
    next_top, total = stage((6, other_ref), (score_ref, top))
    store(total, top, 4)
    _, total = stage(None, (other_ref, next_top))
    store(total, next_top, 5)


def assemble_kernel(edge_ref, middle_ref, before_ref, after_ref, out_ref):
    def frames(begin, count):
        if begin < 0:
            return before_ref[...]
        if begin >= STRETCH:
            return after_ref[...]
        if begin < BLOCK:
            return edge_ref[begin : begin + count, :]
        if begin < STRETCH - BLOCK:
            return middle_ref[begin - BLOCK : begin - BLOCK + count, :]
        begin -= STRETCH - 2 * BLOCK
        return edge_ref[begin : begin + count, :]

    for dest in range(HEADS):
        begin = FR * dest
        low = low_lanes(64)
        out_ref[dest, 0:64, :] = jnp.where(
            low, frames(begin, 64).astype(f32), frames(begin + 64, 64).astype(f32)
        ).astype(bf16)
        low = low_lanes(EDGE)
        out_ref[dest, 64 : 64 + EDGE, :] = jnp.where(
            low, frames(begin - EDGE, EDGE).astype(f32), frames(begin + FR, EDGE).astype(f32)
        ).astype(bf16)


def middle_kernel(
    core_ref,
    att_ref,
    residual_ref,
    before_ref,
    after_ref,
    gain_ref,
    own_ref,
    swapped_ref,
    taps_ref,
    vec_ref,
    grad_ref,
    skip_ref,
    stream_ref,
    payload_ref,
    weight_ref,
    normed_ref,
    low_ref,
    linear_ref,
    gate_ref,
    glu_ref,
    grad_ext_ref,
    sums_ref,
    proj_ref,
    hat_ref,
    copy_sem,
):
    core = core_ref[0]

    def copies(column):
        out = []
        for index, (ref, side) in enumerate(((own_ref, core), (swapped_ref, 1 - core))):
            out.append(
                pltpu.make_async_copy(
                    ref.at[:, column],
                    weight_ref.at[pl.ds(side * 16, 16), column],
                    copy_sem.at[2 * column + index],
                )
            )
        return out

    order = [column for part in range(8) for column in (part, part + 8)]
    for column in order:
        for copy in copies(column):
            copy.start()
    lanes = low_lanes(64 + EDGE)
    for pair in range(HEADS // 2):
        cols = slice(128 * pair, 128 * (pair + 1))
        even = att_ref[2 * pair].astype(f32)
        odd = att_ref[2 * pair + 1].astype(f32)
        low = jnp.where(lanes, even, pltpu.roll(odd, HD, 1))
        high = jnp.where(lanes, pltpu.roll(even, HD, 1), odd)
        normed_ref[0:EDGE, cols] = low[64:] + before_ref[0:EDGE, cols].astype(f32)
        normed_ref[EDGE : EDGE + 64, cols] = low[:64] + residual_ref[0:64, cols].astype(f32)
        normed_ref[EDGE + 64 : EDGE + FR, cols] = high[:64] + residual_ref[64:FR, cols].astype(f32)
        normed_ref[EDGE + FR :, cols] = high[64:] + after_ref[0:EDGE, cols].astype(f32)
    stream = normed_ref[...]
    centred = stream - jnp.mean(stream, axis=1, keepdims=True)
    inv_std = lax.rsqrt(jnp.mean(centred * centred, axis=1, keepdims=True) + epsilon)
    normed = centred * inv_std
    normed_ref[...] = normed
    inv_own = inv_std[EDGE : EDGE + FR]
    low_ref[...] = (normed * gain_ref[...]).astype(bf16)
    sums_ref[...] = jnp.zeros_like(sums_ref)
    for part in range(8):
        for column in (part, part + 8):
            for copy in copies(column):
                copy.wait()
        weights = jnp.concatenate(
            [weight_ref[:, part].reshape(D, 128), weight_ref[:, part + 8].reshape(D, 128)], axis=1
        )
        projected = dot(low_ref[...], weights)
        linear = projected[:, :128]
        gate = jax.nn.sigmoid(projected[:, 128:])
        linear_ref[part] = linear[EDGE : EDGE + FR]
        gate_ref[part] = gate[EDGE : EDGE + FR]
        glu_ref[part] = (linear * gate).astype(bf16).astype(f32)
    for part in range(8):
        cols = slice(128 * part, 128 * (part + 1))

        def put(row, total):
            place = (row % 4) * 8 + part
            sums_ref[row // 4, place : place + 1, :] = total

        conv = jnp.zeros((WIDE, 128), f32)
        for tap in range(KW):
            conv = conv + taps_ref[tap : tap + 1, cols] * glu_ref[part, tap + 1 : tap + 1 + WIDE, :]
        gamma = vec_ref[0:1, cols]
        inv_scale = lax.rsqrt(vec_ref[3:4, cols] + epsilon)
        zhat = (conv - vec_ref[2:3, cols]) * inv_scale
        shifted = gamma * zhat + vec_ref[1:2, cols]
        sig = jax.nn.sigmoid(shifted)
        grads = jnp.concatenate(
            [before_ref[EDGE:, cols], grad_ref[:, cols], after_ref[EDGE:, cols]], axis=0
        ).astype(f32)
        grad_shift = grads * sig * (1.0 + shifted * (1.0 - sig))
        grad_ext_ref[...] = (grad_shift * (gamma * inv_scale)).astype(bf16).astype(f32)
        own = slice(EDGE // 2, EDGE // 2 + FR)
        conv, zhat, grad_shift = conv[own], zhat[own], grad_shift[own]
        for row, value in enumerate((grad_shift * zhat, grad_shift, conv, conv * conv)):
            total = jnp.sum(value, axis=0, keepdims=True)
            put(KW + row, total)
            put(KW + 4 + row, total - total.astype(bf16).astype(f32))
        grad_own = grad_ext_ref[own, :]
        for tap in range(KW):
            begin = EDGE + tap - HALF
            put(tap, jnp.sum(grad_own * glu_ref[part, begin : begin + FR, :], axis=0, keepdims=True))
        grad_glu = jnp.zeros((FR, 128), f32)
        for tap in range(KW):
            begin = EDGE // 2 + HALF - tap
            grad_glu = grad_glu + taps_ref[tap : tap + 1, cols] * grad_ext_ref[begin : begin + FR, :]
        gate = gate_ref[part]
        half = grad_glu * gate
        proj_ref[:, cols] = half.astype(bf16)
        proj_ref[:, D + 128 * part : D + 128 * (part + 1)] = (half * linear_ref[part] * (1.0 - gate)).astype(bf16)
    payload_ref[:, 0:PART_ROWS, :] = sums_ref[...].astype(bf16)
    proj = proj_ref[...]
    for part in range(4):
        cols = slice(256 * part, 256 * (part + 1))
        columns = [weight_ref[8 * part : 8 * (part + 1), s].reshape(256, 128) for s in range(16)]
        hat_ref[:, cols] = dot_nt(proj, jnp.concatenate(columns, axis=1)) * gain_ref[:, cols]
    hat = hat_ref[...]
    normed = normed_ref[EDGE : EDGE + FR, :]
    mean = jnp.mean(hat, axis=1, keepdims=True)
    mean_normed = jnp.mean(hat * normed, axis=1, keepdims=True)
    centre = inv_own * (hat - mean - normed * mean_normed)
    stream = (centre + skip_ref[...].astype(f32)).astype(bf16)
    stream_ref[...] = stream
    for pair in range(HEADS // 2):
        turned = stream[:, 128 * pair : 128 * (pair + 1)].T
        payload_ref[2 * pair, PART_ROWS:, :] = turned[:HD]
        payload_ref[2 * pair + 1, PART_ROWS:, :] = turned[HD:]


def spread_kernel(payload_ref, out_ref):
    total = jnp.sum(payload_ref[...].astype(f32), axis=0)
    out_ref[...] = jnp.broadcast_to(total[None], out_ref.shape)


def backward_kernel(
    qkv_ref,
    edge_att_ref,
    mid_att_ref,
    edge_log_ref,
    mid_log_ref,
    payload_ref,
    out_ref,
    keys_ref,
    values_ref,
    query_ref,
    grad_ref,
    query_rows_ref,
    grad_rows_ref,
    turned_ref,
    total_ref,
):
    pad_rows = lax.broadcasted_iota(jnp.int32, (HD, FR), 0)
    ones = jnp.where(pad_rows < 3, 1.0, 0.0).astype(bf16)
    for source in range(HEADS):
        span = slice(FR * source, FR * (source + 1))
        key_block = qkv_ref[source, HD : 2 * HD, :]
        turned_ref[:, span] = key_block
        keys_ref[span, :] = jnp.concatenate([key_block, ones], axis=0).T
        values_ref[span, :] = jnp.concatenate([qkv_ref[source, 2 * HD :, :], ones], axis=0).T
        grads = payload_ref[source, PART_ROWS:, :]
        block, side = divmod(source, 2)
        if 0 < block < CHUNKS - 1:
            att, log, block = mid_att_ref, mid_log_ref, block - 1
        else:
            att, log, block = edge_att_ref, edge_log_ref, min(block, 1)
        lanes = slice(FR * side, FR * (side + 1))
        delta = jnp.sum(grads.astype(f32) * att[block, :, lanes].astype(f32), axis=0, keepdims=True)
        logs = log[block, 0:1, lanes] * (1.0 / (SCALE * LOG2E))
        for ref, rows_ref, body, row in (
            (query_ref, query_rows_ref, qkv_ref[source, 0:HD, :], logs),
            (grad_ref, grad_rows_ref, grads, delta),
        ):
            parts = three_parts(jnp.broadcast_to(-row, (HD, FR)))
            tail = jnp.zeros((HD, FR), f32)
            for place in range(3):
                tail = jnp.where(pad_rows == place, parts[place].astype(f32), tail)
            both = jnp.concatenate([body, tail.astype(bf16)], axis=0)
            ref[:, span] = both
            rows_ref[span, :] = both.T
    total_ref[...] = jnp.zeros_like(total_ref)

    def step(block, carry):
        rows = block_rows(block)
        keys, values, turned = keys_ref[rows, :], values_ref[rows, :], turned_ref[:, rows]

        def products(chunk):
            cols = block_rows(chunk)
            return dot(keys, query_ref[:, cols]), dot(values, grad_ref[:, cols])

        key_total = jnp.zeros((BLOCK, 128), f32)
        value_total = jnp.zeros((BLOCK, 128), f32)
        ready = products(0)
        for chunk in range(CHUNKS):
            cols = block_rows(chunk)
            scores, grad_probs = ready
            if chunk + 1 < CHUNKS:
                ready = products(chunk + 1)
            probs = jnp.exp2(scores * (SCALE * LOG2E))
            grad_scores = (probs * grad_probs).astype(bf16)
            value_total = value_total + dot(probs.astype(bf16), grad_rows_ref[cols, :])
            key_total = key_total + dot(grad_scores, query_rows_ref[cols, :])
            total_ref[:, cols] += dot(turned, grad_scores)
        for place, total in ((1, key_total * SCALE), (2, value_total)):
            turned_total = total.T[:HD].astype(bf16)
            out_ref[2 * block, HD * place : HD * (place + 1), :] = turned_total[:, :FR]
            out_ref[2 * block + 1, HD * place : HD * (place + 1), :] = turned_total[:, FR:]
        return carry

    lax.fori_loop(0, CHUNKS, step, 0)
    for source in range(HEADS):
        span = slice(FR * source, FR * (source + 1))
        out_ref[source, 0:HD, :] = (total_ref[:, span] * SCALE).astype(bf16)


def finish_kernel(parts_ref, payload_ref, out_ref):
    total = jnp.sum(parts_ref[...], axis=0).astype(bf16)
    out_ref[...] = jnp.broadcast_to(total[None], out_ref.shape)


def unpack_kernel(frame_total, back_ref, query_ref, key_ref, value_ref, taps_ref, affine_ref, moments_ref):
    for item, ref in enumerate((query_ref, key_ref, value_ref)):
        for pair in range(HEADS // 2):
            turned = back_ref[2 * pair : 2 * pair + 2, HD * item : HD * (item + 1), :].reshape(128, FR)
            ref[:, 128 * pair : 128 * (pair + 1)] = turned.T
    totals = [back_ref[source, 3 * HD :, :].astype(f32) for source in range(10)]

    def fetch(row, part):
        place = (row % 4) * 8 + part
        return totals[row // 4][place : place + 1]

    for part in range(8):
        cols = slice(128 * part, 128 * (part + 1))
        for row in range(KW):
            taps_ref[row : row + 1, cols] = fetch(row, part)
        for row in range(4):
            ref, factor = (affine_ref, 1.0) if row < 2 else (moments_ref, 1.0 / frame_total)
            total = fetch(KW + row, part) + fetch(KW + 4 + row, part)
            ref[row % 2 : row % 2 + 1, cols] = total * factor


def call(kernel, out_shape, *args, scratch=(), gflops=0, **extra):
    if gflops:
        extra["cost_estimate"] = pl.CostEstimate(
            flops=gflops * 10**9, bytes_accessed=4 * 2**20, transcendentals=STRETCH * STRETCH
        )
    return pl.pallas_call(
        kernel, out_shape=out_shape, scratch_shapes=list(scratch), compiler_params=params(), **extra
    )(*args)


def shape(dims, dtype):
    return jax.ShapeDtypeStruct(dims, dtype)


def whole(*dims):
    return pl.BlockSpec(dims, lambda i: (0,) * len(dims))


def rows_at(count, index):
    return pl.BlockSpec((count, D), lambda i: (index, 0))


def gather_half(proj_weight):
    place = lax.axis_index("tm")
    chunk = lax.rem(place, 2) * 16 + place // 2
    own = lax.dynamic_slice_in_dim(proj_weight, chunk * 32, 32, axis=0)
    own = jnp.broadcast_to(own[None], (HEADS, 32, 128))
    rows = lax.all_to_all(own, "seq", 0, 0, tiled=True)
    chips = [[2 * chip + core for chip in range(16)] for core in range(2)]
    return lax.all_gather(rows, "tm", axis=0, axis_index_groups=chips)


def swap_half(half):
    pairs = [(place, place ^ 1) for place in range(lax.axis_size("tm"))]
    return lax.ppermute(half, "tm", pairs)


def neighbours(axes, first, last):
    size = lax.axis_size(axes)
    up = [(i, i + 1) for i in range(size - 1)]
    down = [(i + 1, i) for i in range(size - 1)]
    return lax.ppermute(last, axes, up), lax.ppermute(first, axes, down)


def local(
    query_in,
    key_in,
    value_in,
    residual,
    layer_gain,
    proj_weight,
    conv_kernel,
    batch_gamma,
    batch_beta,
    stale_mean,
    stale_variance,
    grad_conv,
    grad_stream_in,
):
    groups = lax.axis_size("tm")
    frame_total = FR * groups * lax.axis_size("seq")
    half = gather_half(proj_weight)
    gain = layer_gain.reshape(1, D)
    vectors = jnp.stack([batch_gamma, batch_beta, stale_mean, stale_variance])
    core = lax.rem(lax.axis_index("tm"), 2).reshape(1)

    edge_rows = EDGE + EDGE // 2
    packed, first, last = call(
        pack_kernel,
        (shape((HEADS, 3 * HD, FR), bf16), shape((edge_rows, D), bf16), shape((edge_rows, D), bf16)),
        query_in,
        key_in,
        value_in,
        residual,
        residual,
        grad_conv,
        grad_conv,
        grid=(1,),
        in_specs=[whole(FR, D)] * 3 + [rows_at(EDGE, 0), rows_at(EDGE, 3), rows_at(16, 0), rows_at(16, 7)],
        out_specs=(whole(HEADS, 3 * HD, FR), whole(edge_rows, D), whole(edge_rows, D)),
    )
    qkv = lax.all_to_all(packed, "seq", 0, 0, tiled=True)
    before, after = neighbours(("tm", "seq"), first, last)
    square = shape((STRETCH, 128), bf16)
    scores = [pltpu.VMEM((BLOCK, STRETCH), f32)] * 2
    keys, queries, values, edge_nat, edge_att, edge_log, first, last = call(
        edge_forward_kernel,
        (
            shape((128, STRETCH), bf16),
            square,
            square,
            shape((2 * BLOCK, 128), bf16),
            shape((2, HD, BLOCK), bf16),
            shape((2, 8, BLOCK), f32),
            shape((EDGE, 128), bf16),
            shape((EDGE, 128), bf16),
        ),
        qkv,
        scratch=scores,
    )
    edge_before, edge_after = neighbours("tm", first, last)
    mid_nat, mid_att, mid_log = call(
        middle_forward_kernel,
        (
            shape((STRETCH - 2 * BLOCK, 128), bf16),
            shape((CHUNKS - 2, HD, BLOCK), bf16),
            shape((CHUNKS - 2, 8, BLOCK), f32),
        ),
        keys,
        queries,
        values,
        scratch=scores,
        gflops=6,
    )
    att_payload = call(
        assemble_kernel,
        shape((HEADS, 64 + EDGE, 128), bf16),
        edge_nat,
        mid_nat,
        edge_before,
        edge_after,
    )
    half, _ = lax.optimization_barrier((half, att_payload))
    swapped = swap_half(half)
    att_rows = lax.all_to_all(att_payload, "seq", 0, 0, tiled=True)
    in_vmem = pl.BlockSpec(memory_space=pltpu.VMEM)
    in_place = pl.BlockSpec(memory_space=pl.ANY)
    grad_stream, payload = call(
        middle_kernel,
        (shape((FR, D), bf16), shape((HEADS, PART_ROWS + HD, FR), bf16)),
        core,
        att_rows,
        residual,
        before,
        after,
        gain,
        half,
        swapped,
        conv_kernel,
        vectors,
        grad_conv,
        grad_stream_in,
        in_specs=[pl.BlockSpec(memory_space=pltpu.SMEM)]
        + [in_vmem] * 5
        + [in_place] * 2
        + [in_vmem] * 4,
        scratch=(
            pltpu.VMEM((32, HEADS, 32, 128), bf16),
            pltpu.VMEM((ROWS, D), f32),
            pltpu.VMEM((ROWS, D), bf16),
            pltpu.VMEM((8, FR, 128), f32),
            pltpu.VMEM((8, FR, 128), f32),
            pltpu.VMEM((8, ROWS, 128), f32),
            pltpu.VMEM((WIDE, 128), f32),
            pltpu.VMEM((HEADS, PART_ROWS, 128), f32),
            pltpu.VMEM((FR, 2 * D), bf16),
            pltpu.VMEM((FR, D), f32),
            pltpu.SemaphoreType.DMA((2 * HEADS,)),
        ),
    )
    payload = lax.all_to_all(payload, "seq", 0, 0, tiled=True)
    spread = call(
        spread_kernel,
        shape((groups, PART_ROWS, 128), f32),
        payload,
        grid=(1,),
        in_specs=[whole(HEADS, PART_ROWS, 128)],
        out_specs=whole(groups, PART_ROWS, 128),
    )
    totals = lax.all_to_all(spread, "tm", 0, 0, tiled=True)
    tall = pltpu.VMEM((STRETCH, 128), bf16)
    flat = pltpu.VMEM((128, STRETCH), bf16)
    back = call(
        backward_kernel,
        shape((HEADS, 3 * HD + PART_ROWS, FR), bf16),
        qkv,
        edge_att,
        mid_att,
        edge_log,
        mid_log,
        payload,
        gflops=12,
        scratch=(
            tall,
            tall,
            flat,
            flat,
            tall,
            tall,
            pltpu.VMEM((HD, STRETCH), bf16),
            pltpu.VMEM((HD, STRETCH), f32),
        ),
    )
    back = call(
        finish_kernel,
        shape(back.shape, bf16),
        totals,
        back,
        grid=(1,),
        in_specs=[whole(groups, PART_ROWS, 128), in_place],
        out_specs=pl.BlockSpec((HEADS, PART_ROWS, 128), lambda i: (0, 6, 0)),
        input_output_aliases={1: 0},
    )
    back = lax.all_to_all(back, "seq", 0, 0, tiled=True)
    narrow = shape((FR, D), bf16)
    query_grad, key_grad, value_grad, kernel_sum, affine_sum, moments = call(
        lambda *refs: unpack_kernel(frame_total, *refs),
        (narrow, narrow, narrow, shape((KW, D), f32), shape((2, D), f32), shape((2, D), f32)),
        back,
    )
    return (query_grad, key_grad, value_grad, grad_stream, kernel_sum, affine_sum, moments)


def solution(mesh):
    rows = P(("tm", "seq"), None)
    in_specs = (rows, rows, rows, rows, P(), P(None, "seq"), P(), P(), P(), P(), P(), rows, rows)
    out_specs = (rows, rows, rows, rows, P(), P(), P())
    return jax.shard_map(local, mesh=mesh, in_specs=in_specs, out_specs=out_specs, check_vma=False)
```

time: 318 us -> 264 us (0.83)
  the two profiles are of different devices: /device:TPU:18 before, /device:TPU:8 now
where the time goes in v2:
time: 264 us; the launch traced here: 263 us
  blocking collectives  127 us (48%)
  waiting for transfers between devices  42 us (16%)
  starting transfers between devices  38.6 us (15%)
  Pallas kernels  33.9 us (13%)
  between operations  14.3 us (5%)
  local copies, waits for them, and re-layouts  7.29 us (3%)
    all_to_all x1, blocking collectives, local(): qkv = lax.all_to_all(packed, 'seq', 0, 0, tiled=True)  41.8 us
    all_to_all x1, blocking collectives, local(): back = lax.all_to_all(back, 'seq', 0, 0, tiled=True)  35.6 us
    pallas_call x9, Pallas kernels, call(): pl.pallas_call(kernel, out_shape=out_shape, scratch_shapes=list(scratch),...  33.9 us
    all_to_all x1, blocking collectives, gather_half(): rows = lax.all_to_all(own, 'seq', 0, 0, tiled=True)  28.1 us
    all_gather x1, waiting for transfers between devices, gather_half(): return lax.all_gather(rows, 'tm', axis=0, axis_index_groups=chips)  26 us
    all_to_all x1, blocking collectives, local(): payload = lax.all_to_all(payload, 'seq', 0, 0, tiled=True)  21.1 us
    ppermute x4, starting transfers between devices, neighbours(): return (lax.ppermute(last, axes, up), lax.ppermute(first, axes, down))  16.7 us
    ppermute x4, waiting for transfers between devices, neighbours(): return (lax.ppermute(last, axes, up), lax.ppermute(first, axes, down))  13.2 us
  transfers between devices with their start and end apart: 8, of which 3 were waited for; matrix products, arithmetic and copies ran while one was open for 0% of the time, Pallas kernels for 8%

profile of v2, /device:TPU:8, one launch (start us, length us, event | category | flops | bytes accessed | tf_op | source)
XLA Modules:
  0.0 262.8 jit_solution(4624465663956736011)
XLA Ops:
  8.1 28.1 %all_to_all.30 = bf16[16,32,128]{2,1,0:T(8,128)(2,1)} all-to-all(bf16[16,32,128]{2,1,0:T(8,128)(2,1)S(1)} %broadcast_in_dim.2), channel_id=1, replica_groups=mesh['tm'=32,'seq'=16] {'seq'}, dimensions={0} | all-to-all | bytes 262144 | tf_op jit(solution)/shard_map/all_to_all | solution.py:479
  37.3 0.9 copy-done.3
  38.2 0.9 copy-done.6
  39.2 0.9 copy-done.7
  40.1 0.9 copy-done.8
  41.3 41.8 %all_to_all.31.qkv_ref = bf16[16,192,128]{2,1,0:T(8,128)(2,1)S(1)} all-to-all(bf16[16,192,128]{2,1,0:T(8,128)(2,1)S(1)} %get-tuple-element.30), channel_id=1, replica_groups=mesh['tm'=32,'seq'=16] {'seq'}, dimensions={0} | all-to-all | bytes 1572864 | tf_op jit(solution)/shard_map/all_to_all | solution.py:533
  83.1 1.9 shard_map.181
  85.0 1.9 collective-permute-start
  87.0 3.6 %collective-permute-start.1 = (bf16[32,128]{1,0:T(8,128)(2,1)S(1)}, bf16[32,128]{1,0:T(8,128)(2,1)S(1)}, u32[]{:S(2)}, u32[]{:S(2)}) collective-permute-start(bf16[32,128]{1,0:T(8,128)(2,1)S(1)} %get-tuple-element.37), channel_id=1, source_target_pairs={{16,0},{32,16},{48,32},{64,48},{80,64},{96,80},{112,96},{128,112},... | collective-permute-start | bytes 24584 | tf_op jit(solution)/shard_map/ppermute | solution.py:493
  90.7 6.2 %shard_map.182 = (bf16[1536,128]{1,0:T(8,128)(2,1)S(1)}, bf16[6,64,256]{2,1,0:T(8,128)(2,1)S(1)}, f32[6,8,256]{2,1,0:T(8,128)S(1)}) custom-call(bf16[128,2048]{1,0:T(8,128)(2,1)S(1)} %get-tuple-element.32.keys_ref, bf16[2048,128]{1,0:T(8,128)(2,1)S(1)} %get-tuple-element.33.query_ref, bf16[2048,128]{1,0:T(8,128)(2,1)S(1)} %get-tuple-element.34.value_ref), custom_call_target="tpu_custom_call" | custom-call | flops 6000000000 | bytes 4194304 | tf_op jit(solution)/shard_map/pallas_call | solution.py:457
  97.8 26.0 %all-gather.3.cloned.1.call-done = bf16[256,32,128]{2,1,0:T(8,128)(2,1)} async-done(((bf16[16,32,128]{2,1,0:T(8,128)(2,1)}), bf16[256,32,128]{2,1,0:T(8,128)(2,1)}) %all-gather.3.cloned.1.call-update) | async-done | bytes 2097168 | tf_op jit(solution)/shard_map/all_gather | solution.py:481
  123.8 1.9 collective-permute-start.4
  125.7 12.3 %all-to-all-start.1 = ((bf16[16,96,128]{2,1,0:T(8,128)(2,1)}), bf16[16,96,128]{2,1,0:T(8,128)(2,1)S(1)}, u32[]{:S(2)}, u32[]{:S(2)}) async-start(bf16[16,96,128]{2,1,0:T(8,128)(2,1)} %shard_map.183), calls=%async_computation.1 | async-start | bytes 786432 | tf_op jit(solution)/shard_map/all_to_all | solution.py:576
  138.0 7.7 %collective-permute-start.2 = (bf16[48,1024]{1,0:T(8,128)(2,1)S(1)}, bf16[48,1024]{1,0:T(8,128)(2,1)S(1)}, u32[]{:S(2)}, u32[]{:S(2)}) collective-permute-start(bf16[48,1024]{1,0:T(8,128)(2,1)S(1)} %get-tuple-element.38), channel_id=1, source_target_pairs={{0,1},{1,2},{2,3},{3,4},{4,5},{5,6},{6,7},{7,8},{8,9},{9,10},{10,1... | collective-permute-start | bytes 294920 | tf_op jit(solution)/shard_map/ppermute | solution.py:493
  145.8 3.4 %collective-permute-start.3 = (bf16[48,1024]{1,0:T(8,128)(2,1)S(1)}, bf16[48,1024]{1,0:T(8,128)(2,1)S(1)}, u32[]{:S(2)}, u32[]{:S(2)}) collective-permute-start(bf16[48,1024]{1,0:T(8,128)(2,1)S(1)} %get-tuple-element.39), channel_id=1, source_target_pairs={{1,0},{2,1},{3,2},{4,3},{5,4},{6,5},{7,6},{8,7},{9,8},{10,9},{11,1... | collective-permute-start | bytes 294920 | tf_op jit(solution)/shard_map/ppermute | solution.py:493
  149.2 13.2 %collective-permute-done.2.before_ref = bf16[48,1024]{1,0:T(8,128)(2,1)S(1)} collective-permute-done((bf16[48,1024]{1,0:T(8,128)(2,1)S(1)}, bf16[48,1024]{1,0:T(8,128)(2,1)S(1)}, u32[]{:S(2)}, u32[]{:S(2)}) %collective-permute-start.2) | collective-permute-done | bytes 98336 | tf_op jit(solution)/shard_map/ppermute | solution.py:493
  162.5 1.6 copy-done.5
  164.0 10.5 %shard_map.184 = (bf16[128,1024]{1,0:T(8,128)(2,1)}, bf16[16,96,128]{2,1,0:T(8,128)(2,1)S(1)}) custom-call(s32[1]{0:T(128)} %bitcast.core_ref, bf16[16,96,128]{2,1,0:T(8,128)(2,1)S(1)} %all-to-all-done.1.att_ref, bf16[128,1024]{1,0:T(8,128)(2,1)S(1)} %copy-done.2, bf16[48,1024]{1,0:T(8,128)(2,1)S(1)} %collective-permute-done.2.before_ref, ...), custom_call_target="tpu_custom_call" | custom-call | tf_op jit(solution)/shard_map/pallas_call | solution.py:457
  174.5 21.1 %all_to_all.32.payload_ref = bf16[16,96,128]{2,1,0:T(8,128)(2,1)S(1)} all-to-all(bf16[16,96,128]{2,1,0:T(8,128)(2,1)S(1)} %get-tuple-element.41), channel_id=1, replica_groups=mesh['tm'=32,'seq'=16] {'seq'}, dimensions={0} | all-to-all | bytes 786432 | tf_op jit(solution)/shard_map/all_to_all | solution.py:612
  196.5 7.7 %all-to-all-start.4 = ((f32[32,32,128]{2,1,0:T(8,128)}), f32[32,32,128]{2,1,0:T(8,128)S(1)}, u32[]{:S(2)}, u32[]{:S(2)}) async-start(f32[32,32,128]{2,1,0:T(8,128)} %shard_map.185), calls=%async_computation.4 | async-start | bytes 1048576 | tf_op jit(solution)/shard_map/all_to_all | solution.py:621
  204.2 12.2 %shard_map.186.payload_ref = bf16[16,224,128]{2,1,0:T(8,128)(2,1)S(1)} custom-call(bf16[16,192,128]{2,1,0:T(8,128)(2,1)S(1)} %all_to_all.31.qkv_ref, bf16[2,64,256]{2,1,0:T(8,128)(2,1)S(1)} %get-tuple-element.42.edge_att_ref, bf16[6,64,256]{2,1,0:T(8,128)(2,1)S(1)} %get-tuple-element.43.mid_att_ref, f32[2,8,256]{2,1,0:T(8,128)S(1)} %get-tuple-element.44.edge_log_ref, ...), custom_call_target="tpu_custom_call" | custom-call | flops 12000000000 | bytes 4194304 | tf_op jit(solution)/shard_map/pallas_call | solution.py:457
  216.4 2.8 %all-to-all-done.4.parts_ref = f32[32,32,128]{2,1,0:T(8,128)S(1)} async-done(((f32[32,32,128]{2,1,0:T(8,128)}), f32[32,32,128]{2,1,0:T(8,128)S(1)}, u32[]{:S(2)}, u32[]{:S(2)}) %all-to-all-start.4) | async-done | bytes 524320 | tf_op jit(solution)/shard_map/all_to_all | solution.py:621
  219.3 35.6 %all_to_all.33.refs_0_ = bf16[16,224,128]{2,1,0:T(8,128)(2,1)S(1)} all-to-all(bf16[16,224,128]{2,1,0:T(8,128)(2,1)S(1)} %shard_map.187), channel_id=1, replica_groups=mesh['tm'=32,'seq'=16] {'seq'}, dimensions={0} | all-to-all | bytes 1835008 | tf_op jit(solution)/shard_map/all_to_all | solution.py:655
  254.9 1.1 shard_map.188
  (41 shorter events, 4.0 us)
Async XLA Ops:
  7.2 1.0 copy-start
  7.2 116.6 %all-gather.3.cloned.1.call-start = ((), (), s32[]{:S(2)}) async-start(), calls=%async_computation.6 | async-start | bytes 2228224 | tf_op jit(solution)/shard_map/all_gather | solution.py:481
  36.3 1.0 copy-start.1
  37.3 0.9 copy-start.3
  38.2 0.9 copy-start.6
  39.2 0.9 copy-start.7
  40.1 0.9 copy-start.8
  85.0 11.9 %collective-permute-start = (bf16[32,128]{1,0:T(8,128)(2,1)S(1)}, bf16[32,128]{1,0:T(8,128)(2,1)S(1)}, u32[]{:S(2)}, u32[]{:S(2)}) collective-permute-start(bf16[32,128]{1,0:T(8,128)(2,1)S(1)} %get-tuple-element.36), channel_id=1, source_target_pairs={{0,16},{16,32},{32,48},{48,64},{64,80},{80,96},{96,112},{112,128},... | collective-permute-start | bytes 24584 | tf_op jit(solution)/shard_map/ppermute | solution.py:493
  87.0 10.0 %collective-permute-start.1 = (bf16[32,128]{1,0:T(8,128)(2,1)S(1)}, bf16[32,128]{1,0:T(8,128)(2,1)S(1)}, u32[]{:S(2)}, u32[]{:S(2)}) collective-permute-start(bf16[32,128]{1,0:T(8,128)(2,1)S(1)} %get-tuple-element.37), channel_id=1, source_target_pairs={{16,0},{32,16},{48,32},{64,48},{80,64},{96,80},{112,96},{128,112},... | collective-permute-start | bytes 24584 | tf_op jit(solution)/shard_map/ppermute | solution.py:493
  90.6 58.5 %copy-start.12 = (f32[1024]{0:T(1024)S(1)}, f32[1024]{0:T(1024)}, u32[]{:S(2)}) copy-start(f32[1024]{0:T(1024)} %param.23) | copy-start | bytes 12292
  90.6 58.5 %copy-start.13 = (f32[1024]{0:T(1024)S(1)}, f32[1024]{0:T(1024)}, u32[]{:S(2)}) copy-start(f32[1024]{0:T(1024)} %param.22) | copy-start | bytes 12292
  90.6 58.5 %copy-start.14 = (f32[1024]{0:T(1024)S(1)}, f32[1024]{0:T(1024)}, u32[]{:S(2)}) copy-start(f32[1024]{0:T(1024)} %param.21) | copy-start | bytes 12292
  90.6 58.5 %copy-start.15 = (f32[1024]{0:T(1024)S(1)}, f32[1024]{0:T(1024)}, u32[]{:S(2)}) copy-start(f32[1024]{0:T(1024)} %param.20) | copy-start | bytes 12292
  90.7 71.7 %copy-start.2 = (bf16[128,1024]{1,0:T(8,128)(2,1)S(1)}, bf16[128,1024]{1,0:T(8,128)(2,1)}, u32[]{:S(2)}) copy-start(bf16[128,1024]{1,0:T(8,128)(2,1)} %residual_ref.1) | copy-start | bytes 786436
  90.7 71.7 %copy-start.4 = (bf16[128,1024]{1,0:T(8,128)(2,1)S(1)}, bf16[128,1024]{1,0:T(8,128)(2,1)}, u32[]{:S(2)}) copy-start(bf16[128,1024]{1,0:T(8,128)(2,1)} %grad_ref.1) | copy-start | bytes 786436
  90.7 71.7 %copy-start.9 = (bf16[128,1024]{1,0:T(8,128)(2,1)S(1)}, bf16[128,1024]{1,0:T(8,128)(2,1)}, u32[]{:S(2)}) copy-start(bf16[128,1024]{1,0:T(8,128)(2,1)} %skip_ref.1) | copy-start | bytes 786436
  90.7 71.7 %copy-start.10 = (f32[31,1024]{1,0:T(8,128)S(1)}, f32[31,1024]{1,0:T(8,128)}, u32[]{:S(2)}) copy-start(f32[31,1024]{1,0:T(8,128)} %taps_ref.1) | copy-start | bytes 380932
  90.7 71.7 %copy-start.11 = (f32[1024]{0:T(1024)S(1)}, f32[1024]{0:T(1024)}, u32[]{:S(2)}) copy-start(f32[1024]{0:T(1024)} %param.17) | copy-start | bytes 12292
  123.8 38.6 %collective-permute-start.4 = (bf16[16,16,32,128]{3,2,1,0:T(8,128)(2,1)}, bf16[16,16,32,128]{3,2,1,0:T(8,128)(2,1)}, u32[]{:S(2)}, u32[]{:S(2)}) collective-permute-start(bf16[16,16,32,128]{3,2,1,0:T(8,128)(2,1)} %bitcast.7), channel_id=1, source_target_pairs={{0,16},{16,0},{32,48},{48,32},{64,80},{80,64},{96,112},{112,96},{1... | collective-permute-start | bytes 6291464 | tf_op jit(solution)/shard_map/ppermute | solution.py:486
  125.7 36.6 %all-to-all-start.1 = ((bf16[16,96,128]{2,1,0:T(8,128)(2,1)}), bf16[16,96,128]{2,1,0:T(8,128)(2,1)S(1)}, u32[]{:S(2)}, u32[]{:S(2)}) async-start(bf16[16,96,128]{2,1,0:T(8,128)(2,1)} %shard_map.183), calls=%async_computation.1 | async-start | bytes 786432 | tf_op jit(solution)/shard_map/all_to_all | solution.py:576
  138.0 24.4 %collective-permute-start.2 = (bf16[48,1024]{1,0:T(8,128)(2,1)S(1)}, bf16[48,1024]{1,0:T(8,128)(2,1)S(1)}, u32[]{:S(2)}, u32[]{:S(2)}) collective-permute-start(bf16[48,1024]{1,0:T(8,128)(2,1)S(1)} %get-tuple-element.38), channel_id=1, source_target_pairs={{0,1},{1,2},{2,3},{3,4},{4,5},{5,6},{6,7},{7,8},{8,9},{9,10},{10,1... | collective-permute-start | bytes 294920 | tf_op jit(solution)/shard_map/ppermute | solution.py:493
  145.8 16.6 %collective-permute-start.3 = (bf16[48,1024]{1,0:T(8,128)(2,1)S(1)}, bf16[48,1024]{1,0:T(8,128)(2,1)S(1)}, u32[]{:S(2)}, u32[]{:S(2)}) collective-permute-start(bf16[48,1024]{1,0:T(8,128)(2,1)S(1)} %get-tuple-element.39), channel_id=1, source_target_pairs={{1,0},{2,1},{3,2},{4,3},{5,4},{6,5},{7,6},{8,7},{9,8},{10,9},{11,1... | collective-permute-start | bytes 294920 | tf_op jit(solution)/shard_map/ppermute | solution.py:493
  162.4 1.6 copy-start.5
  196.5 22.8 %all-to-all-start.4 = ((f32[32,32,128]{2,1,0:T(8,128)}), f32[32,32,128]{2,1,0:T(8,128)S(1)}, u32[]{:S(2)}, u32[]{:S(2)}) async-start(f32[32,32,128]{2,1,0:T(8,128)} %shard_map.185), calls=%async_computation.4 | async-start | bytes 1048576 | tf_op jit(solution)/shard_map/all_to_all | solution.py:621
Sparse Core Ops, SparseCore 0:
  36.4 87.3 all-gather.2

commit v3 on v2

--- a/solution.py
+++ b/solution.py
@@ -55,26 +55,47 @@
 
 
 def pack_kernel(
+    chunk_ref,
+    query_hbm,
+    key_hbm,
+    value_hbm,
+    weight_hbm,
+    res_hbm,
+    grad_hbm,
+    out_ref,
+    first_ref,
+    last_ref,
     query_ref,
     key_ref,
     value_ref,
-    res_first_ref,
-    res_last_ref,
-    grad_first_ref,
-    grad_last_ref,
-    out_ref,
-    first_ref,
-    last_ref,
+    weight_ref,
+    copy_sem,
 ):
+    weight_rows = weight_hbm.at[pl.ds(pl.multiple_of(chunk_ref[0] * 128, 128), 128)]
+    pairs = (
+        (query_hbm, query_ref),
+        (key_hbm, key_ref),
+        (value_hbm, value_ref),
+        (weight_rows, weight_ref),
+        (res_hbm.at[0:EDGE], first_ref.at[0:EDGE]),
+        (res_hbm.at[FR - EDGE : FR], last_ref.at[0:EDGE]),
+        (grad_hbm.at[0:16], first_ref.at[EDGE : EDGE + 16]),
+        (grad_hbm.at[FR - 16 : FR], last_ref.at[EDGE : EDGE + 16]),
+    )
+    copies = [pltpu.make_async_copy(src, dst, copy_sem.at[i]) for i, (src, dst) in enumerate(pairs)]
+    for copy in copies:
+        copy.start()
     for item, ref in enumerate((query_ref, key_ref, value_ref)):
+        copies[item].wait()
         for pair in range(HEADS // 2):
             turned = ref[:, 128 * pair : 128 * (pair + 1)].T
             out_ref[2 * pair, HD * item : HD * (item + 1), :] = turned[:HD]
             out_ref[2 * pair + 1, HD * item : HD * (item + 1), :] = turned[HD:]
-    first_ref[:EDGE] = res_first_ref[...]
-    first_ref[EDGE:] = grad_first_ref[...]
-    last_ref[:EDGE] = res_last_ref[...]
-    last_ref[EDGE:] = grad_last_ref[...]
+    copies[3].wait()
+    for dest in range(HEADS):
+        out_ref[dest, 3 * HD :, :] = weight_ref[...]
+    for copy in copies[4:]:
+        copy.wait()
 
 
 CHUNKS = STRETCH // BLOCK
@@ -205,14 +226,12 @@
 
 
 def middle_kernel(
-    core_ref,
     att_ref,
     residual_ref,
     before_ref,
     after_ref,
     gain_ref,
-    own_ref,
-    swapped_ref,
+    weight_hbm,
     taps_ref,
     vec_ref,
     grad_ref,
@@ -231,24 +250,12 @@
     hat_ref,
     copy_sem,
 ):
-    core = core_ref[0]
-
-    def copies(column):
-        out = []
-        for index, (ref, side) in enumerate(((own_ref, core), (swapped_ref, 1 - core))):
-            out.append(
-                pltpu.make_async_copy(
-                    ref.at[:, column],
-                    weight_ref.at[pl.ds(side * 16, 16), column],
-                    copy_sem.at[2 * column + index],
-                )
-            )
-        return out
-
-    order = [column for part in range(8) for column in (part, part + 8)]
-    for column in order:
-        for copy in copies(column):
-            copy.start()
+    def fetch(column):
+        return pltpu.make_async_copy(weight_hbm.at[:, column], weight_ref.at[:, column], copy_sem.at[column])
+
+    for part in range(8):
+        fetch(part).start()
+        fetch(part + 8).start()
     lanes = low_lanes(64 + EDGE)
     for pair in range(HEADS // 2):
         cols = slice(128 * pair, 128 * (pair + 1))
@@ -269,9 +276,8 @@
     low_ref[...] = (normed * gain_ref[...]).astype(bf16)
     sums_ref[...] = jnp.zeros_like(sums_ref)
     for part in range(8):
-        for column in (part, part + 8):
-            for copy in copies(column):
-                copy.wait()
+        fetch(part).wait()
+        fetch(part + 8).wait()
         weights = jnp.concatenate(
             [weight_ref[:, part].reshape(D, 128), weight_ref[:, part + 8].reshape(D, 128)], axis=1
         )
@@ -323,7 +329,7 @@
     proj = proj_ref[...]
     for part in range(4):
         cols = slice(256 * part, 256 * (part + 1))
-        columns = [weight_ref[8 * part : 8 * (part + 1), s].reshape(256, 128) for s in range(16)]
+        columns = [weight_ref[2 * part : 2 * (part + 1), s].reshape(256, 128) for s in range(16)]
         hat_ref[:, cols] = dot_nt(proj, jnp.concatenate(columns, axis=1)) * gain_ref[:, cols]
     hat = hat_ref[...]
     normed = normed_ref[EDGE : EDGE + FR, :]
@@ -367,7 +373,7 @@
         key_block = qkv_ref[source, HD : 2 * HD, :]
         turned_ref[:, span] = key_block
         keys_ref[span, :] = jnp.concatenate([key_block, ones], axis=0).T
-        values_ref[span, :] = jnp.concatenate([qkv_ref[source, 2 * HD :, :], ones], axis=0).T
+        values_ref[span, :] = jnp.concatenate([qkv_ref[source, 2 * HD : 3 * HD, :], ones], axis=0).T
         grads = payload_ref[source, PART_ROWS:, :]
         block, side = divmod(source, 2)
         if 0 < block < CHUNKS - 1:
@@ -463,27 +469,22 @@
     return jax.ShapeDtypeStruct(dims, dtype)
 
 
+def in_high_memory(array):
+    return pltpu.with_memory_space_constraint(array, pltpu.HBM)
+
+
 def whole(*dims):
     return pl.BlockSpec(dims, lambda i: (0,) * len(dims))
 
 
-def rows_at(count, index):
-    return pl.BlockSpec((count, D), lambda i: (index, 0))
-
-
-def gather_half(proj_weight):
+def weight_chunk():
     place = lax.axis_index("tm")
-    chunk = lax.rem(place, 2) * 16 + place // 2
-    own = lax.dynamic_slice_in_dim(proj_weight, chunk * 32, 32, axis=0)
-    own = jnp.broadcast_to(own[None], (HEADS, 32, 128))
-    rows = lax.all_to_all(own, "seq", 0, 0, tiled=True)
-    chips = [[2 * chip + core for chip in range(16)] for core in range(2)]
-    return lax.all_gather(rows, "tm", axis=0, axis_index_groups=chips)
-
-
-def swap_half(half):
-    pairs = [(place, place ^ 1) for place in range(lax.axis_size("tm"))]
-    return lax.ppermute(half, "tm", pairs)
+    return (place // 8) * 2 + lax.rem(place, 2)
+
+
+def gather_weights(rows):
+    peers = [[8 * x + 2 * low + core for x in range(4) for core in range(2)] for low in range(4)]
+    return lax.all_gather(rows, "tm", axis=0, axis_index_groups=peers)
 
 
 def neighbours(axes, first, last):
@@ -510,28 +511,25 @@
 ):
     groups = lax.axis_size("tm")
     frame_total = FR * groups * lax.axis_size("seq")
-    half = gather_half(proj_weight)
     gain = layer_gain.reshape(1, D)
     vectors = jnp.stack([batch_gamma, batch_beta, stale_mean, stale_variance])
-    core = lax.rem(lax.axis_index("tm"), 2).reshape(1)
+    in_hbm = pl.BlockSpec(memory_space=pltpu.HBM)
+    in_vmem = pl.BlockSpec(memory_space=pltpu.VMEM)
 
     edge_rows = EDGE + EDGE // 2
+    block = pltpu.VMEM((FR, D), bf16)
     packed, first, last = call(
         pack_kernel,
-        (shape((HEADS, 3 * HD, FR), bf16), shape((edge_rows, D), bf16), shape((edge_rows, D), bf16)),
-        query_in,
-        key_in,
-        value_in,
-        residual,
-        residual,
-        grad_conv,
-        grad_conv,
-        grid=(1,),
-        in_specs=[whole(FR, D)] * 3 + [rows_at(EDGE, 0), rows_at(EDGE, 3), rows_at(16, 0), rows_at(16, 7)],
-        out_specs=(whole(HEADS, 3 * HD, FR), whole(edge_rows, D), whole(edge_rows, D)),
+        (shape((HEADS, 3 * HD + 128, FR), bf16), shape((edge_rows, D), bf16), shape((edge_rows, D), bf16)),
+        weight_chunk().reshape(1),
+        *map(in_high_memory, (query_in, key_in, value_in, proj_weight, residual, grad_conv)),
+        in_specs=[pl.BlockSpec(memory_space=pltpu.SMEM)] + [in_hbm] * 6,
+        scratch=(block, block, block, pltpu.VMEM((128, 128), bf16), pltpu.SemaphoreType.DMA((8,))),
     )
     qkv = lax.all_to_all(packed, "seq", 0, 0, tiled=True)
     before, after = neighbours(("tm", "seq"), first, last)
+    qkv, before, after = lax.optimization_barrier((qkv, before, after))
+    weights = gather_weights(qkv[:, 3 * HD :])
     square = shape((STRETCH, 128), bf16)
     scores = [pltpu.VMEM((BLOCK, STRETCH), f32)] * 2
     keys, queries, values, edge_nat, edge_att, edge_log, first, last = call(
@@ -571,32 +569,23 @@
         edge_before,
         edge_after,
     )
-    half, _ = lax.optimization_barrier((half, att_payload))
-    swapped = swap_half(half)
     att_rows = lax.all_to_all(att_payload, "seq", 0, 0, tiled=True)
-    in_vmem = pl.BlockSpec(memory_space=pltpu.VMEM)
-    in_place = pl.BlockSpec(memory_space=pl.ANY)
     grad_stream, payload = call(
         middle_kernel,
         (shape((FR, D), bf16), shape((HEADS, PART_ROWS + HD, FR), bf16)),
-        core,
         att_rows,
         residual,
         before,
         after,
         gain,
-        half,
-        swapped,
+        in_high_memory(weights),
         conv_kernel,
         vectors,
         grad_conv,
         grad_stream_in,
-        in_specs=[pl.BlockSpec(memory_space=pltpu.SMEM)]
-        + [in_vmem] * 5
-        + [in_place] * 2
-        + [in_vmem] * 4,
+        in_specs=[in_vmem] * 5 + [in_hbm] + [in_vmem] * 4,
         scratch=(
-            pltpu.VMEM((32, HEADS, 32, 128), bf16),
+            pltpu.VMEM((8, HEADS, 128, 128), bf16),
             pltpu.VMEM((ROWS, D), f32),
             pltpu.VMEM((ROWS, D), bf16),
             pltpu.VMEM((8, FR, 128), f32),
@@ -606,7 +595,7 @@
             pltpu.VMEM((HEADS, PART_ROWS, 128), f32),
             pltpu.VMEM((FR, 2 * D), bf16),
             pltpu.VMEM((FR, D), f32),
-            pltpu.SemaphoreType.DMA((2 * HEADS,)),
+            pltpu.SemaphoreType.DMA((HEADS,)),
         ),
     )
     payload = lax.all_to_all(payload, "seq", 0, 0, tiled=True)
@@ -648,7 +637,7 @@
         totals,
         back,
         grid=(1,),
-        in_specs=[whole(groups, PART_ROWS, 128), in_place],
+        in_specs=[whole(groups, PART_ROWS, 128), pl.BlockSpec(memory_space=pl.ANY)],
         out_specs=pl.BlockSpec((HEADS, PART_ROWS, 128), lambda i: (0, 6, 0)),
         input_output_aliases={1: 0},
     )

time: 264 us -> 227 us (0.86)
  blocking collectives: 127 us -> 58.9 us
  starting transfers between devices: 38.6 us -> 60.5 us
  waiting for transfers between devices: 42 us -> 54.6 us
  local copies, waits for them, and re-layouts: 7.29 us -> 1.52 us
    all_to_all x2 -> x0, blocking collectives: 69.9 us -> none  [the longest x1 41.8 us: local(): qkv = lax.all_to_all(packed, 'seq', 0, 0, tiled=True)]
    all_gather x1, waiting for transfers between devices: 26 us -> 0.01 us  [gather_weights(): return lax.all_gather(rows, 'tm', axis=0, axis_index_groups=peers)]
    ppermute x4, waiting for transfers between devices: 13.2 us -> 36 us  [neighbours(): return (lax.ppermute(last, axes, up), lax.ppermute(first, axes, down))]
    all_to_all x1, waiting for transfers between devices: 0.01 us -> 15.7 us  [local(): att_rows = lax.all_to_all(att_payload, 'seq', 0, 0, tiled=True)]
    all_to_all x0 -> x1, starting transfers between devices: none -> 14.8 us  [local(): qkv = lax.all_to_all(packed, 'seq', 0, 0, tiled=True)]
    all_to_all x1, starting transfers between devices: 12.3 us -> 24.2 us  [local(): att_rows = lax.all_to_all(att_payload, 'seq', 0, 0, tiled=True)]
    unnamed x32 -> x22, local copies, waits for them, and re-layouts: 7.27 us -> 0.67 us
    all_to_all x1, blocking collectives: 21.1 us -> 25.2 us  [local(): payload = lax.all_to_all(payload, 'seq', 0, 0, tiled=True)]
  transfers between devices with their start and end apart: 8 -> 8, of which waited for: 3 -> 4; matrix products, arithmetic and copies ran while one was open for 0% -> 0% of each run, Pallas kernels for 8% -> 9%
where the time goes in v3:
time: 227 us; the launch traced here: 226 us
  starting transfers between devices  60.5 us (27%)
  blocking collectives  58.9 us (26%)
  waiting for transfers between devices  54.6 us (24%)
  Pallas kernels  36.2 us (16%)
  between operations  14.3 us (6%)
    pallas_call x9, Pallas kernels, call(): pl.pallas_call(kernel, out_shape=out_shape, scratch_shapes=list(scratch),...  36.2 us
    ppermute x4, waiting for transfers between devices, neighbours(): return (lax.ppermute(last, axes, up), lax.ppermute(first, axes, down))  36 us
    all_to_all x1, blocking collectives, local(): back = lax.all_to_all(back, 'seq', 0, 0, tiled=True)  33.7 us
    all_to_all x1, blocking collectives, local(): payload = lax.all_to_all(payload, 'seq', 0, 0, tiled=True)  25.2 us
    all_to_all x1, starting transfers between devices, local(): att_rows = lax.all_to_all(att_payload, 'seq', 0, 0, tiled=True)  24.2 us
    ppermute x4, starting transfers between devices, neighbours(): return (lax.ppermute(last, axes, up), lax.ppermute(first, axes, down))  17 us
    all_to_all x1, waiting for transfers between devices, local(): att_rows = lax.all_to_all(att_payload, 'seq', 0, 0, tiled=True)  15.7 us
    all_to_all x1, starting transfers between devices, local(): qkv = lax.all_to_all(packed, 'seq', 0, 0, tiled=True)  14.8 us
  transfers between devices with their start and end apart: 8, of which 4 were waited for; matrix products, arithmetic and copies ran while one was open for 0% of the time, Pallas kernels for 9%

profile of v3, /device:TPU:8, one launch (start us, length us, event | category | flops | bytes accessed | tf_op | source)
XLA Modules:
  0.0 226.1 jit_solution(12540507342966475207)
XLA Ops:
  7.2 2.6 %shard_map.180 = (bf16[16,320,128]{2,1,0:T(8,128)(2,1)}, bf16[48,1024]{1,0:T(8,128)(2,1)S(1)}, bf16[48,1024]{1,0:T(8,128)(2,1)S(1)}) custom-call(s32[1]{0:T(128)} %bitcast.chunk_ref, bf16[128,1024]{1,0:T(8,128)(2,1)} %query_hbm.1, bf16[128,1024]{1,0:T(8,128)(2,1)} %key_hbm.1, bf16[128,1024]{1,0:T(8,128)(2,1)} %value_hbm.1, bf16[1024,128]{1,0:T(8,128)(2,1)} %weight_hbm.1, ...), custom_call_target="tpu_custom_call" | custom-call | tf_op jit(solution)/shard_map/pallas_call | solution.py:463
  9.7 14.8 %all-to-all-start = ((bf16[16,320,128]{2,1,0:T(8,128)(2,1)}), bf16[16,320,128]{2,1,0:T(8,128)(2,1)S(1)}, u32[]{:S(2)}, u32[]{:S(2)}) async-start(bf16[16,320,128]{2,1,0:T(8,128)(2,1)} %get-tuple-element.32), calls=%async_computation | async-start | bytes 2621440 | tf_op jit(solution)/shard_map/all_to_all | solution.py:529
  24.6 7.7 %collective-permute-start = (bf16[48,1024]{1,0:T(8,128)(2,1)S(1)}, bf16[48,1024]{1,0:T(8,128)(2,1)S(1)}, u32[]{:S(2)}, u32[]{:S(2)}) collective-permute-start(bf16[48,1024]{1,0:T(8,128)(2,1)S(1)} %get-tuple-element.33), channel_id=1, source_target_pairs={{0,1},{1,2},{2,3},{3,4},{4,5},{5,6},{6,7},{7,8},{8,9},{9,10},{10,1... | collective-permute-start | bytes 294920 | tf_op jit(solution)/shard_map/ppermute | solution.py:494
  32.3 2.9 %collective-permute-start.1 = (bf16[48,1024]{1,0:T(8,128)(2,1)S(1)}, bf16[48,1024]{1,0:T(8,128)(2,1)S(1)}, u32[]{:S(2)}, u32[]{:S(2)}) collective-permute-start(bf16[48,1024]{1,0:T(8,128)(2,1)S(1)} %get-tuple-element.34), channel_id=1, source_target_pairs={{1,0},{2,1},{3,2},{4,3},{5,4},{6,5},{7,6},{8,7},{9,8},{10,9},{11,1... | collective-permute-start | bytes 294920 | tf_op jit(solution)/shard_map/ppermute | solution.py:494
  35.3 34.9 %collective-permute-done.before_ref = bf16[48,1024]{1,0:T(8,128)(2,1)S(1)} collective-permute-done((bf16[48,1024]{1,0:T(8,128)(2,1)S(1)}, bf16[48,1024]{1,0:T(8,128)(2,1)S(1)}, u32[]{:S(2)}, u32[]{:S(2)}) %collective-permute-start) | collective-permute-done | bytes 98336 | tf_op jit(solution)/shard_map/ppermute | solution.py:494
  70.1 1.2 collective-permute-done.1.after_ref
  71.4 0.8 slice.3
  72.2 1.9 shard_map.181
  74.2 4.4 %collective-permute-start.2 = (bf16[32,128]{1,0:T(8,128)(2,1)S(1)}, bf16[32,128]{1,0:T(8,128)(2,1)S(1)}, u32[]{:S(2)}, u32[]{:S(2)}) collective-permute-start(bf16[32,128]{1,0:T(8,128)(2,1)S(1)} %get-tuple-element.41), channel_id=1, source_target_pairs={{0,16},{16,32},{32,48},{48,64},{64,80},{80,96},{96,112},{112,128},... | collective-permute-start | bytes 24584 | tf_op jit(solution)/shard_map/ppermute | solution.py:494
  78.5 1.9 collective-permute-start.3
  80.5 6.2 %shard_map.182 = (bf16[1536,128]{1,0:T(8,128)(2,1)S(1)}, bf16[6,64,256]{2,1,0:T(8,128)(2,1)S(1)}, f32[6,8,256]{2,1,0:T(8,128)S(1)}) custom-call(bf16[128,2048]{1,0:T(8,128)(2,1)S(1)} %get-tuple-element.37.keys_ref, bf16[2048,128]{1,0:T(8,128)(2,1)S(1)} %get-tuple-element.38.query_ref, bf16[2048,128]{1,0:T(8,128)(2,1)S(1)} %get-tuple-element.39.value_ref), custom_call_target="tpu_custom_call" | custom-call | flops 6000000000 | bytes 4194304 | tf_op jit(solution)/shard_map/pallas_call | solution.py:463
  86.7 0.6 copy-done.5
  87.4 0.8 shard_map.183
  88.2 24.2 %all-to-all-start.1 = ((bf16[16,96,128]{2,1,0:T(8,128)(2,1)}), bf16[16,96,128]{2,1,0:T(8,128)(2,1)S(1)}, u32[]{:S(2)}, u32[]{:S(2)}) async-start(bf16[16,96,128]{2,1,0:T(8,128)(2,1)} %shard_map.183), calls=%async_computation.1 | async-start | bytes 786432 | tf_op jit(solution)/shard_map/all_to_all | solution.py:572
  112.5 15.7 %all-to-all-done.1.att_ref = bf16[16,96,128]{2,1,0:T(8,128)(2,1)S(1)} async-done(((bf16[16,96,128]{2,1,0:T(8,128)(2,1)}), bf16[16,96,128]{2,1,0:T(8,128)(2,1)S(1)}, u32[]{:S(2)}, u32[]{:S(2)}) %all-to-all-start.1) | async-done | bytes 393248 | tf_op jit(solution)/shard_map/all_to_all | solution.py:572
  128.2 10.5 %shard_map.184 = (bf16[128,1024]{1,0:T(8,128)(2,1)}, bf16[16,96,128]{2,1,0:T(8,128)(2,1)S(1)}) custom-call(bf16[16,96,128]{2,1,0:T(8,128)(2,1)S(1)} %all-to-all-done.1.att_ref, bf16[128,1024]{1,0:T(8,128)(2,1)S(1)} %copy-done, bf16[48,1024]{1,0:T(8,128)(2,1)S(1)} %collective-permute-done.before_ref, bf16[48,1024]{1,0:T(8,128)(2,1)S(1)} %collective-permute-done.1.after_ref, ...), custom_call_target="tpu_custom_call" | custom-call | tf_op jit(solution)/shard_map/pallas_call | solution.py:463
  138.8 25.2 %all_to_all.25.payload_ref = bf16[16,96,128]{2,1,0:T(8,128)(2,1)S(1)} all-to-all(bf16[16,96,128]{2,1,0:T(8,128)(2,1)S(1)} %get-tuple-element.45), channel_id=1, replica_groups=mesh['tm'=32,'seq'=16] {'seq'}, dimensions={0} | all-to-all | bytes 786432 | tf_op jit(solution)/shard_map/all_to_all | solution.py:601
  164.0 0.9 shard_map.185
  164.9 4.6 %all-to-all-start.3 = ((f32[32,32,128]{2,1,0:T(8,128)}), f32[32,32,128]{2,1,0:T(8,128)S(1)}, u32[]{:S(2)}, u32[]{:S(2)}) async-start(f32[32,32,128]{2,1,0:T(8,128)} %shard_map.185), calls=%async_computation.3 | async-start | bytes 1048576 | tf_op jit(solution)/shard_map/all_to_all | solution.py:610
  169.4 12.2 %shard_map.186.payload_ref = bf16[16,224,128]{2,1,0:T(8,128)(2,1)S(1)} custom-call(bf16[16,320,128]{2,1,0:T(8,128)(2,1)S(1)} %all-to-all-done.qkv_ref, bf16[2,64,256]{2,1,0:T(8,128)(2,1)S(1)} %get-tuple-element.46.edge_att_ref, bf16[6,64,256]{2,1,0:T(8,128)(2,1)S(1)} %get-tuple-element.47.mid_att_ref, f32[2,8,256]{2,1,0:T(8,128)S(1)} %get-tuple-element.48.edge_log_ref, ...), custom_call_target="tpu_custom_call" | custom-call | flops 12000000000 | bytes 4194304 | tf_op jit(solution)/shard_map/pallas_call | solution.py:463
  181.6 2.8 %all-to-all-done.3.parts_ref = f32[32,32,128]{2,1,0:T(8,128)S(1)} async-done(((f32[32,32,128]{2,1,0:T(8,128)}), f32[32,32,128]{2,1,0:T(8,128)S(1)}, u32[]{:S(2)}, u32[]{:S(2)}) %all-to-all-start.3) | async-done | bytes 524320 | tf_op jit(solution)/shard_map/all_to_all | solution.py:610
  184.5 0.1 shard_map.187
  184.5 33.7 %all_to_all.26.refs_0_ = bf16[16,224,128]{2,1,0:T(8,128)(2,1)S(1)} all-to-all(bf16[16,224,128]{2,1,0:T(8,128)(2,1)S(1)} %shard_map.187), channel_id=1, replica_groups=mesh['tm'=32,'seq'=16] {'seq'}, dimensions={0} | all-to-all | bytes 1835008 | tf_op jit(solution)/shard_map/all_to_all | solution.py:644
  218.2 1.1 shard_map.188
  (28 shorter events, 0.2 us)
Async XLA Ops:
  9.7 61.6 %all-to-all-start = ((bf16[16,320,128]{2,1,0:T(8,128)(2,1)}), bf16[16,320,128]{2,1,0:T(8,128)(2,1)S(1)}, u32[]{:S(2)}, u32[]{:S(2)}) async-start(bf16[16,320,128]{2,1,0:T(8,128)(2,1)} %get-tuple-element.32), calls=%async_computation | async-start | bytes 2621440 | tf_op jit(solution)/shard_map/all_to_all | solution.py:529
  24.5 103.6 %all-gather.3.cloned.1.call-start = ((), (), s32[]{:S(2)}) async-start(), calls=%async_computation.5 | async-start | bytes 4718592 | tf_op jit(solution)/shard_map/all_gather | solution.py:487
  24.6 45.5 %collective-permute-start = (bf16[48,1024]{1,0:T(8,128)(2,1)S(1)}, bf16[48,1024]{1,0:T(8,128)(2,1)S(1)}, u32[]{:S(2)}, u32[]{:S(2)}) collective-permute-start(bf16[48,1024]{1,0:T(8,128)(2,1)S(1)} %get-tuple-element.33), channel_id=1, source_target_pairs={{0,1},{1,2},{2,3},{3,4},{4,5},{5,6},{6,7},{7,8},{8,9},{9,10},{10,1... | collective-permute-start | bytes 294920 | tf_op jit(solution)/shard_map/ppermute | solution.py:494
  32.3 39.0 %collective-permute-start.1 = (bf16[48,1024]{1,0:T(8,128)(2,1)S(1)}, bf16[48,1024]{1,0:T(8,128)(2,1)S(1)}, u32[]{:S(2)}, u32[]{:S(2)}) collective-permute-start(bf16[48,1024]{1,0:T(8,128)(2,1)S(1)} %get-tuple-element.34), channel_id=1, source_target_pairs={{1,0},{2,1},{3,2},{4,3},{5,4},{6,5},{7,6},{8,7},{9,8},{10,9},{11,1... | collective-permute-start | bytes 294920 | tf_op jit(solution)/shard_map/ppermute | solution.py:494
  74.2 13.2 %collective-permute-start.2 = (bf16[32,128]{1,0:T(8,128)(2,1)S(1)}, bf16[32,128]{1,0:T(8,128)(2,1)S(1)}, u32[]{:S(2)}, u32[]{:S(2)}) collective-permute-start(bf16[32,128]{1,0:T(8,128)(2,1)S(1)} %get-tuple-element.41), channel_id=1, source_target_pairs={{0,16},{16,32},{32,48},{48,64},{64,80},{80,96},{96,112},{112,128},... | collective-permute-start | bytes 24584 | tf_op jit(solution)/shard_map/ppermute | solution.py:494
  78.5 8.9 %collective-permute-start.3 = (bf16[32,128]{1,0:T(8,128)(2,1)S(1)}, bf16[32,128]{1,0:T(8,128)(2,1)S(1)}, u32[]{:S(2)}, u32[]{:S(2)}) collective-permute-start(bf16[32,128]{1,0:T(8,128)(2,1)S(1)} %get-tuple-element.42), channel_id=1, source_target_pairs={{16,0},{32,16},{48,32},{64,48},{80,64},{96,80},{112,96},{128,112},... | collective-permute-start | bytes 24584 | tf_op jit(solution)/shard_map/ppermute | solution.py:494
  86.7 0.6 copy-start.5
  87.3 25.1 %copy-start.7 = (f32[1024]{0:T(1024)S(1)}, f32[1024]{0:T(1024)}, u32[]{:S(2)}) copy-start(f32[1024]{0:T(1024)} %param.23) | copy-start | bytes 12292
  87.3 25.1 %copy-start.8 = (f32[1024]{0:T(1024)S(1)}, f32[1024]{0:T(1024)}, u32[]{:S(2)}) copy-start(f32[1024]{0:T(1024)} %param.22) | copy-start | bytes 12292
  87.3 25.1 %copy-start.9 = (f32[1024]{0:T(1024)S(1)}, f32[1024]{0:T(1024)}, u32[]{:S(2)}) copy-start(f32[1024]{0:T(1024)} %param.21) | copy-start | bytes 12292
  87.3 25.1 %copy-start.10 = (f32[1024]{0:T(1024)S(1)}, f32[1024]{0:T(1024)}, u32[]{:S(2)}) copy-start(f32[1024]{0:T(1024)} %param.20) | copy-start | bytes 12292
  87.3 40.9 %copy-start = (bf16[128,1024]{1,0:T(8,128)(2,1)S(1)}, bf16[128,1024]{1,0:T(8,128)(2,1)}, u32[]{:S(2)}) copy-start(bf16[128,1024]{1,0:T(8,128)(2,1)} %residual_ref.1) | copy-start | bytes 786436
  87.3 40.9 %copy-start.1 = (bf16[128,1024]{1,0:T(8,128)(2,1)S(1)}, bf16[128,1024]{1,0:T(8,128)(2,1)}, u32[]{:S(2)}) copy-start(bf16[128,1024]{1,0:T(8,128)(2,1)} %grad_ref.1) | copy-start | bytes 786436
  87.3 40.9 %copy-start.2 = (bf16[128,1024]{1,0:T(8,128)(2,1)S(1)}, bf16[128,1024]{1,0:T(8,128)(2,1)}, u32[]{:S(2)}) copy-start(bf16[128,1024]{1,0:T(8,128)(2,1)} %skip_ref.1) | copy-start | bytes 786436
  87.4 40.8 %copy-start.3 = (f32[31,1024]{1,0:T(8,128)S(1)}, f32[31,1024]{1,0:T(8,128)}, u32[]{:S(2)}) copy-start(f32[31,1024]{1,0:T(8,128)} %taps_ref.1) | copy-start | bytes 380932
  87.4 40.8 %copy-start.4 = (f32[1024]{0:T(1024)S(1)}, f32[1024]{0:T(1024)}, u32[]{:S(2)}) copy-start(f32[1024]{0:T(1024)} %param.17) | copy-start | bytes 12292
  88.2 40.0 %all-to-all-start.1 = ((bf16[16,96,128]{2,1,0:T(8,128)(2,1)}), bf16[16,96,128]{2,1,0:T(8,128)(2,1)S(1)}, u32[]{:S(2)}, u32[]{:S(2)}) async-start(bf16[16,96,128]{2,1,0:T(8,128)(2,1)} %shard_map.183), calls=%async_computation.1 | async-start | bytes 786432 | tf_op jit(solution)/shard_map/all_to_all | solution.py:572
  138.8 30.7 %copy-start.6 = (f32[6,8,256]{2,1,0:T(8,128)S(1)}, f32[6,8,256]{2,1,0:T(8,128)}, u32[]{:S(2)}) copy-start(f32[6,8,256]{2,1,0:T(8,128)} %copy-done.5) | copy-start | bytes 147460
  164.9 19.6 %all-to-all-start.3 = ((f32[32,32,128]{2,1,0:T(8,128)}), f32[32,32,128]{2,1,0:T(8,128)S(1)}, u32[]{:S(2)}, u32[]{:S(2)}) async-start(f32[32,32,128]{2,1,0:T(8,128)} %shard_map.185), calls=%async_computation.3 | async-start | bytes 1048576 | tf_op jit(solution)/shard_map/all_to_all | solution.py:610
Sparse Core Ops, SparseCore 0:
  72.3 50.1 all-gather.2

commit v4 on v3

--- a/solution.py
+++ b/solution.py
@@ -54,12 +54,19 @@
     return high, mid, low
 
 
+def chunk_kernel(chunk_ref, weight_hbm, out_ref, weight_ref, copy_sem):
+    rows = pl.ds(pl.multiple_of(chunk_ref[0] * 128, 128), 128)
+    copy = pltpu.make_async_copy(weight_hbm.at[rows], weight_ref, copy_sem)
+    copy.start()
+    copy.wait()
+    for dest in range(HEADS):
+        out_ref[dest] = weight_ref[...]
+
+
 def pack_kernel(
-    chunk_ref,
     query_hbm,
     key_hbm,
     value_hbm,
-    weight_hbm,
     res_hbm,
     grad_hbm,
     out_ref,
@@ -68,15 +75,12 @@
     query_ref,
     key_ref,
     value_ref,
-    weight_ref,
     copy_sem,
 ):
-    weight_rows = weight_hbm.at[pl.ds(pl.multiple_of(chunk_ref[0] * 128, 128), 128)]
     pairs = (
         (query_hbm, query_ref),
         (key_hbm, key_ref),
         (value_hbm, value_ref),
-        (weight_rows, weight_ref),
         (res_hbm.at[0:EDGE], first_ref.at[0:EDGE]),
         (res_hbm.at[FR - EDGE : FR], last_ref.at[0:EDGE]),
         (grad_hbm.at[0:16], first_ref.at[EDGE : EDGE + 16]),
@@ -91,10 +95,7 @@
             turned = ref[:, 128 * pair : 128 * (pair + 1)].T
             out_ref[2 * pair, HD * item : HD * (item + 1), :] = turned[:HD]
             out_ref[2 * pair + 1, HD * item : HD * (item + 1), :] = turned[HD:]
-    copies[3].wait()
-    for dest in range(HEADS):
-        out_ref[dest, 3 * HD :, :] = weight_ref[...]
-    for copy in copies[4:]:
+    for copy in copies[3:]:
         copy.wait()
 
 
@@ -518,18 +519,26 @@
 
     edge_rows = EDGE + EDGE // 2
     block = pltpu.VMEM((FR, D), bf16)
+    chunks = call(
+        chunk_kernel,
+        shape((HEADS, 128, 128), bf16),
+        weight_chunk().reshape(1),
+        in_high_memory(proj_weight),
+        in_specs=[pl.BlockSpec(memory_space=pltpu.SMEM), in_hbm],
+        scratch=(pltpu.VMEM((128, 128), bf16), pltpu.SemaphoreType.DMA(())),
+    )
+    weight_rows = lax.all_to_all(chunks, "seq", 0, 0, tiled=True)
     packed, first, last = call(
         pack_kernel,
-        (shape((HEADS, 3 * HD + 128, FR), bf16), shape((edge_rows, D), bf16), shape((edge_rows, D), bf16)),
-        weight_chunk().reshape(1),
-        *map(in_high_memory, (query_in, key_in, value_in, proj_weight, residual, grad_conv)),
-        in_specs=[pl.BlockSpec(memory_space=pltpu.SMEM)] + [in_hbm] * 6,
-        scratch=(block, block, block, pltpu.VMEM((128, 128), bf16), pltpu.SemaphoreType.DMA((8,))),
-    )
+        (shape((HEADS, 3 * HD, FR), bf16), shape((edge_rows, D), bf16), shape((edge_rows, D), bf16)),
+        *map(in_high_memory, (query_in, key_in, value_in, residual, grad_conv)),
+        in_specs=[in_hbm] * 5,
+        scratch=(block, block, block, pltpu.SemaphoreType.DMA((7,))),
+    )
+    packed, weight_rows = lax.optimization_barrier((packed, weight_rows))
+    weights = gather_weights(weight_rows)
     qkv = lax.all_to_all(packed, "seq", 0, 0, tiled=True)
     before, after = neighbours(("tm", "seq"), first, last)
-    qkv, before, after = lax.optimization_barrier((qkv, before, after))
-    weights = gather_weights(qkv[:, 3 * HD :])
     square = shape((STRETCH, 128), bf16)
     scores = [pltpu.VMEM((BLOCK, STRETCH), f32)] * 2
     keys, queries, values, edge_nat, edge_att, edge_log, first, last = call(
@@ -569,6 +578,7 @@
         edge_before,
         edge_after,
     )
+    att_payload, before, after = lax.optimization_barrier((att_payload, before, after))
     att_rows = lax.all_to_all(att_payload, "seq", 0, 0, tiled=True)
     grad_stream, payload = call(
         middle_kernel,

time: 227 us -> 217 us (0.956)
  starting transfers between devices: 60.5 us -> 48.9 us
  waiting for transfers between devices: 54.6 us -> 57.4 us
    ppermute x4, waiting for transfers between devices: 36 us -> 0.01 us  [neighbours(): return (lax.ppermute(last, axes, up), lax.ppermute(first, axes, down))]
    all_to_all x1, waiting for transfers between devices: 0.04 us -> 20.7 us  [local(): qkv = lax.all_to_all(packed, 'seq', 0, 0, tiled=True)]
    all_to_all x0 -> x1, waiting for transfers between devices: none -> 19.7 us  [local(): weight_rows = lax.all_to_all(chunks, 'seq', 0, 0, tiled=True)]
    all_to_all x1, starting transfers between devices: 24.2 us -> 7.07 us  [local(): att_rows = lax.all_to_all(att_payload, 'seq', 0, 0, tiled=True)]
    all_to_all x0 -> x1, starting transfers between devices: none -> 14.8 us  [local(): weight_rows = lax.all_to_all(chunks, 'seq', 0, 0, tiled=True)]
    all_to_all x1, starting transfers between devices: 14.8 us -> 4.74 us  [local(): qkv = lax.all_to_all(packed, 'seq', 0, 0, tiled=True)]
    all_to_all x1, blocking collectives: 25.2 us -> 20.9 us  [local(): payload = lax.all_to_all(payload, 'seq', 0, 0, tiled=True)]
    pallas_call x9 -> x10, Pallas kernels: 36.2 us -> 37.6 us  [call(): pl.pallas_call(kernel, out_shape=out_shape, scratch_shapes=list(scratch),...]
  transfers between devices with their start and end apart: 8 -> 9, of which waited for: 4 -> 4; matrix products, arithmetic and copies ran while one was open for 0% -> 0% of each run, Pallas kernels for 9% -> 11%
where the time goes in v4:
time: 217 us; the launch traced here: 216 us
  waiting for transfers between devices  57.4 us (26%)
  blocking collectives  56.7 us (26%)
  starting transfers between devices  48.9 us (23%)
  Pallas kernels  37.6 us (17%)
  between operations  14.3 us (7%)
    pallas_call x10, Pallas kernels, call(): pl.pallas_call(kernel, out_shape=out_shape, scratch_shapes=list(scratch),...  37.6 us
    all_to_all x1, blocking collectives, local(): back = lax.all_to_all(back, 'seq', 0, 0, tiled=True)  35.8 us
    all_to_all x1, blocking collectives, local(): payload = lax.all_to_all(payload, 'seq', 0, 0, tiled=True)  20.9 us
    all_to_all x1, waiting for transfers between devices, local(): qkv = lax.all_to_all(packed, 'seq', 0, 0, tiled=True)  20.7 us
    all_to_all x1, waiting for transfers between devices, local(): weight_rows = lax.all_to_all(chunks, 'seq', 0, 0, tiled=True)  19.7 us
    ppermute x4, starting transfers between devices, neighbours(): return (lax.ppermute(last, axes, up), lax.ppermute(first, axes, down))  16.2 us
    all_to_all x1, starting transfers between devices, local(): weight_rows = lax.all_to_all(chunks, 'seq', 0, 0, tiled=True)  14.8 us
    all_to_all x1, waiting for transfers between devices, local(): att_rows = lax.all_to_all(att_payload, 'seq', 0, 0, tiled=True)  14.1 us
  transfers between devices with their start and end apart: 9, of which 4 were waited for; matrix products, arithmetic and copies ran while one was open for 0% of the time, Pallas kernels for 11%

profile of v4, /device:TPU:8, one launch (start us, length us, event | category | flops | bytes accessed | tf_op | source)
XLA Modules:
  0.0 215.8 jit_solution(1729617342180286482)
XLA Ops:
  7.2 1.6 shard_map.181
  8.8 14.8 %all-to-all-start = ((bf16[16,128,128]{2,1,0:T(8,128)(2,1)}), bf16[16,128,128]{2,1,0:T(8,128)(2,1)S(1)}, u32[]{:S(2)}, u32[]{:S(2)}) async-start(bf16[16,128,128]{2,1,0:T(8,128)(2,1)} %shard_map.181), calls=%async_computation | async-start | bytes 1048576 | tf_op jit(solution)/shard_map/all_to_all | solution.py:530
  23.7 2.3 %shard_map.180 = (bf16[16,192,128]{2,1,0:T(8,128)(2,1)}, bf16[48,1024]{1,0:T(8,128)(2,1)S(1)}, bf16[48,1024]{1,0:T(8,128)(2,1)S(1)}) custom-call(bf16[128,1024]{1,0:T(8,128)(2,1)} %query_hbm.1, bf16[128,1024]{1,0:T(8,128)(2,1)} %key_hbm.1, bf16[128,1024]{1,0:T(8,128)(2,1)} %value_hbm.1, bf16[128,1024]{1,0:T(8,128)(2,1)} %residual_ref.1, ...), custom_call_target="tpu_custom_call" | custom-call | tf_op jit(solution)/shard_map/pallas_call | solution.py:464
  26.0 19.7 %all-to-all-done = bf16[16,128,128]{2,1,0:T(8,128)(2,1)S(1)} async-done(((bf16[16,128,128]{2,1,0:T(8,128)(2,1)}), bf16[16,128,128]{2,1,0:T(8,128)(2,1)S(1)}, u32[]{:S(2)}, u32[]{:S(2)}) %all-to-all-start) | async-done | bytes 524320 | tf_op jit(solution)/shard_map/all_to_all | solution.py:530
  45.7 0.8 copy-done.5
  46.6 4.7 %all-to-all-start.1 = ((bf16[16,192,128]{2,1,0:T(8,128)(2,1)}), bf16[16,192,128]{2,1,0:T(8,128)(2,1)S(1)}, u32[]{:S(2)}, u32[]{:S(2)}) async-start(bf16[16,192,128]{2,1,0:T(8,128)(2,1)} %get-tuple-element.35), calls=%async_computation.1 | async-start | bytes 1572864 | tf_op jit(solution)/shard_map/all_to_all | solution.py:540
  51.3 7.7 %collective-permute-start.2 = (bf16[48,1024]{1,0:T(8,128)(2,1)S(1)}, bf16[48,1024]{1,0:T(8,128)(2,1)S(1)}, u32[]{:S(2)}, u32[]{:S(2)}) collective-permute-start(bf16[48,1024]{1,0:T(8,128)(2,1)S(1)} %get-tuple-element.43), channel_id=1, source_target_pairs={{0,1},{1,2},{2,3},{3,4},{4,5},{5,6},{6,7},{7,8},{8,9},{9,10},{10,1... | collective-permute-start | bytes 294920 | tf_op jit(solution)/shard_map/ppermute | solution.py:495
  59.1 3.0 %collective-permute-start.3 = (bf16[48,1024]{1,0:T(8,128)(2,1)S(1)}, bf16[48,1024]{1,0:T(8,128)(2,1)S(1)}, u32[]{:S(2)}, u32[]{:S(2)}) collective-permute-start(bf16[48,1024]{1,0:T(8,128)(2,1)S(1)} %get-tuple-element.44), channel_id=1, source_target_pairs={{1,0},{2,1},{3,2},{4,3},{5,4},{6,5},{7,6},{8,7},{9,8},{10,9},{11,1... | collective-permute-start | bytes 294920 | tf_op jit(solution)/shard_map/ppermute | solution.py:495
  62.0 20.7 %all-to-all-done.1.qkv_ref = bf16[16,192,128]{2,1,0:T(8,128)(2,1)S(1)} async-done(((bf16[16,192,128]{2,1,0:T(8,128)(2,1)}), bf16[16,192,128]{2,1,0:T(8,128)(2,1)S(1)}, u32[]{:S(2)}, u32[]{:S(2)}) %all-to-all-start.1) | async-done | bytes 786464 | tf_op jit(solution)/shard_map/all_to_all | solution.py:540
  82.7 1.9 shard_map.182
  84.6 1.9 collective-permute-start
  86.5 3.6 %collective-permute-start.1 = (bf16[32,128]{1,0:T(8,128)(2,1)S(1)}, bf16[32,128]{1,0:T(8,128)(2,1)S(1)}, u32[]{:S(2)}, u32[]{:S(2)}) collective-permute-start(bf16[32,128]{1,0:T(8,128)(2,1)S(1)} %get-tuple-element.42), channel_id=1, source_target_pairs={{16,0},{32,16},{48,32},{64,48},{80,64},{96,80},{112,96},{128,112},... | collective-permute-start | bytes 24584 | tf_op jit(solution)/shard_map/ppermute | solution.py:495
  90.3 6.2 %shard_map.183 = (bf16[1536,128]{1,0:T(8,128)(2,1)S(1)}, bf16[6,64,256]{2,1,0:T(8,128)(2,1)S(1)}, f32[6,8,256]{2,1,0:T(8,128)S(1)}) custom-call(bf16[128,2048]{1,0:T(8,128)(2,1)S(1)} %get-tuple-element.37.keys_ref, bf16[2048,128]{1,0:T(8,128)(2,1)S(1)} %get-tuple-element.38.query_ref, bf16[2048,128]{1,0:T(8,128)(2,1)S(1)} %get-tuple-element.39.value_ref), custom_call_target="tpu_custom_call" | custom-call | flops 6000000000 | bytes 4194304 | tf_op jit(solution)/shard_map/pallas_call | solution.py:464
  96.6 0.8 shard_map.184
  97.4 7.1 %all-to-all-start.2 = ((bf16[16,96,128]{2,1,0:T(8,128)(2,1)}), bf16[16,96,128]{2,1,0:T(8,128)(2,1)S(1)}, u32[]{:S(2)}, u32[]{:S(2)}) async-start(bf16[16,96,128]{2,1,0:T(8,128)(2,1)} %shard_map.184), calls=%async_computation.2 | async-start | bytes 786432 | tf_op jit(solution)/shard_map/all_to_all | solution.py:582
  104.5 14.1 %all-to-all-done.2.att_ref = bf16[16,96,128]{2,1,0:T(8,128)(2,1)S(1)} async-done(((bf16[16,96,128]{2,1,0:T(8,128)(2,1)}), bf16[16,96,128]{2,1,0:T(8,128)(2,1)S(1)}, u32[]{:S(2)}, u32[]{:S(2)}) %all-to-all-start.2) | async-done | bytes 393248 | tf_op jit(solution)/shard_map/all_to_all | solution.py:582
  118.7 10.5 %shard_map.185 = (bf16[128,1024]{1,0:T(8,128)(2,1)}, bf16[16,96,128]{2,1,0:T(8,128)(2,1)S(1)}) custom-call(bf16[16,96,128]{2,1,0:T(8,128)(2,1)S(1)} %all-to-all-done.2.att_ref, bf16[128,1024]{1,0:T(8,128)(2,1)S(1)} %copy-done, bf16[48,1024]{1,0:T(8,128)(2,1)S(1)} %collective-permute-done.2.before_ref, bf16[48,1024]{1,0:T(8,128)(2,1)S(1)} %collective-permute-done.3.after_ref, ...), custom_call_target="tpu_custom_call" | custom-call | tf_op jit(solution)/shard_map/pallas_call | solution.py:464
  129.2 20.9 %all_to_all.30.payload_ref = bf16[16,96,128]{2,1,0:T(8,128)(2,1)S(1)} all-to-all(bf16[16,96,128]{2,1,0:T(8,128)(2,1)S(1)} %get-tuple-element.49), channel_id=1, replica_groups=mesh['tm'=32,'seq'=16] {'seq'}, dimensions={0} | all-to-all | bytes 786432 | tf_op jit(solution)/shard_map/all_to_all | solution.py:611
  150.2 0.9 shard_map.186
  151.0 6.0 %all-to-all-start.4 = ((f32[32,32,128]{2,1,0:T(8,128)}), f32[32,32,128]{2,1,0:T(8,128)S(1)}, u32[]{:S(2)}, u32[]{:S(2)}) async-start(f32[32,32,128]{2,1,0:T(8,128)} %shard_map.186), calls=%async_computation.4 | async-start | bytes 1048576 | tf_op jit(solution)/shard_map/all_to_all | solution.py:620
  157.1 12.2 %shard_map.187.payload_ref = bf16[16,224,128]{2,1,0:T(8,128)(2,1)S(1)} custom-call(bf16[16,192,128]{2,1,0:T(8,128)(2,1)S(1)} %all-to-all-done.1.qkv_ref, bf16[2,64,256]{2,1,0:T(8,128)(2,1)S(1)} %get-tuple-element.50.edge_att_ref, bf16[6,64,256]{2,1,0:T(8,128)(2,1)S(1)} %get-tuple-element.51.mid_att_ref, f32[2,8,256]{2,1,0:T(8,128)S(1)} %get-tuple-element.52.edge_log_ref, ...), custom_call_target="tpu_custom_call" | custom-call | flops 12000000000 | bytes 4194304 | tf_op jit(solution)/shard_map/pallas_call | solution.py:464
  169.3 2.8 %all-to-all-done.4.parts_ref = f32[32,32,128]{2,1,0:T(8,128)S(1)} async-done(((f32[32,32,128]{2,1,0:T(8,128)}), f32[32,32,128]{2,1,0:T(8,128)S(1)}, u32[]{:S(2)}, u32[]{:S(2)}) %all-to-all-start.4) | async-done | bytes 524320 | tf_op jit(solution)/shard_map/all_to_all | solution.py:620
  172.2 35.8 %all_to_all.31.refs_0_ = bf16[16,224,128]{2,1,0:T(8,128)(2,1)S(1)} all-to-all(bf16[16,224,128]{2,1,0:T(8,128)(2,1)S(1)} %shard_map.188), channel_id=1, replica_groups=mesh['tm'=32,'seq'=16] {'seq'}, dimensions={0} | all-to-all | bytes 1835008 | tf_op jit(solution)/shard_map/all_to_all | solution.py:654
  208.0 1.1 shard_map.189
  (28 shorter events, 0.2 us)
Async XLA Ops:
  8.8 36.9 %all-to-all-start = ((bf16[16,128,128]{2,1,0:T(8,128)(2,1)}), bf16[16,128,128]{2,1,0:T(8,128)(2,1)S(1)}, u32[]{:S(2)}, u32[]{:S(2)}) async-start(bf16[16,128,128]{2,1,0:T(8,128)(2,1)} %shard_map.181), calls=%async_computation | async-start | bytes 1048576 | tf_op jit(solution)/shard_map/all_to_all | solution.py:530
  23.6 95.0 %all-gather.3.cloned.1.call-start = ((), (), s32[]{:S(2)}) async-start(), calls=%async_computation.6 | async-start | bytes 4718592 | tf_op jit(solution)/shard_map/all_gather | solution.py:488
  45.7 0.8 copy-start.5
  46.6 36.1 %all-to-all-start.1 = ((bf16[16,192,128]{2,1,0:T(8,128)(2,1)}), bf16[16,192,128]{2,1,0:T(8,128)(2,1)S(1)}, u32[]{:S(2)}, u32[]{:S(2)}) async-start(bf16[16,192,128]{2,1,0:T(8,128)(2,1)} %get-tuple-element.35), calls=%async_computation.1 | async-start | bytes 1572864 | tf_op jit(solution)/shard_map/all_to_all | solution.py:540
  51.3 46.1 %collective-permute-start.2 = (bf16[48,1024]{1,0:T(8,128)(2,1)S(1)}, bf16[48,1024]{1,0:T(8,128)(2,1)S(1)}, u32[]{:S(2)}, u32[]{:S(2)}) collective-permute-start(bf16[48,1024]{1,0:T(8,128)(2,1)S(1)} %get-tuple-element.43), channel_id=1, source_target_pairs={{0,1},{1,2},{2,3},{3,4},{4,5},{5,6},{6,7},{7,8},{8,9},{9,10},{10,1... | collective-permute-start | bytes 294920 | tf_op jit(solution)/shard_map/ppermute | solution.py:495
  59.1 38.3 %collective-permute-start.3 = (bf16[48,1024]{1,0:T(8,128)(2,1)S(1)}, bf16[48,1024]{1,0:T(8,128)(2,1)S(1)}, u32[]{:S(2)}, u32[]{:S(2)}) collective-permute-start(bf16[48,1024]{1,0:T(8,128)(2,1)S(1)} %get-tuple-element.44), channel_id=1, source_target_pairs={{1,0},{2,1},{3,2},{4,3},{5,4},{6,5},{7,6},{8,7},{9,8},{10,9},{11,1... | collective-permute-start | bytes 294920 | tf_op jit(solution)/shard_map/ppermute | solution.py:495
  84.6 11.9 %collective-permute-start = (bf16[32,128]{1,0:T(8,128)(2,1)S(1)}, bf16[32,128]{1,0:T(8,128)(2,1)S(1)}, u32[]{:S(2)}, u32[]{:S(2)}) collective-permute-start(bf16[32,128]{1,0:T(8,128)(2,1)S(1)} %get-tuple-element.41), channel_id=1, source_target_pairs={{0,16},{16,32},{32,48},{48,64},{64,80},{80,96},{96,112},{112,128},... | collective-permute-start | bytes 24584 | tf_op jit(solution)/shard_map/ppermute | solution.py:495
  86.5 10.0 %collective-permute-start.1 = (bf16[32,128]{1,0:T(8,128)(2,1)S(1)}, bf16[32,128]{1,0:T(8,128)(2,1)S(1)}, u32[]{:S(2)}, u32[]{:S(2)}) collective-permute-start(bf16[32,128]{1,0:T(8,128)(2,1)S(1)} %get-tuple-element.42), channel_id=1, source_target_pairs={{16,0},{32,16},{48,32},{64,48},{80,64},{96,80},{112,96},{128,112},... | collective-permute-start | bytes 24584 | tf_op jit(solution)/shard_map/ppermute | solution.py:495
  90.2 14.3 %copy-start.6 = (f32[1024]{0:T(1024)S(1)}, f32[1024]{0:T(1024)}, u32[]{:S(2)}) copy-start(f32[1024]{0:T(1024)} %param.23) | copy-start | bytes 12292
  90.2 14.3 %copy-start.7 = (f32[1024]{0:T(1024)S(1)}, f32[1024]{0:T(1024)}, u32[]{:S(2)}) copy-start(f32[1024]{0:T(1024)} %param.22) | copy-start | bytes 12292
  90.2 14.3 %copy-start.8 = (f32[1024]{0:T(1024)S(1)}, f32[1024]{0:T(1024)}, u32[]{:S(2)}) copy-start(f32[1024]{0:T(1024)} %param.21) | copy-start | bytes 12292
  90.2 14.3 %copy-start.9 = (f32[1024]{0:T(1024)S(1)}, f32[1024]{0:T(1024)}, u32[]{:S(2)}) copy-start(f32[1024]{0:T(1024)} %param.20) | copy-start | bytes 12292
  90.2 28.4 %copy-start = (bf16[128,1024]{1,0:T(8,128)(2,1)S(1)}, bf16[128,1024]{1,0:T(8,128)(2,1)}, u32[]{:S(2)}) copy-start(bf16[128,1024]{1,0:T(8,128)(2,1)} %residual_ref.1) | copy-start | bytes 786436
  90.2 28.4 %copy-start.1 = (bf16[128,1024]{1,0:T(8,128)(2,1)S(1)}, bf16[128,1024]{1,0:T(8,128)(2,1)}, u32[]{:S(2)}) copy-start(bf16[128,1024]{1,0:T(8,128)(2,1)} %grad_ref.1) | copy-start | bytes 786436
  90.3 28.4 %copy-start.2 = (bf16[128,1024]{1,0:T(8,128)(2,1)S(1)}, bf16[128,1024]{1,0:T(8,128)(2,1)}, u32[]{:S(2)}) copy-start(bf16[128,1024]{1,0:T(8,128)(2,1)} %skip_ref.1) | copy-start | bytes 786436
  90.3 28.4 %copy-start.3 = (f32[31,1024]{1,0:T(8,128)S(1)}, f32[31,1024]{1,0:T(8,128)}, u32[]{:S(2)}) copy-start(f32[31,1024]{1,0:T(8,128)} %taps_ref.1) | copy-start | bytes 380932
  90.3 28.4 %copy-start.4 = (f32[1024]{0:T(1024)S(1)}, f32[1024]{0:T(1024)}, u32[]{:S(2)}) copy-start(f32[1024]{0:T(1024)} %param.17) | copy-start | bytes 12292
  97.4 21.3 %all-to-all-start.2 = ((bf16[16,96,128]{2,1,0:T(8,128)(2,1)}), bf16[16,96,128]{2,1,0:T(8,128)(2,1)S(1)}, u32[]{:S(2)}, u32[]{:S(2)}) async-start(bf16[16,96,128]{2,1,0:T(8,128)(2,1)} %shard_map.184), calls=%async_computation.2 | async-start | bytes 786432 | tf_op jit(solution)/shard_map/all_to_all | solution.py:582
  151.0 21.1 %all-to-all-start.4 = ((f32[32,32,128]{2,1,0:T(8,128)}), f32[32,32,128]{2,1,0:T(8,128)S(1)}, u32[]{:S(2)}, u32[]{:S(2)}) async-start(f32[32,32,128]{2,1,0:T(8,128)} %shard_map.186), calls=%async_computation.4 | async-start | bytes 1048576 | tf_op jit(solution)/shard_map/all_to_all | solution.py:620
Sparse Core Ops, SparseCore 0:
  46.7 31.2 all-gather.2

commit v5 on v3

--- a/solution.py
+++ b/solution.py
@@ -54,17 +54,27 @@
     return high, mid, low
 
 
+def rows_kernel(res_hbm, grad_hbm, first_ref, last_ref, copy_sem):
+    pairs = (
+        (res_hbm.at[0:EDGE], first_ref.at[0:EDGE]),
+        (res_hbm.at[FR - EDGE : FR], last_ref.at[0:EDGE]),
+        (grad_hbm.at[0:16], first_ref.at[EDGE : EDGE + 16]),
+        (grad_hbm.at[FR - 16 : FR], last_ref.at[EDGE : EDGE + 16]),
+    )
+    copies = [pltpu.make_async_copy(src, dst, copy_sem.at[i]) for i, (src, dst) in enumerate(pairs)]
+    for copy in copies:
+        copy.start()
+    for copy in copies:
+        copy.wait()
+
+
 def pack_kernel(
     chunk_ref,
     query_hbm,
     key_hbm,
     value_hbm,
     weight_hbm,
-    res_hbm,
-    grad_hbm,
     out_ref,
-    first_ref,
-    last_ref,
     query_ref,
     key_ref,
     value_ref,
@@ -72,16 +82,7 @@
     copy_sem,
 ):
     weight_rows = weight_hbm.at[pl.ds(pl.multiple_of(chunk_ref[0] * 128, 128), 128)]
-    pairs = (
-        (query_hbm, query_ref),
-        (key_hbm, key_ref),
-        (value_hbm, value_ref),
-        (weight_rows, weight_ref),
-        (res_hbm.at[0:EDGE], first_ref.at[0:EDGE]),
-        (res_hbm.at[FR - EDGE : FR], last_ref.at[0:EDGE]),
-        (grad_hbm.at[0:16], first_ref.at[EDGE : EDGE + 16]),
-        (grad_hbm.at[FR - 16 : FR], last_ref.at[EDGE : EDGE + 16]),
-    )
+    pairs = ((query_hbm, query_ref), (key_hbm, key_ref), (value_hbm, value_ref), (weight_rows, weight_ref))
     copies = [pltpu.make_async_copy(src, dst, copy_sem.at[i]) for i, (src, dst) in enumerate(pairs)]
     for copy in copies:
         copy.start()
@@ -94,8 +95,6 @@
     copies[3].wait()
     for dest in range(HEADS):
         out_ref[dest, 3 * HD :, :] = weight_ref[...]
-    for copy in copies[4:]:
-        copy.wait()
 
 
 CHUNKS = STRETCH // BLOCK
@@ -345,7 +344,7 @@
 
 
 def spread_kernel(payload_ref, out_ref):
-    total = jnp.sum(payload_ref[...].astype(f32), axis=0)
+    total = jnp.sum(payload_ref[...].astype(f32), axis=0).astype(bf16)
     out_ref[...] = jnp.broadcast_to(total[None], out_ref.shape)
 
 
@@ -430,7 +429,7 @@
 
 
 def finish_kernel(parts_ref, payload_ref, out_ref):
-    total = jnp.sum(parts_ref[...], axis=0).astype(bf16)
+    total = jnp.sum(parts_ref[...].astype(f32), axis=0).astype(bf16)
     out_ref[...] = jnp.broadcast_to(total[None], out_ref.shape)
 
 
@@ -518,17 +517,25 @@
 
     edge_rows = EDGE + EDGE // 2
     block = pltpu.VMEM((FR, D), bf16)
-    packed, first, last = call(
+    first, last = call(
+        rows_kernel,
+        (shape((edge_rows, D), bf16), shape((edge_rows, D), bf16)),
+        in_high_memory(residual),
+        in_high_memory(grad_conv),
+        in_specs=[in_hbm] * 2,
+        scratch=(pltpu.SemaphoreType.DMA((4,)),),
+    )
+    before, after = neighbours(("tm", "seq"), first, last)
+    packed = call(
         pack_kernel,
-        (shape((HEADS, 3 * HD + 128, FR), bf16), shape((edge_rows, D), bf16), shape((edge_rows, D), bf16)),
+        shape((HEADS, 3 * HD + 128, FR), bf16),
         weight_chunk().reshape(1),
-        *map(in_high_memory, (query_in, key_in, value_in, proj_weight, residual, grad_conv)),
-        in_specs=[pl.BlockSpec(memory_space=pltpu.SMEM)] + [in_hbm] * 6,
-        scratch=(block, block, block, pltpu.VMEM((128, 128), bf16), pltpu.SemaphoreType.DMA((8,))),
-    )
+        *map(in_high_memory, (query_in, key_in, value_in, proj_weight)),
+        in_specs=[pl.BlockSpec(memory_space=pltpu.SMEM)] + [in_hbm] * 4,
+        scratch=(block, block, block, pltpu.VMEM((128, 128), bf16), pltpu.SemaphoreType.DMA((4,))),
+    )
+    packed, before, after = lax.optimization_barrier((packed, before, after))
     qkv = lax.all_to_all(packed, "seq", 0, 0, tiled=True)
-    before, after = neighbours(("tm", "seq"), first, last)
-    qkv, before, after = lax.optimization_barrier((qkv, before, after))
     weights = gather_weights(qkv[:, 3 * HD :])
     square = shape((STRETCH, 128), bf16)
     scores = [pltpu.VMEM((BLOCK, STRETCH), f32)] * 2
@@ -601,7 +608,7 @@
     payload = lax.all_to_all(payload, "seq", 0, 0, tiled=True)
     spread = call(
         spread_kernel,
-        shape((groups, PART_ROWS, 128), f32),
+        shape((groups, PART_ROWS, 128), bf16),
         payload,
         grid=(1,),
         in_specs=[whole(HEADS, PART_ROWS, 128)],

time: 227 us -> 214 us (0.943)
  the two profiles are of different devices: /device:TPU:8 before, /device:TPU:18 now
where the time goes in v5:
time: 214 us; the launch traced here: 213 us
  blocking collectives  109 us (51%)
  Pallas kernels  35.9 us (17%)
  starting transfers between devices  32.4 us (15%)
  waiting for transfers between devices  20.5 us (10%)
  between operations  14.3 us (7%)
    all_to_all x1, blocking collectives, local(): qkv = lax.all_to_all(packed, 'seq', 0, 0, tiled=True)  49.4 us
    all_to_all x1, blocking collectives, local(): back = lax.all_to_all(back, 'seq', 0, 0, tiled=True)  36.8 us
    pallas_call x10, Pallas kernels, call(): pl.pallas_call(kernel, out_shape=out_shape, scratch_shapes=list(scratch),...  35.9 us
    all_to_all x1, blocking collectives, local(): payload = lax.all_to_all(payload, 'seq', 0, 0, tiled=True)  23.2 us
    ppermute x4, starting transfers between devices, neighbours(): return (lax.ppermute(last, axes, up), lax.ppermute(first, axes, down))  21.2 us
    all_to_all x1, waiting for transfers between devices, local(): att_rows = lax.all_to_all(att_payload, 'seq', 0, 0, tiled=True)  16.7 us
    all_to_all x1, starting transfers between devices, local(): totals = lax.all_to_all(spread, 'tm', 0, 0, tiled=True)  7.39 us
  transfers between devices with their start and end apart: 7, of which 3 were waited for; matrix products, arithmetic and copies ran while one was open for 0% of the time, Pallas kernels for 11%

profile of v5, /device:TPU:18, one launch (start us, length us, event | category | flops | bytes accessed | tf_op | source)
XLA Modules:
  0.0 213.4 jit_solution(13972144336814447445)
XLA Ops:
  7.2 0.0 all-gather.3.cloned.1.call-start
  7.2 0.9 shard_map.181
  8.1 5.9 %collective-permute-start = (bf16[48,1024]{1,0:T(8,128)(2,1)S(1)}, bf16[48,1024]{1,0:T(8,128)(2,1)S(1)}, u32[]{:S(2)}, u32[]{:S(2)}) collective-permute-start(bf16[48,1024]{1,0:T(8,128)(2,1)S(1)} %get-tuple-element.31), channel_id=1, source_target_pairs={{0,1},{1,2},{2,3},{3,4},{4,5},{5,6},{6,7},{7,8},{8,9},{9,10},{10,1... | collective-permute-start | bytes 294920 | tf_op jit(solution)/shard_map/ppermute | solution.py:493
  14.1 9.7 %collective-permute-start.1 = (bf16[48,1024]{1,0:T(8,128)(2,1)S(1)}, bf16[48,1024]{1,0:T(8,128)(2,1)S(1)}, u32[]{:S(2)}, u32[]{:S(2)}) collective-permute-start(bf16[48,1024]{1,0:T(8,128)(2,1)S(1)} %get-tuple-element.32), channel_id=1, source_target_pairs={{1,0},{2,1},{3,2},{4,3},{5,4},{6,5},{7,6},{8,7},{9,8},{10,9},{11,1... | collective-permute-start | bytes 294920 | tf_op jit(solution)/shard_map/ppermute | solution.py:493
  23.8 1.4 shard_map.180
  25.3 2.0 collective-permute-done.before_ref
  27.3 1.7 collective-permute-done.1.after_ref
  29.0 49.4 %all_to_all.25.qkv_ref = bf16[16,320,128]{2,1,0:T(8,128)(2,1)S(1)} all-to-all(bf16[16,320,128]{2,1,0:T(8,128)(2,1)S(1)} %shard_map.180), channel_id=1, replica_groups=mesh['tm'=32,'seq'=16] {'seq'}, dimensions={0} | all-to-all | bytes 2621440 | tf_op jit(solution)/shard_map/all_to_all | solution.py:538
  78.4 0.8 slice.4
  79.3 1.9 shard_map.182
  81.2 1.9 collective-permute-start.2
  83.1 3.6 %collective-permute-start.3 = (bf16[32,128]{1,0:T(8,128)(2,1)S(1)}, bf16[32,128]{1,0:T(8,128)(2,1)S(1)}, u32[]{:S(2)}, u32[]{:S(2)}) collective-permute-start(bf16[32,128]{1,0:T(8,128)(2,1)S(1)} %get-tuple-element.40), channel_id=1, source_target_pairs={{16,0},{32,16},{48,32},{64,48},{80,64},{96,80},{112,96},{128,112},... | collective-permute-start | bytes 24584 | tf_op jit(solution)/shard_map/ppermute | solution.py:493
  86.8 6.2 %shard_map.183 = (bf16[1536,128]{1,0:T(8,128)(2,1)S(1)}, bf16[6,64,256]{2,1,0:T(8,128)(2,1)S(1)}, f32[6,8,256]{2,1,0:T(8,128)S(1)}) custom-call(bf16[128,2048]{1,0:T(8,128)(2,1)S(1)} %get-tuple-element.35.keys_ref, bf16[2048,128]{1,0:T(8,128)(2,1)S(1)} %get-tuple-element.36.query_ref, bf16[2048,128]{1,0:T(8,128)(2,1)S(1)} %get-tuple-element.37.value_ref), custom_call_target="tpu_custom_call" | custom-call | flops 6000000000 | bytes 4194304 | tf_op jit(solution)/shard_map/pallas_call | solution.py:462
  93.2 0.8 shard_map.184
  94.0 3.7 %all-to-all-start.1 = ((bf16[16,96,128]{2,1,0:T(8,128)(2,1)}), bf16[16,96,128]{2,1,0:T(8,128)(2,1)S(1)}, u32[]{:S(2)}, u32[]{:S(2)}) async-start(bf16[16,96,128]{2,1,0:T(8,128)(2,1)} %shard_map.184), calls=%async_computation.1 | async-start | bytes 786432 | tf_op jit(solution)/shard_map/all_to_all | solution.py:579
  97.8 16.7 %all-to-all-done.1.att_ref = bf16[16,96,128]{2,1,0:T(8,128)(2,1)S(1)} async-done(((bf16[16,96,128]{2,1,0:T(8,128)(2,1)}), bf16[16,96,128]{2,1,0:T(8,128)(2,1)S(1)}, u32[]{:S(2)}, u32[]{:S(2)}) %all-to-all-start.1) | async-done | bytes 393248 | tf_op jit(solution)/shard_map/all_to_all | solution.py:579
  114.6 10.5 %shard_map.185 = (bf16[128,1024]{1,0:T(8,128)(2,1)}, bf16[16,96,128]{2,1,0:T(8,128)(2,1)S(1)}) custom-call(bf16[16,96,128]{2,1,0:T(8,128)(2,1)S(1)} %all-to-all-done.1.att_ref, bf16[128,1024]{1,0:T(8,128)(2,1)S(1)} %copy-done, bf16[48,1024]{1,0:T(8,128)(2,1)S(1)} %collective-permute-done.before_ref, bf16[48,1024]{1,0:T(8,128)(2,1)S(1)} %collective-permute-done.1.after_ref, ...), custom_call_target="tpu_custom_call" | custom-call | tf_op jit(solution)/shard_map/pallas_call | solution.py:462
  125.1 23.2 %all_to_all.26.payload_ref = bf16[16,96,128]{2,1,0:T(8,128)(2,1)S(1)} all-to-all(bf16[16,96,128]{2,1,0:T(8,128)(2,1)S(1)} %get-tuple-element.43), channel_id=1, replica_groups=mesh['tm'=32,'seq'=16] {'seq'}, dimensions={0} | all-to-all | bytes 786432 | tf_op jit(solution)/shard_map/all_to_all | solution.py:608
  148.3 0.7 shard_map.186
  149.1 7.4 %all-to-all-start.3 = ((bf16[32,32,128]{2,1,0:T(8,128)(2,1)}), bf16[32,32,128]{2,1,0:T(8,128)(2,1)S(1)}, u32[]{:S(2)}, u32[]{:S(2)}) async-start(bf16[32,32,128]{2,1,0:T(8,128)(2,1)} %shard_map.186), calls=%async_computation.3 | async-start | bytes 524288 | tf_op jit(solution)/shard_map/all_to_all | solution.py:617
  156.5 12.2 %shard_map.187.payload_ref = bf16[16,224,128]{2,1,0:T(8,128)(2,1)S(1)} custom-call(bf16[16,320,128]{2,1,0:T(8,128)(2,1)S(1)} %all_to_all.25.qkv_ref, bf16[2,64,256]{2,1,0:T(8,128)(2,1)S(1)} %get-tuple-element.44.edge_att_ref, bf16[6,64,256]{2,1,0:T(8,128)(2,1)S(1)} %get-tuple-element.45.mid_att_ref, f32[2,8,256]{2,1,0:T(8,128)S(1)} %get-tuple-element.46.edge_log_ref, ...), custom_call_target="tpu_custom_call" | custom-call | flops 12000000000 | bytes 4194304 | tf_op jit(solution)/shard_map/pallas_call | solution.py:462
  168.7 0.1 shard_map.188
  168.7 36.8 %all_to_all.27.refs_0_ = bf16[16,224,128]{2,1,0:T(8,128)(2,1)S(1)} all-to-all(bf16[16,224,128]{2,1,0:T(8,128)(2,1)S(1)} %shard_map.188), channel_id=1, replica_groups=mesh['tm'=32,'seq'=16] {'seq'}, dimensions={0} | all-to-all | bytes 1835008 | tf_op jit(solution)/shard_map/all_to_all | solution.py:651
  205.5 1.1 shard_map.189
  (24 shorter events, 0.1 us)
Async XLA Ops:
  7.2 107.4 %all-gather.3.cloned.1.call-start = ((), (), s32[]{:S(2)}) async-start(), calls=%async_computation.5 | async-start | bytes 4718592 | tf_op jit(solution)/shard_map/all_gather | solution.py:486
  8.1 19.2 %collective-permute-start = (bf16[48,1024]{1,0:T(8,128)(2,1)S(1)}, bf16[48,1024]{1,0:T(8,128)(2,1)S(1)}, u32[]{:S(2)}, u32[]{:S(2)}) collective-permute-start(bf16[48,1024]{1,0:T(8,128)(2,1)S(1)} %get-tuple-element.31), channel_id=1, source_target_pairs={{0,1},{1,2},{2,3},{3,4},{4,5},{5,6},{6,7},{7,8},{8,9},{9,10},{10,1... | collective-permute-start | bytes 294920 | tf_op jit(solution)/shard_map/ppermute | solution.py:493
  14.1 14.9 %collective-permute-start.1 = (bf16[48,1024]{1,0:T(8,128)(2,1)S(1)}, bf16[48,1024]{1,0:T(8,128)(2,1)S(1)}, u32[]{:S(2)}, u32[]{:S(2)}) collective-permute-start(bf16[48,1024]{1,0:T(8,128)(2,1)S(1)} %get-tuple-element.32), channel_id=1, source_target_pairs={{1,0},{2,1},{3,2},{4,3},{5,4},{6,5},{7,6},{8,7},{9,8},{10,9},{11,1... | collective-permute-start | bytes 294920 | tf_op jit(solution)/shard_map/ppermute | solution.py:493
  81.2 11.9 %collective-permute-start.2 = (bf16[32,128]{1,0:T(8,128)(2,1)S(1)}, bf16[32,128]{1,0:T(8,128)(2,1)S(1)}, u32[]{:S(2)}, u32[]{:S(2)}) collective-permute-start(bf16[32,128]{1,0:T(8,128)(2,1)S(1)} %get-tuple-element.39), channel_id=1, source_target_pairs={{0,16},{16,32},{32,48},{48,64},{64,80},{80,96},{96,112},{112,128},... | collective-permute-start | bytes 24584 | tf_op jit(solution)/shard_map/ppermute | solution.py:493
  83.1 10.0 %collective-permute-start.3 = (bf16[32,128]{1,0:T(8,128)(2,1)S(1)}, bf16[32,128]{1,0:T(8,128)(2,1)S(1)}, u32[]{:S(2)}, u32[]{:S(2)}) collective-permute-start(bf16[32,128]{1,0:T(8,128)(2,1)S(1)} %get-tuple-element.40), channel_id=1, source_target_pairs={{16,0},{32,16},{48,32},{64,48},{80,64},{96,80},{112,96},{128,112},... | collective-permute-start | bytes 24584 | tf_op jit(solution)/shard_map/ppermute | solution.py:493
  93.0 4.7 %copy-start.5 = (f32[1024]{0:T(1024)S(1)}, f32[1024]{0:T(1024)}, u32[]{:S(2)}) copy-start(f32[1024]{0:T(1024)} %param.23) | copy-start | bytes 12292
  93.0 4.7 %copy-start.6 = (f32[1024]{0:T(1024)S(1)}, f32[1024]{0:T(1024)}, u32[]{:S(2)}) copy-start(f32[1024]{0:T(1024)} %param.22) | copy-start | bytes 12292
  93.1 4.7 %copy-start.7 = (f32[1024]{0:T(1024)S(1)}, f32[1024]{0:T(1024)}, u32[]{:S(2)}) copy-start(f32[1024]{0:T(1024)} %param.21) | copy-start | bytes 12292
  93.1 4.7 %copy-start.8 = (f32[1024]{0:T(1024)S(1)}, f32[1024]{0:T(1024)}, u32[]{:S(2)}) copy-start(f32[1024]{0:T(1024)} %param.20) | copy-start | bytes 12292
  93.1 21.5 %copy-start = (bf16[128,1024]{1,0:T(8,128)(2,1)S(1)}, bf16[128,1024]{1,0:T(8,128)(2,1)}, u32[]{:S(2)}) copy-start(bf16[128,1024]{1,0:T(8,128)(2,1)} %residual_ref.1) | copy-start | bytes 786436
  93.1 21.5 %copy-start.1 = (bf16[128,1024]{1,0:T(8,128)(2,1)S(1)}, bf16[128,1024]{1,0:T(8,128)(2,1)}, u32[]{:S(2)}) copy-start(bf16[128,1024]{1,0:T(8,128)(2,1)} %grad_ref.1) | copy-start | bytes 786436
  93.1 21.4 %copy-start.2 = (bf16[128,1024]{1,0:T(8,128)(2,1)S(1)}, bf16[128,1024]{1,0:T(8,128)(2,1)}, u32[]{:S(2)}) copy-start(bf16[128,1024]{1,0:T(8,128)(2,1)} %skip_ref.1) | copy-start | bytes 786436
  93.1 21.4 %copy-start.3 = (f32[31,1024]{1,0:T(8,128)S(1)}, f32[31,1024]{1,0:T(8,128)}, u32[]{:S(2)}) copy-start(f32[31,1024]{1,0:T(8,128)} %taps_ref.1) | copy-start | bytes 380932
  93.1 21.4 %copy-start.4 = (f32[1024]{0:T(1024)S(1)}, f32[1024]{0:T(1024)}, u32[]{:S(2)}) copy-start(f32[1024]{0:T(1024)} %param.17) | copy-start | bytes 12292
  94.0 20.5 %all-to-all-start.1 = ((bf16[16,96,128]{2,1,0:T(8,128)(2,1)}), bf16[16,96,128]{2,1,0:T(8,128)(2,1)S(1)}, u32[]{:S(2)}, u32[]{:S(2)}) async-start(bf16[16,96,128]{2,1,0:T(8,128)(2,1)} %shard_map.184), calls=%async_computation.1 | async-start | bytes 786432 | tf_op jit(solution)/shard_map/all_to_all | solution.py:579
  149.1 19.6 %all-to-all-start.3 = ((bf16[32,32,128]{2,1,0:T(8,128)(2,1)}), bf16[32,32,128]{2,1,0:T(8,128)(2,1)S(1)}, u32[]{:S(2)}, u32[]{:S(2)}) async-start(bf16[32,32,128]{2,1,0:T(8,128)(2,1)} %shard_map.186), calls=%async_computation.3 | async-start | bytes 524288 | tf_op jit(solution)/shard_map/all_to_all | solution.py:617
Sparse Core Ops, SparseCore 0:
  79.4 29.7 all-gather.2

commit v6 on v5

--- a/solution.py
+++ b/solution.py
@@ -18,6 +18,7 @@
 LOG2E = math.log2(math.e)
 SCALE = HD ** (-0.5)
 BLOCK = 256
+TALL = 512
 PART_ROWS = 32
 EDGE = 32
 ROWS = FR + 2 * EDGE
@@ -54,18 +55,14 @@
     return high, mid, low
 
 
-def rows_kernel(res_hbm, grad_hbm, first_ref, last_ref, copy_sem):
+def row_copies(res_hbm, grad_hbm, first_ref, last_ref, copy_sem):
     pairs = (
         (res_hbm.at[0:EDGE], first_ref.at[0:EDGE]),
         (res_hbm.at[FR - EDGE : FR], last_ref.at[0:EDGE]),
         (grad_hbm.at[0:16], first_ref.at[EDGE : EDGE + 16]),
         (grad_hbm.at[FR - 16 : FR], last_ref.at[EDGE : EDGE + 16]),
     )
-    copies = [pltpu.make_async_copy(src, dst, copy_sem.at[i]) for i, (src, dst) in enumerate(pairs)]
-    for copy in copies:
-        copy.start()
-    for copy in copies:
-        copy.wait()
+    return [pltpu.make_async_copy(src, dst, copy_sem.at[i]) for i, (src, dst) in enumerate(pairs)]
 
 
 def pack_kernel(
@@ -100,10 +97,14 @@
 CHUNKS = STRETCH // BLOCK
 
 
-def block_rows(block):
+TALLS = STRETCH // TALL
+PER_TALL = TALL // FR
+
+
+def block_rows(block, size=BLOCK):
     if isinstance(block, int):
-        return slice(block * BLOCK, (block + 1) * BLOCK)
-    return pl.ds(pl.multiple_of(block * BLOCK, BLOCK), BLOCK)
+        return slice(block * size, (block + 1) * size)
+    return pl.ds(pl.multiple_of(block * size, size), size)
 
 
 def low_lanes(rows):
@@ -114,7 +115,7 @@
     queries = peak = total = None
     if following is not None:
         block, next_ref = following
-        queries = query_ref[block_rows(block), :]
+        queries = query_ref[block_rows(block, TALL), :]
     for chunk in range(CHUNKS):
         rows = slice(BLOCK * chunk, BLOCK * (chunk + 1))
         if following is not None:
@@ -128,14 +129,14 @@
             part = dot(weights, value_ref[rows, :])
             total = part if total is None else total + part
     if peak is not None:
-        peak = jnp.broadcast_to(jnp.max(peak, axis=1, keepdims=True), (BLOCK, 128))
+        peak = jnp.broadcast_to(jnp.max(peak, axis=1, keepdims=True), (TALL, 128))
     return peak, total
 
 
 def store_attended(total, peak, nat_ref, rows, turned_ref, log_ref, place):
-    norm = jnp.broadcast_to(total[:, HD : HD + 1], (BLOCK, 128))
+    norm = jnp.broadcast_to(total[:, HD : HD + 1], (TALL, 128))
     attended = (total / norm).astype(bf16).astype(f32)
-    low = low_lanes(BLOCK)
+    low = low_lanes(TALL)
     nat_ref[rows, :] = jnp.where(low, attended, pltpu.roll(attended, HD, 1)).astype(bf16)
     turned = jnp.where(low, attended, peak + jnp.log2(norm)).T
     turned_ref[place] = turned[:HD].astype(bf16)
@@ -144,6 +145,8 @@
 
 def edge_forward_kernel(
     qkv_ref,
+    res_hbm,
+    grad_hbm,
     keys_ref,
     query_ref,
     value_ref,
@@ -152,9 +155,15 @@
     log_ref,
     first_ref,
     last_ref,
+    row_first_ref,
+    row_last_ref,
     score_ref,
     other_ref,
+    copy_sem,
 ):
+    copies = row_copies(res_hbm, grad_hbm, row_first_ref, row_last_ref, copy_sem)
+    for copy in copies:
+        copy.start()
     pad_rows = lax.broadcasted_iota(jnp.int32, (HD, FR), 0)
     ones = jnp.where(pad_rows == 0, 1.0, 0.0).astype(bf16)
     for source in range(HEADS):
@@ -167,12 +176,14 @@
         value_ref[span, :] = jnp.concatenate([qkv_ref[source, 2 * HD : 3 * HD, :], ones], axis=0).T
     stage = lambda *pair: soft_stage(keys_ref, query_ref, value_ref, *pair)
     top, _ = stage((0, score_ref), None)
-    final_top, total = stage((CHUNKS - 1, other_ref), (score_ref, top))
-    store_attended(total, top, nat_ref, slice(0, BLOCK), turned_ref, log_ref, 0)
+    final_top, total = stage((TALLS - 1, other_ref), (score_ref, top))
+    store_attended(total, top, nat_ref, slice(0, TALL), turned_ref, log_ref, 0)
     _, total = stage(None, (other_ref, final_top))
-    store_attended(total, final_top, nat_ref, slice(BLOCK, 2 * BLOCK), turned_ref, log_ref, 1)
+    store_attended(total, final_top, nat_ref, slice(TALL, 2 * TALL), turned_ref, log_ref, 1)
     first_ref[...] = nat_ref[0:EDGE, :]
-    last_ref[...] = nat_ref[2 * BLOCK - EDGE : 2 * BLOCK, :]
+    last_ref[...] = nat_ref[2 * TALL - EDGE : 2 * TALL, :]
+    for copy in copies:
+        copy.wait()
 
 
 def middle_forward_kernel(
@@ -180,23 +191,11 @@
 ):
     stage = lambda *pair: soft_stage(keys_ref, query_ref, value_ref, *pair)
 
-    def store(total, top, place):
-        store_attended(total, top, nat_ref, block_rows(place), turned_ref, log_ref, place)
-
-    def two(index, top):
-        place = 2 * index
-        next_top, total = stage((place + 2, other_ref), (score_ref, top))
-        store(total, top, place)
-        last_top, total = stage((place + 3, score_ref), (other_ref, next_top))
-        store(total, next_top, place + 1)
-        return last_top
-
     top, _ = stage((1, score_ref), None)
-    top = lax.fori_loop(0, 2, two, top)
-    next_top, total = stage((6, other_ref), (score_ref, top))
-    store(total, top, 4)
+    next_top, total = stage((2, other_ref), (score_ref, top))
+    store_attended(total, top, nat_ref, slice(0, TALL), turned_ref, log_ref, 0)
     _, total = stage(None, (other_ref, next_top))
-    store(total, next_top, 5)
+    store_attended(total, next_top, nat_ref, slice(TALL, 2 * TALL), turned_ref, log_ref, 1)
 
 
 def assemble_kernel(edge_ref, middle_ref, before_ref, after_ref, out_ref):
@@ -205,11 +204,11 @@
             return before_ref[...]
         if begin >= STRETCH:
             return after_ref[...]
-        if begin < BLOCK:
+        if begin < TALL:
             return edge_ref[begin : begin + count, :]
-        if begin < STRETCH - BLOCK:
-            return middle_ref[begin - BLOCK : begin - BLOCK + count, :]
-        begin -= STRETCH - 2 * BLOCK
+        if begin < STRETCH - TALL:
+            return middle_ref[begin - TALL : begin - TALL + count, :]
+        begin -= STRETCH - 2 * TALL
         return edge_ref[begin : begin + count, :]
 
     for dest in range(HEADS):
@@ -374,8 +373,8 @@
         keys_ref[span, :] = jnp.concatenate([key_block, ones], axis=0).T
         values_ref[span, :] = jnp.concatenate([qkv_ref[source, 2 * HD : 3 * HD, :], ones], axis=0).T
         grads = payload_ref[source, PART_ROWS:, :]
-        block, side = divmod(source, 2)
-        if 0 < block < CHUNKS - 1:
+        block, side = divmod(source, PER_TALL)
+        if 0 < block < TALLS - 1:
             att, log, block = mid_att_ref, mid_log_ref, block - 1
         else:
             att, log, block = edge_att_ref, edge_log_ref, min(block, 1)
@@ -396,15 +395,15 @@
     total_ref[...] = jnp.zeros_like(total_ref)
 
     def step(block, carry):
-        rows = block_rows(block)
+        rows = block_rows(block, TALL)
         keys, values, turned = keys_ref[rows, :], values_ref[rows, :], turned_ref[:, rows]
 
         def products(chunk):
             cols = block_rows(chunk)
             return dot(keys, query_ref[:, cols]), dot(values, grad_ref[:, cols])
 
-        key_total = jnp.zeros((BLOCK, 128), f32)
-        value_total = jnp.zeros((BLOCK, 128), f32)
+        key_total = jnp.zeros((TALL, 128), f32)
+        value_total = jnp.zeros((TALL, 128), f32)
         ready = products(0)
         for chunk in range(CHUNKS):
             cols = block_rows(chunk)
@@ -418,11 +417,13 @@
             total_ref[:, cols] += dot(turned, grad_scores)
         for place, total in ((1, key_total * SCALE), (2, value_total)):
             turned_total = total.T[:HD].astype(bf16)
-            out_ref[2 * block, HD * place : HD * (place + 1), :] = turned_total[:, :FR]
-            out_ref[2 * block + 1, HD * place : HD * (place + 1), :] = turned_total[:, FR:]
+            for side in range(PER_TALL):
+                out_ref[PER_TALL * block + side, HD * place : HD * (place + 1), :] = turned_total[
+                    :, FR * side : FR * (side + 1)
+                ]
         return carry
 
-    lax.fori_loop(0, CHUNKS, step, 0)
+    lax.fori_loop(0, TALLS, step, 0)
     for source in range(HEADS):
         span = slice(FR * source, FR * (source + 1))
         out_ref[source, 0:HD, :] = (total_ref[:, span] * SCALE).astype(bf16)
@@ -517,15 +518,6 @@
 
     edge_rows = EDGE + EDGE // 2
     block = pltpu.VMEM((FR, D), bf16)
-    first, last = call(
-        rows_kernel,
-        (shape((edge_rows, D), bf16), shape((edge_rows, D), bf16)),
-        in_high_memory(residual),
-        in_high_memory(grad_conv),
-        in_specs=[in_hbm] * 2,
-        scratch=(pltpu.SemaphoreType.DMA((4,)),),
-    )
-    before, after = neighbours(("tm", "seq"), first, last)
     packed = call(
         pack_kernel,
         shape((HEADS, 3 * HD + 128, FR), bf16),
@@ -534,33 +526,38 @@
         in_specs=[pl.BlockSpec(memory_space=pltpu.SMEM)] + [in_hbm] * 4,
         scratch=(block, block, block, pltpu.VMEM((128, 128), bf16), pltpu.SemaphoreType.DMA((4,))),
     )
-    packed, before, after = lax.optimization_barrier((packed, before, after))
     qkv = lax.all_to_all(packed, "seq", 0, 0, tiled=True)
     weights = gather_weights(qkv[:, 3 * HD :])
     square = shape((STRETCH, 128), bf16)
-    scores = [pltpu.VMEM((BLOCK, STRETCH), f32)] * 2
-    keys, queries, values, edge_nat, edge_att, edge_log, first, last = call(
+    scores = [pltpu.VMEM((TALL, STRETCH), f32)] * 2
+    keys, queries, values, edge_nat, edge_att, edge_log, first, last, row_first, row_last = call(
         edge_forward_kernel,
         (
             shape((128, STRETCH), bf16),
             square,
             square,
-            shape((2 * BLOCK, 128), bf16),
-            shape((2, HD, BLOCK), bf16),
-            shape((2, 8, BLOCK), f32),
+            shape((2 * TALL, 128), bf16),
+            shape((2, HD, TALL), bf16),
+            shape((2, 8, TALL), f32),
             shape((EDGE, 128), bf16),
             shape((EDGE, 128), bf16),
+            shape((edge_rows, D), bf16),
+            shape((edge_rows, D), bf16),
         ),
         qkv,
-        scratch=scores,
+        in_high_memory(residual),
+        in_high_memory(grad_conv),
+        in_specs=[in_vmem, in_hbm, in_hbm],
+        scratch=(*scores, pltpu.SemaphoreType.DMA((4,))),
     )
     edge_before, edge_after = neighbours("tm", first, last)
+    before, after = neighbours(("tm", "seq"), row_first, row_last)
     mid_nat, mid_att, mid_log = call(
         middle_forward_kernel,
         (
-            shape((STRETCH - 2 * BLOCK, 128), bf16),
-            shape((CHUNKS - 2, HD, BLOCK), bf16),
-            shape((CHUNKS - 2, 8, BLOCK), f32),
+            shape((STRETCH - 2 * TALL, 128), bf16),
+            shape((TALLS - 2, HD, TALL), bf16),
+            shape((TALLS - 2, 8, TALL), f32),
         ),
         keys,
         queries,
@@ -576,6 +573,7 @@
         edge_before,
         edge_after,
     )
+    att_payload, before, after = lax.optimization_barrier((att_payload, before, after))
     att_rows = lax.all_to_all(att_payload, "seq", 0, 0, tiled=True)
     grad_stream, payload = call(
         middle_kernel,

time: 214 us -> 210 us (0.981)
  Pallas kernels: 35.9 us -> 32.9 us
  waiting for transfers between devices: 20.5 us -> 17.7 us
    all_to_all x1, starting transfers between devices: 3.73 us -> 9.94 us  [local(): att_rows = lax.all_to_all(att_payload, 'seq', 0, 0, tiled=True)]
    ppermute x4, starting transfers between devices: 21.2 us -> 16.7 us  [neighbours(): return (lax.ppermute(last, axes, up), lax.ppermute(first, axes, down))]
    ppermute x4, waiting for transfers between devices: 3.76 us -> 0.01 us  [neighbours(): return (lax.ppermute(last, axes, up), lax.ppermute(first, axes, down))]
    all_to_all x1, blocking collectives: 49.4 us -> 52.6 us  [local(): qkv = lax.all_to_all(packed, 'seq', 0, 0, tiled=True)]
    pallas_call x10 -> x9, Pallas kernels: 35.9 us -> 32.9 us  [call(): pl.pallas_call(kernel, out_shape=out_shape, scratch_shapes=list(scratch),...]
  transfers between devices with their start and end apart: 7 -> 7, of which waited for: 3 -> 1; matrix products, arithmetic and copies ran while one was open for 0% -> 0% of each run, Pallas kernels for 11% -> 9%
where the time goes in v6:
time: 210 us
  blocking collectives  111 us (53%)
  starting transfers between devices  33.5 us (16%)
  Pallas kernels  32.9 us (16%)
  waiting for transfers between devices  17.7 us (8%)
  between operations  14.3 us (7%)
    all_to_all x1, blocking collectives, local(): qkv = lax.all_to_all(packed, 'seq', 0, 0, tiled=True)  52.6 us
    all_to_all x1, blocking collectives, local(): back = lax.all_to_all(back, 'seq', 0, 0, tiled=True)  35.8 us
    pallas_call x9, Pallas kernels, call(): pl.pallas_call(kernel, out_shape=out_shape, scratch_shapes=list(scratch),...  32.9 us
    all_to_all x1, blocking collectives, local(): payload = lax.all_to_all(payload, 'seq', 0, 0, tiled=True)  22.1 us
    all_to_all x1, waiting for transfers between devices, local(): att_rows = lax.all_to_all(att_payload, 'seq', 0, 0, tiled=True)  17.7 us
    ppermute x4, starting transfers between devices, neighbours(): return (lax.ppermute(last, axes, up), lax.ppermute(first, axes, down))  16.7 us
    all_to_all x1, starting transfers between devices, local(): att_rows = lax.all_to_all(att_payload, 'seq', 0, 0, tiled=True)  9.94 us
    all_to_all x1, starting transfers between devices, local(): totals = lax.all_to_all(spread, 'tm', 0, 0, tiled=True)  6.79 us
  transfers between devices with their start and end apart: 7, of which 1 were waited for; matrix products, arithmetic and copies ran while one was open for 0% of the time, Pallas kernels for 9%

profile of v6, /device:TPU:18, one launch (start us, length us, event | category | flops | bytes accessed | tf_op | source)
XLA Modules:
  0.0 209.9 jit_solution(5520448402711757871)
XLA Ops:
  7.2 0.0 all-gather.3.cloned.1.call-start
  7.2 1.4 shard_map.180
  8.7 52.6 %all_to_all.25.qkv_ref = bf16[16,320,128]{2,1,0:T(8,128)(2,1)S(1)} all-to-all(bf16[16,320,128]{2,1,0:T(8,128)(2,1)S(1)} %shard_map.180), channel_id=1, replica_groups=mesh['tm'=32,'seq'=16] {'seq'}, dimensions={0} | all-to-all | bytes 2621440 | tf_op jit(solution)/shard_map/all_to_all | solution.py:529
  61.3 0.8 slice.4
  62.1 0.0 all-gather.3.cloned.1.call-update
  62.2 4.0 %shard_map.181 = (bf16[128,2048]{1,0:T(8,128)(2,1)S(1)}, bf16[2048,128]{1,0:T(8,128)(2,1)S(1)}, bf16[2048,128]{1,0:T(8,128)(2,1)S(1)}, bf16[1024,128]{1,0:T(8,12...) custom-call(bf16[16,320,128]{2,1,0:T(8,128)(2,1)S(1)} %all_to_all.25, ...), custom_call_target="tpu_custom_call" | custom-call | tf_op jit(solution)/shard_map/pallas_call | solution.py:463
  66.1 1.9 collective-permute-start
  68.1 4.1 %collective-permute-start.1 = (bf16[32,128]{1,0:T(8,128)(2,1)S(1)}, bf16[32,128]{1,0:T(8,128)(2,1)S(1)}, u32[]{:S(2)}, u32[]{:S(2)}) collective-permute-start(bf16[32,128]{1,0:T(8,128)(2,1)S(1)} %get-tuple-element.37), channel_id=1, source_target_pairs={{16,0},{32,16},{48,32},{64,48},{80,64},{96,80},{112,96},{128,112},... | collective-permute-start | bytes 24584 | tf_op jit(solution)/shard_map/ppermute | solution.py:494
  72.2 3.1 %collective-permute-start.2 = (bf16[48,1024]{1,0:T(8,128)(2,1)S(1)}, bf16[48,1024]{1,0:T(8,128)(2,1)S(1)}, u32[]{:S(2)}, u32[]{:S(2)}) collective-permute-start(bf16[48,1024]{1,0:T(8,128)(2,1)S(1)} %get-tuple-element.38), channel_id=1, source_target_pairs={{0,1},{1,2},{2,3},{3,4},{4,5},{5,6},{6,7},{7,8},{8,9},{9,10},{10,1... | collective-permute-start | bytes 294920 | tf_op jit(solution)/shard_map/ppermute | solution.py:494
  75.3 7.6 %collective-permute-start.3 = (bf16[48,1024]{1,0:T(8,128)(2,1)S(1)}, bf16[48,1024]{1,0:T(8,128)(2,1)S(1)}, u32[]{:S(2)}, u32[]{:S(2)}) collective-permute-start(bf16[48,1024]{1,0:T(8,128)(2,1)S(1)} %get-tuple-element.39), channel_id=1, source_target_pairs={{1,0},{2,1},{3,2},{4,3},{5,4},{6,5},{7,6},{8,7},{9,8},{10,9},{11,1... | collective-permute-start | bytes 294920 | tf_op jit(solution)/shard_map/ppermute | solution.py:494
  82.9 2.9 %shard_map.182 = (bf16[1024,128]{1,0:T(8,128)(2,1)S(1)}, bf16[2,64,512]{2,1,0:T(8,128)(2,1)S(1)}, f32[2,8,512]{2,1,0:T(8,128)S(1)}) custom-call(bf16[128,2048]{1,0:T(8,128)(2,1)S(1)} %get-tuple-element.32.keys_ref, bf16[2048,128]{1,0:T(8,128)(2,1)S(1)} %get-tuple-element.33.query_ref, bf16[2048,128]{1,0:T(8,128)(2,1)S(1)} %get-tuple-element.34.value_ref), custom_call_target="tpu_custom_call" | custom-call | flops 6000000000 | bytes 4194304 | tf_op jit(solution)/shard_map/pallas_call | solution.py:463
  85.8 0.0 copy-start.5
  85.8 0.0 copy-start.8
  85.9 0.8 shard_map.183
  86.7 9.9 %all-to-all-start.1 = ((bf16[16,96,128]{2,1,0:T(8,128)(2,1)}), bf16[16,96,128]{2,1,0:T(8,128)(2,1)S(1)}, u32[]{:S(2)}, u32[]{:S(2)}) async-start(bf16[16,96,128]{2,1,0:T(8,128)(2,1)} %shard_map.183), calls=%async_computation.1 | async-start | bytes 786432 | tf_op jit(solution)/shard_map/all_to_all | solution.py:577
  96.8 17.7 %all-to-all-done.1.att_ref = bf16[16,96,128]{2,1,0:T(8,128)(2,1)S(1)} async-done(((bf16[16,96,128]{2,1,0:T(8,128)(2,1)}), bf16[16,96,128]{2,1,0:T(8,128)(2,1)S(1)}, u32[]{:S(2)}, u32[]{:S(2)}) %all-to-all-start.1) | async-done | bytes 393248 | tf_op jit(solution)/shard_map/all_to_all | solution.py:577
  114.5 10.5 %shard_map.184 = (bf16[128,1024]{1,0:T(8,128)(2,1)}, bf16[16,96,128]{2,1,0:T(8,128)(2,1)S(1)}) custom-call(bf16[16,96,128]{2,1,0:T(8,128)(2,1)S(1)} %all-to-all-done.1.att_ref, bf16[128,1024]{1,0:T(8,128)(2,1)S(1)} %copy-done, bf16[48,1024]{1,0:T(8,128)(2,1)S(1)} %collective-permute-done.2.before_ref, bf16[48,1024]{1,0:T(8,128)(2,1)S(1)} %collective-permute-done.3.after_ref, ...), custom_call_target="tpu_custom_call" | custom-call | tf_op jit(solution)/shard_map/pallas_call | solution.py:463
  125.0 22.1 %all_to_all.26.payload_ref = bf16[16,96,128]{2,1,0:T(8,128)(2,1)S(1)} all-to-all(bf16[16,96,128]{2,1,0:T(8,128)(2,1)S(1)} %get-tuple-element.43), channel_id=1, replica_groups=mesh['tm'=32,'seq'=16] {'seq'}, dimensions={0} | all-to-all | bytes 786432 | tf_op jit(solution)/shard_map/all_to_all | solution.py:606
  147.1 0.7 shard_map.185
  147.8 6.8 %all-to-all-start.3 = ((bf16[32,32,128]{2,1,0:T(8,128)(2,1)}), bf16[32,32,128]{2,1,0:T(8,128)(2,1)S(1)}, u32[]{:S(2)}, u32[]{:S(2)}) async-start(bf16[32,32,128]{2,1,0:T(8,128)(2,1)} %shard_map.185), calls=%async_computation.3 | async-start | bytes 524288 | tf_op jit(solution)/shard_map/all_to_all | solution.py:615
  154.6 11.4 %shard_map.186.payload_ref = bf16[16,224,128]{2,1,0:T(8,128)(2,1)S(1)} custom-call(bf16[16,320,128]{2,1,0:T(8,128)(2,1)S(1)} %all_to_all.25.qkv_ref, bf16[2,64,512]{2,1,0:T(8,128)(2,1)S(1)} %get-tuple-element.44.edge_att_ref, bf16[2,64,512]{2,1,0:T(8,128)(2,1)S(1)} %get-tuple-element.45.mid_att_ref, f32[2,8,512]{2,1,0:T(8,128)S(1)} %get-tuple-element.46.edge_log_ref, ...), custom_call_target="tpu_custom_call" | custom-call | flops 12000000000 | bytes 4194304 | tf_op jit(solution)/shard_map/pallas_call | solution.py:463
  166.1 0.1 shard_map.187
  166.1 35.8 %all_to_all.27.refs_0_ = bf16[16,224,128]{2,1,0:T(8,128)(2,1)S(1)} all-to-all(bf16[16,224,128]{2,1,0:T(8,128)(2,1)S(1)} %shard_map.187), channel_id=1, replica_groups=mesh['tm'=32,'seq'=16] {'seq'}, dimensions={0} | all-to-all | bytes 1835008 | tf_op jit(solution)/shard_map/all_to_all | solution.py:649
  202.0 1.1 shard_map.188
  (23 shorter events, 0.1 us)
Async XLA Ops:
  7.2 107.3 %all-gather.3.cloned.1.call-start = ((), (), s32[]{:S(2)}) async-start(), calls=%async_computation.5 | async-start | bytes 4718592 | tf_op jit(solution)/shard_map/all_gather | solution.py:487
  66.1 19.8 %collective-permute-start = (bf16[32,128]{1,0:T(8,128)(2,1)S(1)}, bf16[32,128]{1,0:T(8,128)(2,1)S(1)}, u32[]{:S(2)}, u32[]{:S(2)}) collective-permute-start(bf16[32,128]{1,0:T(8,128)(2,1)S(1)} %get-tuple-element.36), channel_id=1, source_target_pairs={{0,16},{16,32},{32,48},{48,64},{64,80},{80,96},{96,112},{112,128},... | collective-permute-start | bytes 24584 | tf_op jit(solution)/shard_map/ppermute | solution.py:494
  68.1 17.8 %collective-permute-start.1 = (bf16[32,128]{1,0:T(8,128)(2,1)S(1)}, bf16[32,128]{1,0:T(8,128)(2,1)S(1)}, u32[]{:S(2)}, u32[]{:S(2)}) collective-permute-start(bf16[32,128]{1,0:T(8,128)(2,1)S(1)} %get-tuple-element.37), channel_id=1, source_target_pairs={{16,0},{32,16},{48,32},{64,48},{80,64},{96,80},{112,96},{128,112},... | collective-permute-start | bytes 24584 | tf_op jit(solution)/shard_map/ppermute | solution.py:494
  72.2 14.6 %collective-permute-start.2 = (bf16[48,1024]{1,0:T(8,128)(2,1)S(1)}, bf16[48,1024]{1,0:T(8,128)(2,1)S(1)}, u32[]{:S(2)}, u32[]{:S(2)}) collective-permute-start(bf16[48,1024]{1,0:T(8,128)(2,1)S(1)} %get-tuple-element.38), channel_id=1, source_target_pairs={{0,1},{1,2},{2,3},{3,4},{4,5},{5,6},{6,7},{7,8},{8,9},{9,10},{10,1... | collective-permute-start | bytes 294920 | tf_op jit(solution)/shard_map/ppermute | solution.py:494
  75.3 11.4 %collective-permute-start.3 = (bf16[48,1024]{1,0:T(8,128)(2,1)S(1)}, bf16[48,1024]{1,0:T(8,128)(2,1)S(1)}, u32[]{:S(2)}, u32[]{:S(2)}) collective-permute-start(bf16[48,1024]{1,0:T(8,128)(2,1)S(1)} %get-tuple-element.39), channel_id=1, source_target_pairs={{1,0},{2,1},{3,2},{4,3},{5,4},{6,5},{7,6},{8,7},{9,8},{10,9},{11,1... | collective-permute-start | bytes 294920 | tf_op jit(solution)/shard_map/ppermute | solution.py:494
  85.8 10.9 %copy-start.5 = (f32[1024]{0:T(1024)S(1)}, f32[1024]{0:T(1024)}, u32[]{:S(2)}) copy-start(f32[1024]{0:T(1024)} %param.23) | copy-start | bytes 12292
  85.8 10.9 %copy-start.6 = (f32[1024]{0:T(1024)S(1)}, f32[1024]{0:T(1024)}, u32[]{:S(2)}) copy-start(f32[1024]{0:T(1024)} %param.22) | copy-start | bytes 12292
  85.8 10.9 %copy-start.7 = (f32[1024]{0:T(1024)S(1)}, f32[1024]{0:T(1024)}, u32[]{:S(2)}) copy-start(f32[1024]{0:T(1024)} %param.21) | copy-start | bytes 12292
  85.8 10.9 %copy-start.8 = (f32[1024]{0:T(1024)S(1)}, f32[1024]{0:T(1024)}, u32[]{:S(2)}) copy-start(f32[1024]{0:T(1024)} %param.20) | copy-start | bytes 12292
  85.8 28.6 %copy-start = (bf16[128,1024]{1,0:T(8,128)(2,1)S(1)}, bf16[128,1024]{1,0:T(8,128)(2,1)}, u32[]{:S(2)}) copy-start(bf16[128,1024]{1,0:T(8,128)(2,1)} %residual_ref.1) | copy-start | bytes 786436
  85.8 28.6 %copy-start.1 = (bf16[128,1024]{1,0:T(8,128)(2,1)S(1)}, bf16[128,1024]{1,0:T(8,128)(2,1)}, u32[]{:S(2)}) copy-start(bf16[128,1024]{1,0:T(8,128)(2,1)} %grad_ref.1) | copy-start | bytes 786436
  85.8 28.6 %copy-start.2 = (bf16[128,1024]{1,0:T(8,128)(2,1)S(1)}, bf16[128,1024]{1,0:T(8,128)(2,1)}, u32[]{:S(2)}) copy-start(bf16[128,1024]{1,0:T(8,128)(2,1)} %skip_ref.1) | copy-start | bytes 786436
  85.9 28.6 %copy-start.3 = (f32[31,1024]{1,0:T(8,128)S(1)}, f32[31,1024]{1,0:T(8,128)}, u32[]{:S(2)}) copy-start(f32[31,1024]{1,0:T(8,128)} %taps_ref.1) | copy-start | bytes 380932
  85.9 28.6 %copy-start.4 = (f32[1024]{0:T(1024)S(1)}, f32[1024]{0:T(1024)}, u32[]{:S(2)}) copy-start(f32[1024]{0:T(1024)} %param.17) | copy-start | bytes 12292
  86.7 27.7 %all-to-all-start.1 = ((bf16[16,96,128]{2,1,0:T(8,128)(2,1)}), bf16[16,96,128]{2,1,0:T(8,128)(2,1)S(1)}, u32[]{:S(2)}, u32[]{:S(2)}) async-start(bf16[16,96,128]{2,1,0:T(8,128)(2,1)} %shard_map.183), calls=%async_computation.1 | async-start | bytes 786432 | tf_op jit(solution)/shard_map/all_to_all | solution.py:577
  147.8 18.2 %all-to-all-start.3 = ((bf16[32,32,128]{2,1,0:T(8,128)(2,1)}), bf16[32,32,128]{2,1,0:T(8,128)(2,1)S(1)}, u32[]{:S(2)}, u32[]{:S(2)}) async-start(bf16[32,32,128]{2,1,0:T(8,128)(2,1)} %shard_map.185), calls=%async_computation.3 | async-start | bytes 524288 | tf_op jit(solution)/shard_map/all_to_all | solution.py:615
Sparse Core Ops, SparseCore 0:
  62.3 32.8 all-gather.2

commit v7 on v6

--- a/solution.py
+++ b/solution.py
@@ -19,6 +19,7 @@
 SCALE = HD ** (-0.5)
 BLOCK = 256
 TALL = 512
+BACK = 1024
 PART_ROWS = 32
 EDGE = 32
 ROWS = FR + 2 * EDGE
@@ -55,14 +56,18 @@
     return high, mid, low
 
 
-def row_copies(res_hbm, grad_hbm, first_ref, last_ref, copy_sem):
+def rows_kernel(res_hbm, grad_hbm, first_ref, last_ref, copy_sem):
     pairs = (
         (res_hbm.at[0:EDGE], first_ref.at[0:EDGE]),
         (res_hbm.at[FR - EDGE : FR], last_ref.at[0:EDGE]),
         (grad_hbm.at[0:16], first_ref.at[EDGE : EDGE + 16]),
         (grad_hbm.at[FR - 16 : FR], last_ref.at[EDGE : EDGE + 16]),
     )
-    return [pltpu.make_async_copy(src, dst, copy_sem.at[i]) for i, (src, dst) in enumerate(pairs)]
+    copies = [pltpu.make_async_copy(src, dst, copy_sem.at[i]) for i, (src, dst) in enumerate(pairs)]
+    for copy in copies:
+        copy.start()
+    for copy in copies:
+        copy.wait()
 
 
 def pack_kernel(
@@ -145,8 +150,6 @@
 
 def edge_forward_kernel(
     qkv_ref,
-    res_hbm,
-    grad_hbm,
     keys_ref,
     query_ref,
     value_ref,
@@ -155,15 +158,9 @@
     log_ref,
     first_ref,
     last_ref,
-    row_first_ref,
-    row_last_ref,
     score_ref,
     other_ref,
-    copy_sem,
 ):
-    copies = row_copies(res_hbm, grad_hbm, row_first_ref, row_last_ref, copy_sem)
-    for copy in copies:
-        copy.start()
     pad_rows = lax.broadcasted_iota(jnp.int32, (HD, FR), 0)
     ones = jnp.where(pad_rows == 0, 1.0, 0.0).astype(bf16)
     for source in range(HEADS):
@@ -182,8 +179,6 @@
     store_attended(total, final_top, nat_ref, slice(TALL, 2 * TALL), turned_ref, log_ref, 1)
     first_ref[...] = nat_ref[0:EDGE, :]
     last_ref[...] = nat_ref[2 * TALL - EDGE : 2 * TALL, :]
-    for copy in copies:
-        copy.wait()
 
 
 def middle_forward_kernel(
@@ -395,15 +390,15 @@
     total_ref[...] = jnp.zeros_like(total_ref)
 
     def step(block, carry):
-        rows = block_rows(block, TALL)
+        rows = block_rows(block, BACK)
         keys, values, turned = keys_ref[rows, :], values_ref[rows, :], turned_ref[:, rows]
 
         def products(chunk):
             cols = block_rows(chunk)
             return dot(keys, query_ref[:, cols]), dot(values, grad_ref[:, cols])
 
-        key_total = jnp.zeros((TALL, 128), f32)
-        value_total = jnp.zeros((TALL, 128), f32)
+        key_total = jnp.zeros((BACK, 128), f32)
+        value_total = jnp.zeros((BACK, 128), f32)
         ready = products(0)
         for chunk in range(CHUNKS):
             cols = block_rows(chunk)
@@ -417,13 +412,13 @@
             total_ref[:, cols] += dot(turned, grad_scores)
         for place, total in ((1, key_total * SCALE), (2, value_total)):
             turned_total = total.T[:HD].astype(bf16)
-            for side in range(PER_TALL):
-                out_ref[PER_TALL * block + side, HD * place : HD * (place + 1), :] = turned_total[
+            for side in range(BACK // FR):
+                out_ref[BACK // FR * block + side, HD * place : HD * (place + 1), :] = turned_total[
                     :, FR * side : FR * (side + 1)
                 ]
         return carry
 
-    lax.fori_loop(0, TALLS, step, 0)
+    lax.fori_loop(0, STRETCH // BACK, step, 0)
     for source in range(HEADS):
         span = slice(FR * source, FR * (source + 1))
         out_ref[source, 0:HD, :] = (total_ref[:, span] * SCALE).astype(bf16)
@@ -526,11 +521,20 @@
         in_specs=[pl.BlockSpec(memory_space=pltpu.SMEM)] + [in_hbm] * 4,
         scratch=(block, block, block, pltpu.VMEM((128, 128), bf16), pltpu.SemaphoreType.DMA((4,))),
     )
+    row_first, row_last = call(
+        rows_kernel,
+        (shape((edge_rows, D), bf16), shape((edge_rows, D), bf16)),
+        in_high_memory(residual),
+        in_high_memory(grad_conv),
+        in_specs=[in_hbm] * 2,
+        scratch=(pltpu.SemaphoreType.DMA((4,)),),
+    )
+    before, after = neighbours(("tm", "seq"), row_first, row_last)
     qkv = lax.all_to_all(packed, "seq", 0, 0, tiled=True)
     weights = gather_weights(qkv[:, 3 * HD :])
     square = shape((STRETCH, 128), bf16)
     scores = [pltpu.VMEM((TALL, STRETCH), f32)] * 2
-    keys, queries, values, edge_nat, edge_att, edge_log, first, last, row_first, row_last = call(
+    keys, queries, values, edge_nat, edge_att, edge_log, first, last = call(
         edge_forward_kernel,
         (
             shape((128, STRETCH), bf16),
@@ -541,17 +545,11 @@
             shape((2, 8, TALL), f32),
             shape((EDGE, 128), bf16),
             shape((EDGE, 128), bf16),
-            shape((edge_rows, D), bf16),
-            shape((edge_rows, D), bf16),
         ),
         qkv,
-        in_high_memory(residual),
-        in_high_memory(grad_conv),
-        in_specs=[in_vmem, in_hbm, in_hbm],
-        scratch=(*scores, pltpu.SemaphoreType.DMA((4,))),
+        scratch=scores,
     )
     edge_before, edge_after = neighbours("tm", first, last)
-    before, after = neighbours(("tm", "seq"), row_first, row_last)
     mid_nat, mid_att, mid_log = call(
         middle_forward_kernel,
         (

time: 210 us -> 208 us (level)
  the two profiles are of different devices: /device:TPU:18 before, /device:TPU:20 now
where the time goes in v7:
time: 208 us; the launch traced here: 207 us
  blocking collectives  112 us (54%)
  Pallas kernels  32.9 us (16%)
  starting transfers between devices  32 us (15%)
  waiting for transfers between devices  14.7 us (7%)
  between operations  14.3 us (7%)
    all_to_all x1, blocking collectives, local(): qkv = lax.all_to_all(packed, 'seq', 0, 0, tiled=True)  52.6 us
    all_to_all x1, blocking collectives, local(): back = lax.all_to_all(back, 'seq', 0, 0, tiled=True)  40.4 us
    pallas_call x10, Pallas kernels, call(): pl.pallas_call(kernel, out_shape=out_shape, scratch_shapes=list(scratch),...  32.9 us
    all_to_all x1, blocking collectives, local(): payload = lax.all_to_all(payload, 'seq', 0, 0, tiled=True)  19.2 us
    ppermute x4, starting transfers between devices, neighbours(): return (lax.ppermute(last, axes, up), lax.ppermute(first, axes, down))  17.6 us
    all_to_all x1, waiting for transfers between devices, local(): att_rows = lax.all_to_all(att_payload, 'seq', 0, 0, tiled=True)  14.7 us
    all_to_all x1, starting transfers between devices, local(): totals = lax.all_to_all(spread, 'tm', 0, 0, tiled=True)  10.7 us
  transfers between devices with their start and end apart: 7, of which 1 were waited for; matrix products, arithmetic and copies ran while one was open for 0% of the time, Pallas kernels for 9%

profile of v7, /device:TPU:20, one launch (start us, length us, event | category | flops | bytes accessed | tf_op | source)
XLA Modules:
  0.0 207.0 jit_solution(12034375185841963387)
XLA Ops:
  7.2 0.0 all-gather.3.cloned.1.call-start
  7.2 1.4 shard_map.180
  8.7 52.6 %all_to_all.25.qkv_ref = bf16[16,320,128]{2,1,0:T(8,128)(2,1)S(1)} all-to-all(bf16[16,320,128]{2,1,0:T(8,128)(2,1)S(1)} %shard_map.180), channel_id=1, replica_groups=mesh['tm'=32,'seq'=16] {'seq'}, dimensions={0} | all-to-all | bytes 2621440 | tf_op jit(solution)/shard_map/all_to_all | solution.py:533
  61.3 0.8 slice.4
  62.1 0.0 all-gather.3.cloned.1.call-update
  62.2 0.9 shard_map.184
  63.1 3.0 %collective-permute-start.2 = (bf16[48,1024]{1,0:T(8,128)(2,1)S(1)}, bf16[48,1024]{1,0:T(8,128)(2,1)S(1)}, u32[]{:S(2)}, u32[]{:S(2)}) collective-permute-start(bf16[48,1024]{1,0:T(8,128)(2,1)S(1)} %get-tuple-element.38), channel_id=1, source_target_pairs={{0,1},{1,2},{2,3},{3,4},{4,5},{5,6},{6,7},{7,8},{8,9},{9,10},{10,1... | collective-permute-start | bytes 294920 | tf_op jit(solution)/shard_map/ppermute | solution.py:489
  66.1 7.7 %collective-permute-start.3 = (bf16[48,1024]{1,0:T(8,128)(2,1)S(1)}, bf16[48,1024]{1,0:T(8,128)(2,1)S(1)}, u32[]{:S(2)}, u32[]{:S(2)}) collective-permute-start(bf16[48,1024]{1,0:T(8,128)(2,1)S(1)} %get-tuple-element.39), channel_id=1, source_target_pairs={{1,0},{2,1},{3,2},{4,3},{5,4},{6,5},{7,6},{8,7},{9,8},{10,9},{11,1... | collective-permute-start | bytes 294920 | tf_op jit(solution)/shard_map/ppermute | solution.py:489
  73.8 3.2 %shard_map.181 = (bf16[128,2048]{1,0:T(8,128)(2,1)S(1)}, bf16[2048,128]{1,0:T(8,128)(2,1)S(1)}, bf16[2048,128]{1,0:T(8,128)(2,1)S(1)}, bf16[1024,128]{1,0:T(8,12...) custom-call(bf16[16,320,128]{2,1,0:T(8,128)(2,1)S(1)} %all_to_all.25, ...), custom_call_target="tpu_custom_call" | custom-call | tf_op jit(solution)/shard_map/pallas_call | solution.py:458
  77.0 1.9 collective-permute-start
  78.9 5.0 %collective-permute-start.1 = (bf16[32,128]{1,0:T(8,128)(2,1)S(1)}, bf16[32,128]{1,0:T(8,128)(2,1)S(1)}, u32[]{:S(2)}, u32[]{:S(2)}) collective-permute-start(bf16[32,128]{1,0:T(8,128)(2,1)S(1)} %get-tuple-element.37), channel_id=1, source_target_pairs={{16,0},{32,16},{48,32},{64,48},{80,64},{96,80},{112,96},{128,112},... | collective-permute-start | bytes 24584 | tf_op jit(solution)/shard_map/ppermute | solution.py:489
  83.9 2.9 %shard_map.182 = (bf16[1024,128]{1,0:T(8,128)(2,1)S(1)}, bf16[2,64,512]{2,1,0:T(8,128)(2,1)S(1)}, f32[2,8,512]{2,1,0:T(8,128)S(1)}) custom-call(bf16[128,2048]{1,0:T(8,128)(2,1)S(1)} %get-tuple-element.32.keys_ref, bf16[2048,128]{1,0:T(8,128)(2,1)S(1)} %get-tuple-element.33.query_ref, bf16[2048,128]{1,0:T(8,128)(2,1)S(1)} %get-tuple-element.34.value_ref), custom_call_target="tpu_custom_call" | custom-call | flops 6000000000 | bytes 4194304 | tf_op jit(solution)/shard_map/pallas_call | solution.py:458
  86.8 0.0 copy-start.6
  86.9 0.8 shard_map.183
  87.8 3.7 %all-to-all-start.1 = ((bf16[16,96,128]{2,1,0:T(8,128)(2,1)}), bf16[16,96,128]{2,1,0:T(8,128)(2,1)S(1)}, u32[]{:S(2)}, u32[]{:S(2)}) async-start(bf16[16,96,128]{2,1,0:T(8,128)(2,1)} %shard_map.183), calls=%async_computation.1 | async-start | bytes 786432 | tf_op jit(solution)/shard_map/all_to_all | solution.py:575
  91.6 14.7 %all-to-all-done.1.att_ref = bf16[16,96,128]{2,1,0:T(8,128)(2,1)S(1)} async-done(((bf16[16,96,128]{2,1,0:T(8,128)(2,1)}), bf16[16,96,128]{2,1,0:T(8,128)(2,1)S(1)}, u32[]{:S(2)}, u32[]{:S(2)}) %all-to-all-start.1) | async-done | bytes 393248 | tf_op jit(solution)/shard_map/all_to_all | solution.py:575
  106.3 10.5 %shard_map.185 = (bf16[128,1024]{1,0:T(8,128)(2,1)}, bf16[16,96,128]{2,1,0:T(8,128)(2,1)S(1)}) custom-call(bf16[16,96,128]{2,1,0:T(8,128)(2,1)S(1)} %all-to-all-done.1.att_ref, bf16[128,1024]{1,0:T(8,128)(2,1)S(1)} %copy-done, bf16[48,1024]{1,0:T(8,128)(2,1)S(1)} %collective-permute-done.2.before_ref, bf16[48,1024]{1,0:T(8,128)(2,1)S(1)} %collective-permute-done.3.after_ref, ...), custom_call_target="tpu_custom_call" | custom-call | tf_op jit(solution)/shard_map/pallas_call | solution.py:458
  116.8 19.2 %all_to_all.26.payload_ref = bf16[16,96,128]{2,1,0:T(8,128)(2,1)S(1)} all-to-all(bf16[16,96,128]{2,1,0:T(8,128)(2,1)S(1)} %get-tuple-element.43), channel_id=1, replica_groups=mesh['tm'=32,'seq'=16] {'seq'}, dimensions={0} | all-to-all | bytes 786432 | tf_op jit(solution)/shard_map/all_to_all | solution.py:604
  136.0 0.7 shard_map.186
  136.7 10.7 %all-to-all-start.3 = ((bf16[32,32,128]{2,1,0:T(8,128)(2,1)}), bf16[32,32,128]{2,1,0:T(8,128)(2,1)S(1)}, u32[]{:S(2)}, u32[]{:S(2)}) async-start(bf16[32,32,128]{2,1,0:T(8,128)(2,1)} %shard_map.186), calls=%async_computation.3 | async-start | bytes 524288 | tf_op jit(solution)/shard_map/all_to_all | solution.py:613
  147.4 11.2 %shard_map.187.payload_ref = bf16[16,224,128]{2,1,0:T(8,128)(2,1)S(1)} custom-call(bf16[16,320,128]{2,1,0:T(8,128)(2,1)S(1)} %all_to_all.25.qkv_ref, bf16[2,64,512]{2,1,0:T(8,128)(2,1)S(1)} %get-tuple-element.44.edge_att_ref, bf16[2,64,512]{2,1,0:T(8,128)(2,1)S(1)} %get-tuple-element.45.mid_att_ref, f32[2,8,512]{2,1,0:T(8,128)S(1)} %get-tuple-element.46.edge_log_ref, ...), custom_call_target="tpu_custom_call" | custom-call | flops 12000000000 | bytes 4194304 | tf_op jit(solution)/shard_map/pallas_call | solution.py:458
  158.7 0.1 shard_map.188
  158.7 40.4 %all_to_all.27.refs_0_ = bf16[16,224,128]{2,1,0:T(8,128)(2,1)S(1)} all-to-all(bf16[16,224,128]{2,1,0:T(8,128)(2,1)S(1)} %shard_map.188), channel_id=1, replica_groups=mesh['tm'=32,'seq'=16] {'seq'}, dimensions={0} | all-to-all | bytes 1835008 | tf_op jit(solution)/shard_map/all_to_all | solution.py:647
  199.1 1.1 shard_map.189
  (24 shorter events, 0.1 us)
Async XLA Ops:
  7.2 99.1 %all-gather.3.cloned.1.call-start = ((), (), s32[]{:S(2)}) async-start(), calls=%async_computation.5 | async-start | bytes 4718592 | tf_op jit(solution)/shard_map/all_gather | solution.py:482
  63.1 24.7 %collective-permute-start.2 = (bf16[48,1024]{1,0:T(8,128)(2,1)S(1)}, bf16[48,1024]{1,0:T(8,128)(2,1)S(1)}, u32[]{:S(2)}, u32[]{:S(2)}) collective-permute-start(bf16[48,1024]{1,0:T(8,128)(2,1)S(1)} %get-tuple-element.38), channel_id=1, source_target_pairs={{0,1},{1,2},{2,3},{3,4},{4,5},{5,6},{6,7},{7,8},{8,9},{9,10},{10,1... | collective-permute-start | bytes 294920 | tf_op jit(solution)/shard_map/ppermute | solution.py:489
  66.1 21.7 %collective-permute-start.3 = (bf16[48,1024]{1,0:T(8,128)(2,1)S(1)}, bf16[48,1024]{1,0:T(8,128)(2,1)S(1)}, u32[]{:S(2)}, u32[]{:S(2)}) collective-permute-start(bf16[48,1024]{1,0:T(8,128)(2,1)S(1)} %get-tuple-element.39), channel_id=1, source_target_pairs={{1,0},{2,1},{3,2},{4,3},{5,4},{6,5},{7,6},{8,7},{9,8},{10,9},{11,1... | collective-permute-start | bytes 294920 | tf_op jit(solution)/shard_map/ppermute | solution.py:489
  77.0 9.9 %collective-permute-start = (bf16[32,128]{1,0:T(8,128)(2,1)S(1)}, bf16[32,128]{1,0:T(8,128)(2,1)S(1)}, u32[]{:S(2)}, u32[]{:S(2)}) collective-permute-start(bf16[32,128]{1,0:T(8,128)(2,1)S(1)} %get-tuple-element.36), channel_id=1, source_target_pairs={{0,16},{16,32},{32,48},{48,64},{64,80},{80,96},{96,112},{112,128},... | collective-permute-start | bytes 24584 | tf_op jit(solution)/shard_map/ppermute | solution.py:489
  78.9 8.0 %collective-permute-start.1 = (bf16[32,128]{1,0:T(8,128)(2,1)S(1)}, bf16[32,128]{1,0:T(8,128)(2,1)S(1)}, u32[]{:S(2)}, u32[]{:S(2)}) collective-permute-start(bf16[32,128]{1,0:T(8,128)(2,1)S(1)} %get-tuple-element.37), channel_id=1, source_target_pairs={{16,0},{32,16},{48,32},{64,48},{80,64},{96,80},{112,96},{128,112},... | collective-permute-start | bytes 24584 | tf_op jit(solution)/shard_map/ppermute | solution.py:489
  86.8 4.7 %copy-start.5 = (f32[1024]{0:T(1024)S(1)}, f32[1024]{0:T(1024)}, u32[]{:S(2)}) copy-start(f32[1024]{0:T(1024)} %param.23) | copy-start | bytes 12292
  86.8 4.7 %copy-start.6 = (f32[1024]{0:T(1024)S(1)}, f32[1024]{0:T(1024)}, u32[]{:S(2)}) copy-start(f32[1024]{0:T(1024)} %param.22) | copy-start | bytes 12292
  86.8 4.7 %copy-start.7 = (f32[1024]{0:T(1024)S(1)}, f32[1024]{0:T(1024)}, u32[]{:S(2)}) copy-start(f32[1024]{0:T(1024)} %param.21) | copy-start | bytes 12292
  86.8 4.7 %copy-start.8 = (f32[1024]{0:T(1024)S(1)}, f32[1024]{0:T(1024)}, u32[]{:S(2)}) copy-start(f32[1024]{0:T(1024)} %param.20) | copy-start | bytes 12292
  86.8 19.4 %copy-start = (bf16[128,1024]{1,0:T(8,128)(2,1)S(1)}, bf16[128,1024]{1,0:T(8,128)(2,1)}, u32[]{:S(2)}) copy-start(bf16[128,1024]{1,0:T(8,128)(2,1)} %residual_ref.1) | copy-start | bytes 786436
  86.9 19.4 %copy-start.1 = (bf16[128,1024]{1,0:T(8,128)(2,1)S(1)}, bf16[128,1024]{1,0:T(8,128)(2,1)}, u32[]{:S(2)}) copy-start(bf16[128,1024]{1,0:T(8,128)(2,1)} %grad_ref.1) | copy-start | bytes 786436
  86.9 19.4 %copy-start.2 = (bf16[128,1024]{1,0:T(8,128)(2,1)S(1)}, bf16[128,1024]{1,0:T(8,128)(2,1)}, u32[]{:S(2)}) copy-start(bf16[128,1024]{1,0:T(8,128)(2,1)} %skip_ref.1) | copy-start | bytes 786436
  86.9 19.4 %copy-start.3 = (f32[31,1024]{1,0:T(8,128)S(1)}, f32[31,1024]{1,0:T(8,128)}, u32[]{:S(2)}) copy-start(f32[31,1024]{1,0:T(8,128)} %taps_ref.1) | copy-start | bytes 380932
  86.9 19.4 %copy-start.4 = (f32[1024]{0:T(1024)S(1)}, f32[1024]{0:T(1024)}, u32[]{:S(2)}) copy-start(f32[1024]{0:T(1024)} %param.17) | copy-start | bytes 12292
  87.8 18.5 %all-to-all-start.1 = ((bf16[16,96,128]{2,1,0:T(8,128)(2,1)}), bf16[16,96,128]{2,1,0:T(8,128)(2,1)S(1)}, u32[]{:S(2)}, u32[]{:S(2)}) async-start(bf16[16,96,128]{2,1,0:T(8,128)(2,1)} %shard_map.183), calls=%async_computation.1 | async-start | bytes 786432 | tf_op jit(solution)/shard_map/all_to_all | solution.py:575
  136.7 21.9 %all-to-all-start.3 = ((bf16[32,32,128]{2,1,0:T(8,128)(2,1)}), bf16[32,32,128]{2,1,0:T(8,128)(2,1)S(1)}, u32[]{:S(2)}, u32[]{:S(2)}) async-start(bf16[32,32,128]{2,1,0:T(8,128)(2,1)} %shard_map.186), calls=%async_computation.3 | async-start | bytes 524288 | tf_op jit(solution)/shard_map/all_to_all | solution.py:613
Sparse Core Ops, SparseCore 0:
  62.3 32.5 all-gather.2

commit v8 on v7

--- a/solution.py
+++ b/solution.py
@@ -56,27 +56,17 @@
     return high, mid, low
 
 
-def rows_kernel(res_hbm, grad_hbm, first_ref, last_ref, copy_sem):
-    pairs = (
-        (res_hbm.at[0:EDGE], first_ref.at[0:EDGE]),
-        (res_hbm.at[FR - EDGE : FR], last_ref.at[0:EDGE]),
-        (grad_hbm.at[0:16], first_ref.at[EDGE : EDGE + 16]),
-        (grad_hbm.at[FR - 16 : FR], last_ref.at[EDGE : EDGE + 16]),
-    )
-    copies = [pltpu.make_async_copy(src, dst, copy_sem.at[i]) for i, (src, dst) in enumerate(pairs)]
-    for copy in copies:
-        copy.start()
-    for copy in copies:
-        copy.wait()
-
-
 def pack_kernel(
     chunk_ref,
     query_hbm,
     key_hbm,
     value_hbm,
     weight_hbm,
+    res_hbm,
+    grad_hbm,
     out_ref,
+    first_ref,
+    last_ref,
     query_ref,
     key_ref,
     value_ref,
@@ -84,7 +74,16 @@
     copy_sem,
 ):
     weight_rows = weight_hbm.at[pl.ds(pl.multiple_of(chunk_ref[0] * 128, 128), 128)]
-    pairs = ((query_hbm, query_ref), (key_hbm, key_ref), (value_hbm, value_ref), (weight_rows, weight_ref))
+    pairs = (
+        (query_hbm, query_ref),
+        (key_hbm, key_ref),
+        (value_hbm, value_ref),
+        (weight_rows, weight_ref),
+        (res_hbm.at[0:EDGE], first_ref.at[0:EDGE]),
+        (res_hbm.at[FR - EDGE : FR], last_ref.at[0:EDGE]),
+        (grad_hbm.at[0:16], first_ref.at[EDGE : EDGE + 16]),
+        (grad_hbm.at[FR - 16 : FR], last_ref.at[EDGE : EDGE + 16]),
+    )
     copies = [pltpu.make_async_copy(src, dst, copy_sem.at[i]) for i, (src, dst) in enumerate(pairs)]
     for copy in copies:
         copy.start()
@@ -97,6 +96,8 @@
     copies[3].wait()
     for dest in range(HEADS):
         out_ref[dest, 3 * HD :, :] = weight_ref[...]
+    for copy in copies[4:]:
+        copy.wait()
 
 
 CHUNKS = STRETCH // BLOCK
@@ -513,21 +514,13 @@
 
     edge_rows = EDGE + EDGE // 2
     block = pltpu.VMEM((FR, D), bf16)
-    packed = call(
+    packed, row_first, row_last = call(
         pack_kernel,
-        shape((HEADS, 3 * HD + 128, FR), bf16),
+        (shape((HEADS, 3 * HD + 128, FR), bf16), shape((edge_rows, D), bf16), shape((edge_rows, D), bf16)),
         weight_chunk().reshape(1),
-        *map(in_high_memory, (query_in, key_in, value_in, proj_weight)),
-        in_specs=[pl.BlockSpec(memory_space=pltpu.SMEM)] + [in_hbm] * 4,
-        scratch=(block, block, block, pltpu.VMEM((128, 128), bf16), pltpu.SemaphoreType.DMA((4,))),
-    )
-    row_first, row_last = call(
-        rows_kernel,
-        (shape((edge_rows, D), bf16), shape((edge_rows, D), bf16)),
-        in_high_memory(residual),
-        in_high_memory(grad_conv),
-        in_specs=[in_hbm] * 2,
-        scratch=(pltpu.SemaphoreType.DMA((4,)),),
+        *map(in_high_memory, (query_in, key_in, value_in, proj_weight, residual, grad_conv)),
+        in_specs=[pl.BlockSpec(memory_space=pltpu.SMEM)] + [in_hbm] * 6,
+        scratch=(block, block, block, pltpu.VMEM((128, 128), bf16), pltpu.SemaphoreType.DMA((8,))),
     )
     before, after = neighbours(("tm", "seq"), row_first, row_last)
     qkv = lax.all_to_all(packed, "seq", 0, 0, tiled=True)

time: 208 us -> 206 us (level)
  the two profiles are of different devices: /device:TPU:20 before, /device:TPU:18 now
where the time goes in v8:
time: 206 us
  blocking collectives  112 us (54%)
  starting transfers between devices  32.1 us (16%)
  Pallas kernels  32 us (16%)
  waiting for transfers between devices  14.7 us (7%)
  between operations  14.3 us (7%)
    all_to_all x1, blocking collectives, local(): qkv = lax.all_to_all(packed, 'seq', 0, 0, tiled=True)  52.6 us
    all_to_all x1, blocking collectives, local(): back = lax.all_to_all(back, 'seq', 0, 0, tiled=True)  40.3 us
    pallas_call x9, Pallas kernels, call(): pl.pallas_call(kernel, out_shape=out_shape, scratch_shapes=list(scratch),...  32 us
    all_to_all x1, blocking collectives, local(): payload = lax.all_to_all(payload, 'seq', 0, 0, tiled=True)  19.2 us
    ppermute x4, starting transfers between devices, neighbours(): return (lax.ppermute(last, axes, up), lax.ppermute(first, axes, down))  17.6 us
    all_to_all x1, waiting for transfers between devices, local(): att_rows = lax.all_to_all(att_payload, 'seq', 0, 0, tiled=True)  14.6 us
    all_to_all x1, starting transfers between devices, local(): totals = lax.all_to_all(spread, 'tm', 0, 0, tiled=True)  10.7 us
  transfers between devices with their start and end apart: 7, of which 1 were waited for; matrix products, arithmetic and copies ran while one was open for 0% of the time, Pallas kernels for 9%

profile of v8, /device:TPU:18, one launch (start us, length us, event | category | flops | bytes accessed | tf_op | source)
XLA Modules:
  0.0 206.0 jit_solution(1919206602127055901)
XLA Ops:
  7.2 0.0 all-gather.3.cloned.1.call-start
  7.2 1.5 shard_map.180
  8.7 52.6 %all_to_all.25.qkv_ref = bf16[16,320,128]{2,1,0:T(8,128)(2,1)S(1)} all-to-all(bf16[16,320,128]{2,1,0:T(8,128)(2,1)S(1)} %get-tuple-element.32), channel_id=1, replica_groups=mesh['tm'=32,'seq'=16] {'seq'}, dimensions={0} | all-to-all | bytes 2621440 | tf_op jit(solution)/shard_map/all_to_all | solution.py:526
  61.4 0.8 slice.4
  62.2 0.0 all-gather.3.cloned.1.call-update
  62.2 3.0 %collective-permute-start.2 = (bf16[48,1024]{1,0:T(8,128)(2,1)S(1)}, bf16[48,1024]{1,0:T(8,128)(2,1)S(1)}, u32[]{:S(2)}, u32[]{:S(2)}) collective-permute-start(bf16[48,1024]{1,0:T(8,128)(2,1)S(1)} %get-tuple-element.40), channel_id=1, source_target_pairs={{0,1},{1,2},{2,3},{3,4},{4,5},{5,6},{6,7},{7,8},{8,9},{9,10},{10,1... | collective-permute-start | bytes 294920 | tf_op jit(solution)/shard_map/ppermute | solution.py:490
  65.2 7.7 %collective-permute-start.3 = (bf16[48,1024]{1,0:T(8,128)(2,1)S(1)}, bf16[48,1024]{1,0:T(8,128)(2,1)S(1)}, u32[]{:S(2)}, u32[]{:S(2)}) collective-permute-start(bf16[48,1024]{1,0:T(8,128)(2,1)S(1)} %get-tuple-element.41), channel_id=1, source_target_pairs={{1,0},{2,1},{3,2},{4,3},{5,4},{6,5},{7,6},{8,7},{9,8},{10,9},{11,1... | collective-permute-start | bytes 294920 | tf_op jit(solution)/shard_map/ppermute | solution.py:490
  72.9 3.2 %shard_map.181 = (bf16[128,2048]{1,0:T(8,128)(2,1)S(1)}, bf16[2048,128]{1,0:T(8,128)(2,1)S(1)}, bf16[2048,128]{1,0:T(8,128)(2,1)S(1)}, bf16[1024,128]{1,0:T(8,12...) custom-call(bf16[16,320,128]{2,1,0:T(8,128)(2,1)S(1)} %all_to_all.25, ...), custom_call_target="tpu_custom_call" | custom-call | tf_op jit(solution)/shard_map/pallas_call | solution.py:459
  76.1 1.9 collective-permute-start
  78.0 5.0 %collective-permute-start.1 = (bf16[32,128]{1,0:T(8,128)(2,1)S(1)}, bf16[32,128]{1,0:T(8,128)(2,1)S(1)}, u32[]{:S(2)}, u32[]{:S(2)}) collective-permute-start(bf16[32,128]{1,0:T(8,128)(2,1)S(1)} %get-tuple-element.39), channel_id=1, source_target_pairs={{16,0},{32,16},{48,32},{64,48},{80,64},{96,80},{112,96},{128,112},... | collective-permute-start | bytes 24584 | tf_op jit(solution)/shard_map/ppermute | solution.py:490
  83.0 2.9 %shard_map.182 = (bf16[1024,128]{1,0:T(8,128)(2,1)S(1)}, bf16[2,64,512]{2,1,0:T(8,128)(2,1)S(1)}, f32[2,8,512]{2,1,0:T(8,128)S(1)}) custom-call(bf16[128,2048]{1,0:T(8,128)(2,1)S(1)} %get-tuple-element.34.keys_ref, bf16[2048,128]{1,0:T(8,128)(2,1)S(1)} %get-tuple-element.35.query_ref, bf16[2048,128]{1,0:T(8,128)(2,1)S(1)} %get-tuple-element.36.value_ref), custom_call_target="tpu_custom_call" | custom-call | flops 6000000000 | bytes 4194304 | tf_op jit(solution)/shard_map/pallas_call | solution.py:459
  85.9 0.0 copy-start.5
  86.0 0.0 copy-start.7
  86.1 0.8 shard_map.183
  86.9 3.7 %all-to-all-start.1 = ((bf16[16,96,128]{2,1,0:T(8,128)(2,1)}), bf16[16,96,128]{2,1,0:T(8,128)(2,1)S(1)}, u32[]{:S(2)}, u32[]{:S(2)}) async-start(bf16[16,96,128]{2,1,0:T(8,128)(2,1)} %shard_map.183), calls=%async_computation.1 | async-start | bytes 786432 | tf_op jit(solution)/shard_map/all_to_all | solution.py:568
  90.7 14.6 %all-to-all-done.1.att_ref = bf16[16,96,128]{2,1,0:T(8,128)(2,1)S(1)} async-done(((bf16[16,96,128]{2,1,0:T(8,128)(2,1)}), bf16[16,96,128]{2,1,0:T(8,128)(2,1)S(1)}, u32[]{:S(2)}, u32[]{:S(2)}) %all-to-all-start.1) | async-done | bytes 393248 | tf_op jit(solution)/shard_map/all_to_all | solution.py:568
  105.4 10.5 %shard_map.184 = (bf16[128,1024]{1,0:T(8,128)(2,1)}, bf16[16,96,128]{2,1,0:T(8,128)(2,1)S(1)}) custom-call(bf16[16,96,128]{2,1,0:T(8,128)(2,1)S(1)} %all-to-all-done.1.att_ref, bf16[128,1024]{1,0:T(8,128)(2,1)S(1)} %copy-done, bf16[48,1024]{1,0:T(8,128)(2,1)S(1)} %collective-permute-done.2.before_ref, bf16[48,1024]{1,0:T(8,128)(2,1)S(1)} %collective-permute-done.3.after_ref, ...), custom_call_target="tpu_custom_call" | custom-call | tf_op jit(solution)/shard_map/pallas_call | solution.py:459
  115.9 19.2 %all_to_all.26.payload_ref = bf16[16,96,128]{2,1,0:T(8,128)(2,1)S(1)} all-to-all(bf16[16,96,128]{2,1,0:T(8,128)(2,1)S(1)} %get-tuple-element.45), channel_id=1, replica_groups=mesh['tm'=32,'seq'=16] {'seq'}, dimensions={0} | all-to-all | bytes 786432 | tf_op jit(solution)/shard_map/all_to_all | solution.py:597
  135.1 0.7 shard_map.185
  135.8 10.7 %all-to-all-start.3 = ((bf16[32,32,128]{2,1,0:T(8,128)(2,1)}), bf16[32,32,128]{2,1,0:T(8,128)(2,1)S(1)}, u32[]{:S(2)}, u32[]{:S(2)}) async-start(bf16[32,32,128]{2,1,0:T(8,128)(2,1)} %shard_map.185), calls=%async_computation.3 | async-start | bytes 524288 | tf_op jit(solution)/shard_map/all_to_all | solution.py:606
  146.5 11.2 %shard_map.186.payload_ref = bf16[16,224,128]{2,1,0:T(8,128)(2,1)S(1)} custom-call(bf16[16,320,128]{2,1,0:T(8,128)(2,1)S(1)} %all_to_all.25.qkv_ref, bf16[2,64,512]{2,1,0:T(8,128)(2,1)S(1)} %get-tuple-element.46.edge_att_ref, bf16[2,64,512]{2,1,0:T(8,128)(2,1)S(1)} %get-tuple-element.47.mid_att_ref, f32[2,8,512]{2,1,0:T(8,128)S(1)} %get-tuple-element.48.edge_log_ref, ...), custom_call_target="tpu_custom_call" | custom-call | flops 12000000000 | bytes 4194304 | tf_op jit(solution)/shard_map/pallas_call | solution.py:459
  157.8 0.1 shard_map.187
  157.8 40.3 %all_to_all.27.refs_0_ = bf16[16,224,128]{2,1,0:T(8,128)(2,1)S(1)} all-to-all(bf16[16,224,128]{2,1,0:T(8,128)(2,1)S(1)} %shard_map.187), channel_id=1, replica_groups=mesh['tm'=32,'seq'=16] {'seq'}, dimensions={0} | all-to-all | bytes 1835008 | tf_op jit(solution)/shard_map/all_to_all | solution.py:640
  198.1 1.1 shard_map.188
  (23 shorter events, 0.1 us)
Async XLA Ops:
  7.2 98.2 %all-gather.3.cloned.1.call-start = ((), (), s32[]{:S(2)}) async-start(), calls=%async_computation.5 | async-start | bytes 4718592 | tf_op jit(solution)/shard_map/all_gather | solution.py:483
  62.2 24.7 %collective-permute-start.2 = (bf16[48,1024]{1,0:T(8,128)(2,1)S(1)}, bf16[48,1024]{1,0:T(8,128)(2,1)S(1)}, u32[]{:S(2)}, u32[]{:S(2)}) collective-permute-start(bf16[48,1024]{1,0:T(8,128)(2,1)S(1)} %get-tuple-element.40), channel_id=1, source_target_pairs={{0,1},{1,2},{2,3},{3,4},{4,5},{5,6},{6,7},{7,8},{8,9},{9,10},{10,1... | collective-permute-start | bytes 294920 | tf_op jit(solution)/shard_map/ppermute | solution.py:490
  65.2 21.7 %collective-permute-start.3 = (bf16[48,1024]{1,0:T(8,128)(2,1)S(1)}, bf16[48,1024]{1,0:T(8,128)(2,1)S(1)}, u32[]{:S(2)}, u32[]{:S(2)}) collective-permute-start(bf16[48,1024]{1,0:T(8,128)(2,1)S(1)} %get-tuple-element.41), channel_id=1, source_target_pairs={{1,0},{2,1},{3,2},{4,3},{5,4},{6,5},{7,6},{8,7},{9,8},{10,9},{11,1... | collective-permute-start | bytes 294920 | tf_op jit(solution)/shard_map/ppermute | solution.py:490
  76.1 9.9 %collective-permute-start = (bf16[32,128]{1,0:T(8,128)(2,1)S(1)}, bf16[32,128]{1,0:T(8,128)(2,1)S(1)}, u32[]{:S(2)}, u32[]{:S(2)}) collective-permute-start(bf16[32,128]{1,0:T(8,128)(2,1)S(1)} %get-tuple-element.38), channel_id=1, source_target_pairs={{0,16},{16,32},{32,48},{48,64},{64,80},{80,96},{96,112},{112,128},... | collective-permute-start | bytes 24584 | tf_op jit(solution)/shard_map/ppermute | solution.py:490
  78.0 8.0 %collective-permute-start.1 = (bf16[32,128]{1,0:T(8,128)(2,1)S(1)}, bf16[32,128]{1,0:T(8,128)(2,1)S(1)}, u32[]{:S(2)}, u32[]{:S(2)}) collective-permute-start(bf16[32,128]{1,0:T(8,128)(2,1)S(1)} %get-tuple-element.39), channel_id=1, source_target_pairs={{16,0},{32,16},{48,32},{64,48},{80,64},{96,80},{112,96},{128,112},... | collective-permute-start | bytes 24584 | tf_op jit(solution)/shard_map/ppermute | solution.py:490
  85.9 4.7 %copy-start.5 = (f32[1024]{0:T(1024)S(1)}, f32[1024]{0:T(1024)}, u32[]{:S(2)}) copy-start(f32[1024]{0:T(1024)} %param.23) | copy-start | bytes 12292
  85.9 4.7 %copy-start.6 = (f32[1024]{0:T(1024)S(1)}, f32[1024]{0:T(1024)}, u32[]{:S(2)}) copy-start(f32[1024]{0:T(1024)} %param.22) | copy-start | bytes 12292
  86.0 4.7 %copy-start.7 = (f32[1024]{0:T(1024)S(1)}, f32[1024]{0:T(1024)}, u32[]{:S(2)}) copy-start(f32[1024]{0:T(1024)} %param.21) | copy-start | bytes 12292
  86.0 4.7 %copy-start.8 = (f32[1024]{0:T(1024)S(1)}, f32[1024]{0:T(1024)}, u32[]{:S(2)}) copy-start(f32[1024]{0:T(1024)} %param.20) | copy-start | bytes 12292
  86.0 19.4 %copy-start = (bf16[128,1024]{1,0:T(8,128)(2,1)S(1)}, bf16[128,1024]{1,0:T(8,128)(2,1)}, u32[]{:S(2)}) copy-start(bf16[128,1024]{1,0:T(8,128)(2,1)} %residual_ref.1) | copy-start | bytes 786436
  86.0 19.4 %copy-start.1 = (bf16[128,1024]{1,0:T(8,128)(2,1)S(1)}, bf16[128,1024]{1,0:T(8,128)(2,1)}, u32[]{:S(2)}) copy-start(bf16[128,1024]{1,0:T(8,128)(2,1)} %grad_ref.1) | copy-start | bytes 786436
  86.0 19.4 %copy-start.2 = (bf16[128,1024]{1,0:T(8,128)(2,1)S(1)}, bf16[128,1024]{1,0:T(8,128)(2,1)}, u32[]{:S(2)}) copy-start(bf16[128,1024]{1,0:T(8,128)(2,1)} %skip_ref.1) | copy-start | bytes 786436
  86.0 19.3 %copy-start.3 = (f32[31,1024]{1,0:T(8,128)S(1)}, f32[31,1024]{1,0:T(8,128)}, u32[]{:S(2)}) copy-start(f32[31,1024]{1,0:T(8,128)} %taps_ref.1) | copy-start | bytes 380932
  86.0 19.3 %copy-start.4 = (f32[1024]{0:T(1024)S(1)}, f32[1024]{0:T(1024)}, u32[]{:S(2)}) copy-start(f32[1024]{0:T(1024)} %param.17) | copy-start | bytes 12292
  86.9 18.4 %all-to-all-start.1 = ((bf16[16,96,128]{2,1,0:T(8,128)(2,1)}), bf16[16,96,128]{2,1,0:T(8,128)(2,1)S(1)}, u32[]{:S(2)}, u32[]{:S(2)}) async-start(bf16[16,96,128]{2,1,0:T(8,128)(2,1)} %shard_map.183), calls=%async_computation.1 | async-start | bytes 786432 | tf_op jit(solution)/shard_map/all_to_all | solution.py:568
  135.8 21.9 %all-to-all-start.3 = ((bf16[32,32,128]{2,1,0:T(8,128)(2,1)}), bf16[32,32,128]{2,1,0:T(8,128)(2,1)S(1)}, u32[]{:S(2)}, u32[]{:S(2)}) async-start(bf16[32,32,128]{2,1,0:T(8,128)(2,1)} %shard_map.185), calls=%async_computation.3 | async-start | bytes 524288 | tf_op jit(solution)/shard_map/all_to_all | solution.py:606
Sparse Core Ops, SparseCore 0:
  62.3 32.8 all-gather.2
